TPU v7x, 32 devices: a whole 2x2x4 slice. The times are simulated.
32 devices in a mesh: dp: 16 (over z, y, x), fsdp: 2 (over core).
Axes of the slice: x: 2, y: 2, z: 4, core: 2. Of those that a mesh axis runs over, the one named last changes fastest.
Arguments:
- inputs: bfloat16 [32768, 512], P(('dp', 'fsdp')), may hold values from -6 to 6
- cotangent: bfloat16 [32768, 512], P(('dp', 'fsdp')), may hold values from -6 to 6
- doc_ids: int32 [32, 1024], P(('dp', 'fsdp')), may hold values from 0 to 3, never falling along the last dimension, each value on 1 to 768 neighbouring positions
- slot_ids: int32 [32, 512, 4], P(('dp', 'fsdp')), may hold values from 0 to 511
- qkv_flat: bfloat16 [786432], P(('dp', 'fsdp')), may hold values from -0.375 to 0.375
- out_flat: bfloat16 [262144], P(('dp', 'fsdp')), may hold values from -1 to 1
- norm_gains: bfloat16 [1024], P(('dp', 'fsdp')), may hold values from 0.099609375 to 1.8984375
- gate_flat: bfloat16 [4096], P(('dp', 'fsdp')), may hold values from -0.25 to 0.25
- up_flat: bfloat16 [1048576], P(('dp', 'fsdp')), may hold values from -0.25 to 0.25
- down_flat: bfloat16 [1048576], P(('dp', 'fsdp')), may hold values from -0.125 to 0.125
Outputs:
- layer_out: bfloat16 [32768, 512], P(('dp', 'fsdp'))
- grad_input: bfloat16 [32768, 512], P(('dp', 'fsdp'))
- grad_qkv: float32 [786432], P(('dp', 'fsdp'))
- grad_out: float32 [262144], P(('dp', 'fsdp'))
- grad_gains: float32 [1024], P(('dp', 'fsdp'))
- grad_gate: float32 [4096], P(('dp', 'fsdp'))
- grad_up: float32 [1048576], P(('dp', 'fsdp'))
- grad_down: float32 [1048576], P(('dp', 'fsdp'))
Inputs may be any that keep to these rules, and one draw needn't show every extreme that they name: `doc_ids`: along each sequence the document numbers start at 0 and never fall; each document covers 1 to 768 positions, and one of each sequence exactly that many. `slot_ids`: positions within the first segment of the same sequence.
All inputs are finite; a program needn't handle non-finite values.
Results may differ from a plain program's by a relative error of at most 0.012.
The roundings to bfloat16 on the way count: a program that leaves them out, or rounds other values in their place, can miss the bound.
Values may be sent and summed in bfloat16 or wider, within the bound.
No kernel may reach another device: no remote copies, remote signals or barrier semaphores. Data moves between devices by JAX's collectives and lax.ppermute only.
A program may use at most 192 MiB of HBM per device.

v0:
```python
import math

import jax
import jax.numpy as jnp
from jax import lax
from jax.sharding import PartitionSpec as P

D = 512
H = 8
HD = 64
K = 4


def norm_forward(values, gain_vec):
    factor = lax.rsqrt(jnp.mean(values * values, axis=1, keepdims=True) + 1e-06)
    return (values * factor * gain_vec, factor)


def norm_backward(values, factor, gain_vec, upstream):
    inner = jnp.mean(upstream * gain_vec * values, axis=1, keepdims=True)
    return factor * gain_vec * upstream - values * (factor * factor * factor) * inner


def unpack_attn(pieces):
    gains_all = pieces[2].astype(jnp.float32)
    return (
        pieces[0].reshape(D, 3 * D),
        pieces[1].reshape(D, D),
        gains_all[:D],
        gains_all[D:],
        pieces[3].reshape(D, H),
    )


def block_scores(queries, key_rows, doc_block):
    seg_len = queries.shape[0]
    head_scale = 1.0 / math.sqrt(HD)
    query_h = queries.reshape(seg_len, H, HD)
    key_h = key_rows.reshape(seg_len, H, HD)
    scores = (
        jnp.einsum("ihd,jhd->hij", query_h, key_h, preferred_element_type=jnp.float32) * head_scale
    )
    places = lax.broadcasted_iota(jnp.int32, (seg_len, seg_len), 0)
    sources = lax.broadcasted_iota(jnp.int32, (seg_len, seg_len), 1)
    allowed = (sources <= places) & (doc_block[:, None] == doc_block[None, :])
    return jnp.where(allowed[None], scores, -1e30)


def block_forward(packed):
    queries, key_rows, value_rows, doc_block = packed
    seg_len = queries.shape[0]
    scores = block_scores(queries, key_rows, doc_block)
    row_peak = jnp.max(scores, axis=2, keepdims=True)
    expo_terms = jnp.exp(scores - row_peak)
    row_total = jnp.sum(expo_terms, axis=2, keepdims=True)
    attn_prob = (expo_terms / row_total).astype(jnp.bfloat16)
    local_h = jnp.einsum(
        "hij,jhd->ihd",
        attn_prob,
        value_rows.reshape(seg_len, H, HD),
        preferred_element_type=jnp.float32,
    )
    return (local_h.reshape(seg_len, H * HD), (row_peak + jnp.log(row_total))[:, :, 0])


def block_backward(packed):
    queries, key_rows, value_rows, doc_block, log_sums, d_local = packed
    seg_len = queries.shape[0]
    head_scale = 1.0 / math.sqrt(HD)
    query_h = queries.reshape(seg_len, H, HD)
    key_h = key_rows.reshape(seg_len, H, HD)
    value_h = value_rows.reshape(seg_len, H, HD)
    d_local_h = d_local.reshape(seg_len, H, HD)
    scores = block_scores(queries, key_rows, doc_block)
    attn_prob = jnp.exp(scores - log_sums[:, :, None])
    d_prob = jnp.einsum("ihd,jhd->hij", d_local_h, value_h, preferred_element_type=jnp.float32)
    d_values = jnp.einsum(
        "hij,ihd->jhd",
        attn_prob.astype(jnp.bfloat16),
        d_local_h,
        preferred_element_type=jnp.float32,
    )
    d_scores = (attn_prob * (d_prob - jnp.sum(attn_prob * d_prob, axis=2, keepdims=True))).astype(
        jnp.bfloat16
    )
    d_queries = (
        jnp.einsum("hij,jhd->ihd", d_scores, key_h, preferred_element_type=jnp.float32) * head_scale
    )
    d_keys = (
        jnp.einsum("hij,ihd->jhd", d_scores, query_h, preferred_element_type=jnp.float32)
        * head_scale
    )
    return (d_queries.reshape(seg_len, D), d_keys.reshape(seg_len, D), d_values.reshape(seg_len, D))


def pick_rows(table_rows, indices):
    return jax.vmap(lambda source_rows, picked: source_rows[picked])(table_rows, indices)


def spread_rows(update_rows, indices, length):
    return jax.vmap(
        lambda upd_rows, picked: jnp.zeros((length, D), jnp.float32).at[picked].add(upd_rows)
    )(update_rows, indices)


def local(
    inputs,
    cotangent,
    doc_ids,
    slot_ids,
    qkv_flat,
    out_flat,
    norm_gains,
    gate_flat,
    up_flat,
    down_flat,
):
    seq_count = doc_ids.shape[0]
    seq_len = doc_ids.shape[1]
    seg_len = seq_len // 2
    row_count = seq_count * seq_len
    block_count = seq_count * 2
    head_scale = 1.0 / math.sqrt(HD)
    attn_parts = (
        lax.all_gather(qkv_flat, ("dp", "fsdp"), axis=0, tiled=True),
        lax.all_gather(out_flat, ("dp", "fsdp"), axis=0, tiled=True),
        lax.all_gather(norm_gains, ("dp", "fsdp"), axis=0, tiled=True),
        lax.all_gather(gate_flat, ("dp", "fsdp"), axis=0, tiled=True),
    )
    ffn_parts = (
        lax.all_gather(up_flat, ("dp", "fsdp"), axis=0, tiled=True),
        lax.all_gather(down_flat, ("dp", "fsdp"), axis=0, tiled=True),
    )
    w_qkv, w_out, gain_one, gain_two, w_gate = unpack_attn(attn_parts)
    w_up = ffn_parts[0].reshape(D, -1)
    w_down = ffn_parts[1].reshape(-1, D)
    in_float = inputs.astype(jnp.float32)
    normed_one, factor_one = norm_forward(in_float, gain_one)
    hid_one = normed_one.astype(jnp.bfloat16)
    qkv_rows = jnp.dot(hid_one, w_qkv, preferred_element_type=jnp.float32).astype(jnp.bfloat16)
    query_rows = qkv_rows[:, :D]
    key_rows = qkv_rows[:, D : 2 * D]
    value_rows = qkv_rows[:, 2 * D :]
    gate_prob = jax.nn.sigmoid(jnp.dot(hid_one, w_gate, preferred_element_type=jnp.float32))
    query_blocks = query_rows.reshape(block_count, seg_len, D)
    key_blocks = key_rows.reshape(block_count, seg_len, D)
    value_blocks = value_rows.reshape(block_count, seg_len, D)
    doc_blocks = doc_ids.reshape(block_count, seg_len)
    local_out, log_sums = lax.map(
        block_forward, (query_blocks, key_blocks, value_blocks, doc_blocks)
    )
    local_out = local_out.reshape(row_count, D)
    query_two = (
        query_rows.reshape(seq_count, 2, seg_len, D)[:, 1]
        .astype(jnp.float32)
        .reshape(seq_count, seg_len, H, HD)
    )
    key_first = key_rows.reshape(seq_count, 2, seg_len, D)[:, 0]
    value_first = value_rows.reshape(seq_count, 2, seg_len, D)[:, 0]
    doc_pairs = doc_ids.reshape(seq_count, 2, seg_len)
    key_ret = (
        pick_rows(key_first, slot_ids).astype(jnp.float32).reshape(seq_count, seg_len, K, H, HD)
    )
    value_ret = (
        pick_rows(value_first, slot_ids).astype(jnp.float32).reshape(seq_count, seg_len, K, H, HD)
    )
    valid = pick_rows(doc_pairs[:, 0], slot_ids) == doc_pairs[:, 1][:, :, None]
    mem_score = jnp.sum(query_two[:, :, None] * key_ret, axis=4) * head_scale
    mem_score = jnp.where(valid[:, :, :, None], mem_score, -1e30)
    mem_peak = jnp.maximum(jnp.max(mem_score, axis=2, keepdims=True), 0.0)
    mem_expo = jnp.exp(mem_score - mem_peak)
    mem_prob = mem_expo / (jnp.exp(-mem_peak) + jnp.sum(mem_expo, axis=2, keepdims=True))
    mem_two = jnp.sum(mem_prob[..., None] * value_ret, axis=2).reshape(seq_count, seg_len, D)
    mem_out = jnp.stack([jnp.zeros_like(mem_two), mem_two], axis=1).reshape(row_count, D)
    gate_wide = jnp.repeat(gate_prob, HD, axis=1)
    mixed = (gate_wide * local_out + (1.0 - gate_wide) * mem_out).astype(jnp.bfloat16)
    resid = in_float + jnp.dot(mixed, w_out, preferred_element_type=jnp.float32)
    normed_two, factor_two = norm_forward(resid, gain_two)
    hid_two = normed_two.astype(jnp.bfloat16)
    upper = jnp.dot(hid_two, w_up, preferred_element_type=jnp.float32)
    activated, gelu_pull = jax.vjp(jax.nn.gelu, upper)
    act_rows = activated.astype(jnp.bfloat16)
    layer_out = (resid + jnp.dot(act_rows, w_down, preferred_element_type=jnp.float32)).astype(
        jnp.bfloat16
    )
    attn_parts = (
        lax.all_gather(qkv_flat, ("dp", "fsdp"), axis=0, tiled=True),
        lax.all_gather(out_flat, ("dp", "fsdp"), axis=0, tiled=True),
        lax.all_gather(norm_gains, ("dp", "fsdp"), axis=0, tiled=True),
        lax.all_gather(gate_flat, ("dp", "fsdp"), axis=0, tiled=True),
    )
    ffn_parts = (
        lax.all_gather(up_flat, ("dp", "fsdp"), axis=0, tiled=True),
        lax.all_gather(down_flat, ("dp", "fsdp"), axis=0, tiled=True),
    )
    w_qkv, w_out, gain_one, gain_two, w_gate = unpack_attn(attn_parts)
    w_up = ffn_parts[0].reshape(D, -1)
    w_down = ffn_parts[1].reshape(-1, D)
    cot_float = cotangent.astype(jnp.float32)
    d_act = jnp.dot(cotangent, w_down.T, preferred_element_type=jnp.float32)
    grad_down = jnp.dot(act_rows.T, cotangent, preferred_element_type=jnp.float32)
    d_upper = gelu_pull(d_act)[0].astype(jnp.bfloat16)
    grad_up = jnp.dot(hid_two.T, d_upper, preferred_element_type=jnp.float32)
    ffn_pieces = (grad_up.reshape(-1), grad_down.reshape(-1))
    ffn_grads = (
        lax.psum_scatter(ffn_pieces[0], ("dp", "fsdp"), scatter_dimension=0, tiled=True),
        lax.psum_scatter(ffn_pieces[1], ("dp", "fsdp"), scatter_dimension=0, tiled=True),
    )
    d_hid_two = jnp.dot(d_upper, w_up.T, preferred_element_type=jnp.float32)
    grad_gain_two = jnp.sum(d_hid_two * resid * factor_two, axis=0)
    d_resid = cot_float + norm_backward(resid, factor_two, gain_two, d_hid_two)
    d_resid_b = d_resid.astype(jnp.bfloat16)
    grad_out = jnp.dot(mixed.T, d_resid_b, preferred_element_type=jnp.float32)
    d_mixed = lax.optimization_barrier(
        jnp.dot(d_resid_b, w_out.T, preferred_element_type=jnp.float32).astype(jnp.bfloat16)
    ).astype(jnp.float32)
    d_local = (gate_wide * d_mixed).astype(jnp.bfloat16)
    d_mem = (1.0 - gate_wide) * d_mixed
    d_gate_sum = jnp.sum((d_mixed * (local_out - mem_out)).reshape(row_count, H, HD), axis=2)
    d_gate_logit = (d_gate_sum * gate_prob * (1.0 - gate_prob)).astype(jnp.bfloat16)
    d_query, d_key, d_value = lax.map(
        block_backward,
        (
            query_blocks,
            key_blocks,
            value_blocks,
            doc_blocks,
            log_sums,
            d_local.reshape(block_count, seg_len, D),
        ),
    )
    d_query = d_query.reshape(row_count, D)
    d_key = d_key.reshape(row_count, D)
    d_value = d_value.reshape(row_count, D)
    d_mem_two = d_mem.reshape(seq_count, 2, seg_len, H, HD)[:, 1]
    d_mem_prob = jnp.sum(d_mem_two[:, :, None] * value_ret, axis=4)
    d_mem_score = mem_prob * (d_mem_prob - jnp.sum(mem_prob * d_mem_prob, axis=2, keepdims=True))
    d_query_mem = (jnp.sum(d_mem_score[..., None] * key_ret, axis=2) * head_scale).reshape(
        seq_count, seg_len, D
    )
    d_key_ret = (d_mem_score[..., None] * query_two[:, :, None] * head_scale).reshape(
        seq_count, seg_len * K, D
    )
    d_value_ret = (mem_prob[..., None] * d_mem_two[:, :, None]).reshape(seq_count, seg_len * K, D)
    flat_slots = slot_ids.reshape(seq_count, seg_len * K)
    d_key_first = spread_rows(d_key_ret, flat_slots, seg_len)
    d_value_first = spread_rows(d_value_ret, flat_slots, seg_len)
    zero_rows = jnp.zeros_like(d_query_mem)
    d_query = d_query + jnp.stack([zero_rows, d_query_mem], axis=1).reshape(row_count, D)
    d_key = d_key + jnp.stack([d_key_first, zero_rows], axis=1).reshape(row_count, D)
    d_value = d_value + jnp.stack([d_value_first, zero_rows], axis=1).reshape(row_count, D)
    d_qkv = jnp.concatenate([d_query, d_key, d_value], axis=1).astype(jnp.bfloat16)
    grad_qkv = jnp.dot(hid_one.T, d_qkv, preferred_element_type=jnp.float32)
    grad_gate = jnp.dot(hid_one.T, d_gate_logit, preferred_element_type=jnp.float32)
    d_hid_one = jnp.dot(d_qkv, w_qkv.T, preferred_element_type=jnp.float32) + jnp.dot(
        d_gate_logit, w_gate.T, preferred_element_type=jnp.float32
    )
    grad_gain_one = jnp.sum(d_hid_one * in_float * factor_one, axis=0)
    grad_input = d_resid + norm_backward(in_float, factor_one, gain_one, d_hid_one)
    attn_pieces = (
        grad_qkv.reshape(-1),
        grad_out.reshape(-1),
        jnp.concatenate([grad_gain_one, grad_gain_two]),
        grad_gate.reshape(-1),
    )
    attn_grads = (
        lax.psum_scatter(attn_pieces[0], ("dp", "fsdp"), scatter_dimension=0, tiled=True),
        lax.psum_scatter(attn_pieces[1], ("dp", "fsdp"), scatter_dimension=0, tiled=True),
        lax.psum_scatter(attn_pieces[2], ("dp", "fsdp"), scatter_dimension=0, tiled=True),
        lax.psum_scatter(attn_pieces[3], ("dp", "fsdp"), scatter_dimension=0, tiled=True),
    )
    return (
        layer_out,
        grad_input.astype(jnp.bfloat16),
        attn_grads[0],
        attn_grads[1],
        attn_grads[2],
        attn_grads[3],
        ffn_grads[0],
        ffn_grads[1],
    )


def solution(mesh):
    placed = (
        P(("dp", "fsdp"), None),
        P(("dp", "fsdp"), None),
        P(("dp", "fsdp"), None),
        P(("dp", "fsdp"), None, None),
        P(("dp", "fsdp")),
        P(("dp", "fsdp")),
        P(("dp", "fsdp")),
        P(("dp", "fsdp")),
        P(("dp", "fsdp")),
        P(("dp", "fsdp")),
    )
    return jax.shard_map(
        local,
        mesh=mesh,
        in_specs=placed,
        out_specs=(
            P(("dp", "fsdp"), None),
            P(("dp", "fsdp"), None),
            P(("dp", "fsdp")),
            P(("dp", "fsdp")),
            P(("dp", "fsdp")),
            P(("dp", "fsdp")),
            P(("dp", "fsdp")),
            P(("dp", "fsdp")),
        ),
        check_vma=False,
    )
```

profile of v0, /device:TPU:0, one launch (start us, length us, event | category | flops | bytes accessed | tf_op | source)
XLA Modules:
  0.0 788.4 jit_solution(7990041569408061913)
XLA Ops:
  12.8 42.1 %all-reduce.4 = bf16[1024]{0:T(1024)(128)(2,1)S(1)} all-reduce(bf16[1024]{0:T(1024)(128)(2,1)S(1)} %dynamic-update-slice), channel_id=1, replica_groups=mesh['dp'=16,'fsdp'=2] {'dp','fsdp'}, use_global_device_ids=true, to_apply=%add.4 | all-reduce | flops 1024 | bytes 4096
  56.7 12.4 %gather_fusion = s32[2048]{0:T(1024)S(1)} fusion(s32[1,512]{1,0:T(1,128)S(1)} %get-tuple-element.271, s32[2048]{0:T(1024)S(1)} %reshape.713), kind=kCustom, calls=%fused_computation | custom fusion | bytes 32768 | tf_op jit(solution)/shard_map/vmap()/gather | solution.py:97
  70.6 40.0 %all-gather = bf16[32,1,128]{2,1,0:T(2,128)(2,1)S(1)} all-gather(bf16[1,1,128]{2,1,0:T(2,128)(2,1)S(1)} %bitcast.231), channel_id=1, replica_groups=mesh['dp'=16,'fsdp'=2] {'dp','fsdp'}, dimensions={0}, use_global_device_ids=true | all-gather | bytes 8448 | tf_op jit(solution)/shard_map/all_gather | solution.py:128
  110.8 38.5 %all_gather.27 = bf16[262144]{0:T(1024)(128)(2,1)S(1)} all-gather(bf16[8192]{0:T(1024)(128)(2,1)S(1)} %copy-done.44), channel_id=1, replica_groups=mesh['dp'=16,'fsdp'=2] {'dp','fsdp'}, dimensions={0}, use_global_device_ids=true | all-gather | bytes 540672 | tf_op jit(solution)/shard_map/all_gather | solution.py:126
  167.9 21.7 %gather_fusion.1 = bf16[2048,512]{1,0:T(8,128)(2,1)} fusion(bf16[1,512,512]{2,1,0:T(8,128)(2,1)S(1)} %slice_bitcast_fusion.1, s32[2048]{0:T(1024)S(1)} %reshape.713), kind=kCustom, calls=%fused_computation.1 | custom fusion | bytes 4210688 | tf_op jit(solution)/shard_map/vmap()/gather | solution.py:97
  189.5 6.7 reshape.705
  206.3 20.1 %while.26 = (s32[]{:T(128)}, f32[2,512,512]{1,2,0:T(8,128)}, f32[2,8,512]{2,1,0:T(8,128)S(1)}, bf16[2,512,512]{1,2,0:T(8,128)(2,1)}, s32[2,512]{1,0:T(2,128)S(1)...) while((s32[]{:T(128)}, f32[2,512,512]{1,2,0:T(8,128)}, ...), condition=%wide.region_4.5_spmd, body=%wide.region_1.4_spmd.sunk | while | flops 562819072 | bytes 50993320 | solution.py:149
  226.4 6.6 multiply_reduce_fusion.4
  233.1 21.7 %gather_fusion.2 = bf16[2048,512]{1,0:T(8,128)(2,1)} fusion(bf16[1,512,512]{2,1,0:T(8,128)(2,1)S(1)} %slice_bitcast_fusion, s32[2048]{0:T(1024)S(1)} %reshape.713), kind=kCustom, calls=%fused_computation.2 | custom fusion | bytes 4210688 | tf_op jit(solution)/shard_map/vmap()/gather | solution.py:97
  254.8 6.7 reshape.706
  269.9 7.0 multiply_reduce_fusion.3
  293.9 6.6 reshape.708
  300.6 6.7 reshape.707
  324.6 7.3 fusion.61
  336.4 9.7 %fusion.19 = bf16[1024,2048]{1,0:T(8,128)(2,1)S(1)} fusion(f32[1024,2048]{1,0:T(8,128)} %fusion.61, bf16[1024,512]{1,0:T(8,128)(2,1)} %param.15, bf16[2048,512]{1,0:T(8,128)(2,1)} %reshape.673), kind=kOutput, calls=%fused_computation.50 | convolution fusion | flops 2189426688 | bytes 15728640 | tf_op jit(solution)/shard_map/dot_general | solution.py:200
  383.2 7.5 reshape.747
  390.6 13.5 %scatter_custom_fusion.1 = f32[512,512]{1,0:T(8,128)S(1)} fusion(s32[2048]{0:T(1024)} %broadcast_select_fusion, f32[2048,512]{1,0:T(8,128)} %reshape.747, f32[]{:T(128)} %constant.43.clone.1), kind=kCustom, calls=%fused_computation.121 | custom fusion | flops 1048576 | bytes 1049088
  405.8 69.7 %while.27 = (s32[]{:T(128)}, f32[2,512,512]{2,1,0:T(8,128)}, f32[2,512,512]{2,1,0:T(8,128)}, f32[2,512,512]{2,1,0:T(8,128)}, bf16[2,512,512]{1,2,0:T(8,128)(2,1)...) while((s32[]{:T(128)}, f32[2,512,512]{2,1,0:T(8,128)}, ...), condition=%wide.region_13.14_spmd, body=%wide.region_11.13_spmd.sunk | while | flops 1374941184 | bytes 130668768 | solution.py:221
  483.7 11.5 %multiply_reduce_fusion.1 = (f32[512,8,64]{2,1,0:T(8,128)}, f32[512,4,8,64]{3,2,1,0:T(8,128)}) fusion(f32[512,4,8,64]{3,2,1,0:T(8,128)} %reshape.708, f32[512,4,8]{2,1,0:T(4,128)S(1)} %subtract_multiply_fusion, f32[512,8,64]{2,1,0:T(8,128)S(1)} %copy-done.8), kind=kLoop, calls=%fused_computation.52 | loop fusion | flops 3932160 | bytes 10551296 | tf_op jit(solution)/shard_map/reduce_sum | solution.py:238
  495.1 7.5 reshape.739
  502.6 13.5 %scatter_custom_fusion = f32[512,512]{1,0:T(8,128)S(1)} fusion(s32[2048]{0:T(1024)} %broadcast_select_fusion, f32[2048,512]{1,0:T(8,128)} %reshape.739, f32[]{:T(128)} %constant.43.clone.1), kind=kCustom, calls=%fused_computation.123 | custom fusion | flops 1048576 | bytes 1049088
  544.8 9.9 %add_convert_fusion = bf16[1024,512]{0,1:T(8,128)(2,1)} fusion(f32[1024,512]{0,1:T(8,128)} %get-tuple-element.277, bf16[2048,512]{1,0:T(8,128)(2,1)} %reshape.673, f32[1024,2048]{1,0:T(8,128)} %fusion.61), kind=kOutput, calls=%fused_computation.97 | convolution fusion | flops 2167406592 | bytes 13631488 | tf_op jit(solution)/shard_map/dot_general | solution.py:183
  571.3 38.9 %all-reduce.11 = (f32[1024]{0:T(1024)S(1)}, f32[4096]{0:T(1024)S(1)}) all-reduce(f32[1024]{0:T(1024)S(1)} %pad_maximum_fusion.3, f32[4096]{0:T(1024)S(1)} %reshape.689), channel_id=4, replica_groups=mesh['dp'=16,'fsdp'=2] {'dp','fsdp'}, use_global_device_ids=true, to_apply=%region_25.26.clone | all-reduce | flops 5120 | bytes 40960
  611.4 164.0 %all-reduce.15.cloned.1.call-done = (f32[786432]{0:T(1024)}, f32[262144]{0:T(1024)}, f32[1048576]{0:T(1024)}, f32[1048576]{0:T(1024)}) async-done(((f32[786432]{0:T(1024)}, f32[262144]{0:T(1024)}, f32[1048576]{0:T(1024)}, f32[1048576]{0:T(1024)}), (f32[786432]{0:T(1024)}, f32[262144]{0:T(1024)}, f32[1048576]{0:T(1024)}, f32[1048576]{0:T(1024)})) %all-reduce.15.cloned.1.call-update) | async-done | bytes 12582928
  (296 shorter events, 272.7 us)
Async XLA Ops:
  7.2 5.4 copy-start.50
  7.2 150.8 %all-gather.5.cloned.1.call-start = ((), (), s32[]{:S(2)}) async-start(), calls=%async_computation | async-start | bytes 1622016 | tf_op jit(solution)/shard_map/all_gather | solution.py:125
  7.9 48.8 %copy-start.45 = (s32[1,1024]{1,0:T(1,128)S(1)}, s32[1,1024]{1,0:T(1,128)}, u32[]{:S(2)}) copy-start(s32[1,1024]{1,0:T(1,128)} %param.16) | copy-start | bytes 12292
  7.9 312.3 %all-gather.7.cloned.1.call-start = ((), (), s32[]{:S(2)}) async-start(), calls=%async_computation.1 | async-start | bytes 2162688 | tf_op jit(solution)/shard_map/all_gather | solution.py:131
  8.7 323.2 %all-gather.9.cloned.1.call-start = ((), (), s32[]{:S(2)}) async-start(), calls=%async_computation.2 | async-start | bytes 2162688 | tf_op jit(solution)/shard_map/all_gather | solution.py:132
  9.4 766.0 %all-reduce.15.cloned.1.call-start = ((), (), s32[]{:S(2)}) async-start(), calls=%async_computation.3 | async-start | bytes 25165824
  12.5 305.6 %copy-start.3 = (bf16[1024,512]{0,1:T(8,128)(2,1)}, bf16[1024,512]{0,1:T(8,128)(2,1)S(1)}, u32[]{:S(2)}) copy-start(bf16[1024,512]{0,1:T(8,128)(2,1)S(1)} %copy.132) | copy-start | bytes 3145732
  55.5 106.8 %copy-start.41 = (f32[512]{0:T(512)}, f32[512]{0:T(512)S(1)}, u32[]{:S(2)}) copy-start(f32[512]{0:T(512)S(1)} %get-tuple-element.273) | copy-start | bytes 6148
  56.3 106.0 %copy-start.38 = (f32[1024]{0:T(1024)}, f32[1024]{0:T(1024)S(1)}, u32[]{:S(2)}) copy-start(f32[1024]{0:T(1024)S(1)} %get-tuple-element.267) | copy-start | bytes 12292
  56.7 13.9 %copy-start.47 = (bf16[128]{0:T(256)(128)(2,1)S(1)}, bf16[128]{0:T(256)(128)(2,1)}, u32[]{:S(2)}) copy-start(bf16[128]{0:T(256)(128)(2,1)} %param.21) | copy-start | bytes 772
  56.7 54.1 %copy-start.44 = (bf16[8192]{0:T(1024)(128)(2,1)S(1)}, bf16[8192]{0:T(1024)(128)(2,1)}, u32[]{:S(2)}) copy-start(bf16[8192]{0:T(1024)(128)(2,1)} %param.19) | copy-start | bytes 49156
  69.4 82.7 %copy-start.49 = (s32[2]{0:T(128)S(1)}, s32[2]{0:T(128)}, u32[]{:S(2)}) copy-start(s32[2]{0:T(128)} %constant.102) | copy-start | bytes 28
  69.4 82.8 %copy-start.48 = (s32[2]{0:T(128)S(1)}, s32[2]{0:T(128)}, u32[]{:S(2)}) copy-start(s32[2]{0:T(128)} %constant.99) | copy-start | bytes 28
  110.8 41.9 %copy-start.34 = (bf16[512,8]{1,0:T(8,128)(2,1)}, bf16[512,8]{1,0:T(8,128)(2,1)S(1)}, u32[]{:S(2)}) copy-start(bf16[512,8]{1,0:T(8,128)(2,1)S(1)} %reshape.659) | copy-start | bytes 24580
  152.7 162.6 %copy-start.36 = (f32[1024,8]{0,1:T(8,128)}, f32[1024,8]{0,1:T(8,128)S(1)}, u32[]{:S(2)}) copy-start(f32[1024,8]{0,1:T(8,128)S(1)} %get-tuple-element.275) | copy-start | bytes 98308
  166.8 34.5 %copy-start.20 = (bf16[1024,512]{1,0:T(8,128)(2,1)}, bf16[1024,512]{1,0:T(8,128)(2,1)S(1)}, u32[]{:S(2)}) copy-start(bf16[1024,512]{1,0:T(8,128)(2,1)S(1)} %get-tuple-element.263) | copy-start | bytes 3145732
  226.4 6.6 copy-start.21
  336.4 9.7 %copy-start.19 = (bf16[512,2048]{1,0:T(8,128)(2,1)S(1)}, bf16[512,2048]{1,0:T(8,128)(2,1)}, u32[]{:S(2)}) copy-start(bf16[512,2048]{1,0:T(8,128)(2,1)} %reshape.672) | copy-start | bytes 6291460
  377.5 5.6 copy-start.7
  415.2 5.2 slice-start
  415.3 5.9 slice-start.1
  450.0 5.2 slice-start
  450.0 5.9 slice-start.1
  475.5 6.6 copy-start.11
  (38 other events, 95.9 us)
Sparse Core Ops, SparseCore 0:
  10.9 57.6 all-gather.4
  71.5 55.5 all-gather.6
  130.0 56.0 all-gather.8
  544.9 230.3 all-reduce.14
where the time goes:
time: 799 us; the launch traced here: 788 us
  local copies, waits for them, and re-layouts  240 us (30%)
  waiting for transfers between devices  166 us (21%)
  blocking collectives  159 us (20%)
  matrix products  106 us (13%)
  other arithmetic  101 us (13%)
  between operations  15 us (2%)
    unnamed x5, waiting for transfers between devices  166 us
    unnamed x2, blocking collectives  81 us
    gather x7, local copies, waits for them, and re-layouts, pick_rows(): source_rows[picked]  56.4 us
    all_gather x1, blocking collectives, local(): lax.all_gather(gate_flat, ('dp', 'fsdp'), axis=0, tiled=True)  40 us
    all_gather x1, blocking collectives, local(): lax.all_gather(out_flat, ('dp', 'fsdp'), axis=0, tiled=True)  38.5 us
    unnamed x115, local copies, waits for them, and re-layouts  36 us
    unnamed x6, other arithmetic  28.4 us
  transfers between devices with their start and end apart: 4, of which 1 were waited for; matrix products, arithmetic and copies ran while one was open for 28% of the time, Pallas kernels for 0%

commit v1 on v0

v1 whole, which is shorter than its diff:
```python
import jax
import jax.numpy as jnp
from jax import lax
from jax.experimental import pallas as pl
from jax.experimental.pallas import tpu as pltpu
from jax.sharding import PartitionSpec as P

D = 512
H = 8
HD = 64
K = 4
FF = 2048
SEQ = 1024
SEG = 512
PIECES = 32
ROWS = D // PIECES
EXT = 3 * D + 128
GCOL = 8
GLEN = 2 * D // PIECES
NEG = -1e30
BF = jnp.bfloat16
F32 = jnp.float32
AXES = ("dp", "fsdp")
NT = (((1,), (1,)), ((), ()))
TN = (((0,), (0,)), ((), ()))
ANY = pl.BlockSpec(memory_space=pl.ANY)
VLIMIT = 60 * 1024 * 1024


def mm(a, b):
    return jnp.dot(a, b, preferred_element_type=F32)


def mm_nt(a, b):
    return lax.dot_general(a, b, NT, preferred_element_type=F32)


def mm_tn(a, b):
    return lax.dot_general(a, b, TN, preferred_element_type=F32)


def perm_z(v, shift):
    return lax.ppermute(v, "dp", [(i, (i + 4 * shift) % 16) for i in range(16)])


def perm_bit(v, bit):
    return lax.ppermute(v, "dp", [(i, i ^ bit) for i in range(16)])


def perm_core(v):
    return lax.ppermute(v, "fsdp", [(0, 1), (1, 0)])


def gather_z(shard):
    return jnp.stack([shard] + [perm_z(shard, -k) for k in (1, 2, 3)])


def gather_rest(stacked, first, second):
    wider = jnp.concatenate([stacked, perm_bit(stacked, first)])
    wider = jnp.concatenate([wider, perm_bit(wider, second)])
    return (wider, perm_core(wider))


def reduce_core(keep, send):
    return keep.astype(F32) + perm_core(send).astype(F32)


def reduce_bit(total, bit):
    half = total.shape[0] // 2
    return total[:half] + perm_bit(total[half:].astype(BF), bit).astype(F32)


def reduce_z(total):
    out = total[0]
    for k in (1, 2, 3):
        out = out + perm_z(total[k].astype(BF), k).astype(F32)
    return out


def piece_owner(piece, x_first):
    place = lax.axis_index("dp")
    z, y, x = place >> 2, (place >> 1) & 1, place & 1
    kz, low, high, kc = piece & 3, (piece >> 2) & 1, (piece >> 3) & 1, piece >> 4
    kx, ky = (low, high) if x_first else (high, low)
    chip = ((((z + kz) & 3) * 2 + (y ^ ky)) * 2) + (x ^ kx)
    return chip * 2 + (lax.axis_index("fsdp") ^ kc)


def owner_fn(relative, x_first):
    if relative:
        return lambda piece: piece_owner(piece, x_first)
    return lambda piece: piece


def bias_kernel(doc_row, doc_col, slots, bias):
    sources = lax.broadcasted_iota(jnp.int32, (SEG, SEG), 0)
    places = lax.broadcasted_iota(jnp.int32, (SEG, SEG), 1)
    for seg in range(2):
        part = slice(seg * SEG, (seg + 1) * SEG)
        same = doc_col[part, :] == doc_row[:, part]
        bias[seg] = jnp.where((sources <= places) & same, 0.0, NEG)
    count = jnp.zeros((SEG, SEG), F32)
    for c in range(K):
        count = count + jnp.where(sources == slots[c : c + 1, :], 1.0, 0.0)
    kept = (doc_col[0:SEG, :] == doc_row[:, SEG : 2 * SEG]) & (count > 0.0)
    bias[2] = jnp.where(kept, jnp.log(jnp.maximum(count, 1.0)), NEG)


def rows_from_ext(ext):
    pick = lax.broadcasted_iota(jnp.int32, (PIECES, D), 1) == ROWS * lax.broadcasted_iota(
        jnp.int32, (PIECES, D), 0
    )
    gains = mm(pick.astype(BF), ext).astype(BF)
    source = lax.broadcasted_iota(jnp.int32, (128, D), 0) - GCOL
    column = lax.broadcasted_iota(jnp.int32, (128, D), 1)
    spread = mm(gains, (source == (column & (GLEN - 1))).astype(BF))
    piece = lax.broadcasted_iota(jnp.int32, (PIECES, D), 0)
    block = lax.broadcasted_iota(jnp.int32, (PIECES, D), 1) // GLEN
    one = jnp.sum(jnp.where(block == piece, spread, 0.0), axis=0, keepdims=True)
    two = jnp.sum(jnp.where(block + D // GLEN == piece, spread, 0.0), axis=0, keepdims=True)
    return one, two


def ext_from_rows(one, two):
    piece = lax.broadcasted_iota(jnp.int32, (PIECES, D), 0)
    block = lax.broadcasted_iota(jnp.int32, (PIECES, D), 1) // GLEN
    laid = jnp.where(block == piece, one, 0.0) + jnp.where(block + D // GLEN == piece, two, 0.0)
    column = lax.broadcasted_iota(jnp.int32, (D, 128), 0)
    target = lax.broadcasted_iota(jnp.int32, (D, 128), 1) - GCOL
    packed = mm(laid.astype(BF), (target == (column & (GLEN - 1))).astype(BF)).astype(BF)
    pick = lax.broadcasted_iota(jnp.int32, (D, PIECES), 0) == ROWS * lax.broadcasted_iota(
        jnp.int32, (D, PIECES), 1
    )
    return mm(pick.astype(BF), packed)


def start_pieces(parts, owner, make):
    base = 0
    for part in parts:
        for i in range(part.shape[0]):
            make(part.at[i], owner(base + i)).start()
        base += part.shape[0]


def head_half(rows, upper_half):
    blank = jnp.zeros_like(rows)
    return jnp.concatenate([blank, rows] if upper_half else [rows, blank], axis=0)


def attention_forward_kernel(owner, count_a, count_b, *refs):
    x, bias = refs[:2]
    parts_a = refs[2 : 2 + count_a]
    parts_b = refs[2 + count_a : 2 + count_a + count_b]
    outs = refs[2 + count_a + count_b :]
    qkvt_o, vtok_o, hidt_o, w_o, gatet, gains, probs, local_t, mem_t, inv_sums, mixed_t, mixed = (
        outs[:12]
    )
    w_vm, ktok, vtok, qkvt, hidt, in_sem, out_sem = outs[12:]
    pair = pl.program_id(0)
    half = w_vm.shape[1] - parts_b[0].shape[2]

    @pl.when(pair == 0)
    def _():
        start_pieces(
            parts_a,
            owner[0],
            lambda src, d: pltpu.make_async_copy(
                src,
                w_vm.at[pl.ds(pl.multiple_of(d * ROWS, ROWS), ROWS), pl.ds(0, half)],
                in_sem,
            ),
        )
        start_pieces(
            parts_b,
            owner[1],
            lambda src, d: pltpu.make_async_copy(
                src,
                w_vm.at[pl.ds(pl.multiple_of(d * ROWS, ROWS), ROWS), pl.ds(half, EXT - half)],
                in_sem,
            ),
        )
        pltpu.make_async_copy(w_o, w_vm, in_sem).wait()
        g_one, g_two = rows_from_ext(w_vm[:, 3 * D :])
        gains[...] = jnp.concatenate([g_one, g_two], axis=0)

        @pl.loop(0, 4)
        def _(block):
            rows = pl.ds(pl.multiple_of(block * 256, 256), 256)
            xf = x[rows, :].astype(F32)
            factor = lax.rsqrt(jnp.mean(xf * xf, axis=1, keepdims=True) + 1e-06)
            hid = (xf * factor * g_one).astype(BF)
            out = mm(hid, w_vm[...])
            ktok[rows, :] = out[:, D : 2 * D].astype(BF)
            vtok[rows, :] = out[:, 2 * D : 3 * D].astype(BF)
            qkvt[0:D, rows] = (out[:, :D].astype(BF) * 0.125).T
            qkvt[D : 2 * D, rows] = out[:, D : 2 * D].astype(BF).T
            qkvt[2 * D : 3 * D, rows] = out[:, 2 * D : 3 * D].astype(BF).T
            gatet[:, rows] = jax.nn.sigmoid(out[:, 3 * D :]).T[0:H, :]
            hidt[:, rows] = hid.T

        pltpu.make_async_copy(qkvt, qkvt_o, out_sem.at[0]).start()
        pltpu.make_async_copy(vtok, vtok_o, out_sem.at[1]).start()
        pltpu.make_async_copy(hidt, hidt_o, out_sem.at[2]).start()
        pltpu.make_async_copy(w_vm, w_o, out_sem.at[3]).start()

    lanes = pl.ds(pl.multiple_of(pair * 128, 128), 128)

    def head_rows(third, hh, columns):
        start = pl.multiple_of(third * D + pair * 128 + hh * HD, HD)
        return qkvt[pl.ds(start, HD), columns]

    for hh in range(2):
        rows = slice(hh * HD, (hh + 1) * HD)
        gate = gatet[pl.ds(2 * pair + hh, 1), :]
        base = 0
        for seg in range(3):
            for ib in range(2):
                key_first = SEG if seg == 1 else 0
                key_count = SEG if seg == 2 else 256 * (ib + 1)
                column = (0 if seg == 0 else SEG) + 256 * ib
                query = head_half(head_rows(0, hh, slice(column, column + 256)), hh)
                keys = ktok[key_first : key_first + key_count, lanes]
                score = mm(keys, query) + bias[seg, 0:key_count, 256 * ib : 256 * ib + 256]
                peak = jnp.max(score, axis=0, keepdims=True)
                if seg == 2:
                    peak = jnp.maximum(peak, 0.0)
                expo = jnp.exp(score - peak)
                total = jnp.sum(expo, axis=0, keepdims=True)
                if seg == 2:
                    total = total + jnp.exp(-peak)
                expo_b = expo.astype(BF)
                probs[0, hh, base : base + key_count, :] = expo_b
                base += key_count
                inverse = 1.0 / total
                value = head_rows(2, hh, slice(key_first, key_first + key_count))
                found = mm(value, expo_b) * inverse
                if seg < 2:
                    local_t[rows, column : column + 256] = found
                    inv_sums[0, hh : hh + 1, column : column + 256] = inverse
                    if seg == 0:
                        mixed_t[rows, column : column + 256] = (
                            gate[:, column : column + 256] * found
                        ).astype(BF)
                else:
                    mem_t[rows, 256 * ib : 256 * ib + 256] = found
                    inv_sums[0, 2 + hh : 3 + hh, column - SEG : column - SEG + 256] = inverse
                    here = gate[:, column : column + 256]
                    mixed_t[rows, column : column + 256] = (
                        here * local_t[rows, column : column + 256] + (1.0 - here) * found
                    ).astype(BF)
    inv_sums[0, 2:4, SEG:] = jnp.zeros((2, SEG), F32)
    mixed[...] = mixed_t[...].T

    @pl.when(pair == 3)
    def _():
        pltpu.make_async_copy(qkvt, qkvt_o, out_sem.at[0]).wait()
        pltpu.make_async_copy(vtok, vtok_o, out_sem.at[1]).wait()
        pltpu.make_async_copy(hidt, hidt_o, out_sem.at[2]).wait()
        pltpu.make_async_copy(w_vm, w_o, out_sem.at[3]).wait()


PROB_ROWS = 2 * 768 + 1024


def attention_forward(x, bias, parts_a, parts_b, owner):
    const2 = lambda p: (0, 0)

    def body(*refs):
        attention_forward_kernel(owner, len(parts_a), len(parts_b), *refs)

    return pl.pallas_call(
        body,
        grid=(4,),
        in_specs=[
            pl.BlockSpec((SEQ, D), const2),
            pl.BlockSpec((3, SEG, SEG), lambda p: (0, 0, 0)),
        ]
        + [ANY] * (len(parts_a) + len(parts_b)),
        out_specs=[
            ANY,
            ANY,
            ANY,
            ANY,
            pl.BlockSpec((H, SEQ), const2),
            pl.BlockSpec((2, D), const2),
            pl.BlockSpec((1, 2, PROB_ROWS, 256), lambda p: (p, 0, 0, 0)),
            pl.BlockSpec((128, SEQ), lambda p: (p, 0)),
            pl.BlockSpec((128, SEG), lambda p: (p, 0)),
            pl.BlockSpec((1, 4, SEQ), lambda p: (p, 0, 0)),
            pl.BlockSpec((128, SEQ), lambda p: (p, 0)),
            pl.BlockSpec((SEQ, 128), lambda p: (0, p)),
        ],
        out_shape=[
            jax.ShapeDtypeStruct((3 * D, SEQ), BF),
            jax.ShapeDtypeStruct((SEQ, D), BF),
            jax.ShapeDtypeStruct((D, SEQ), BF),
            jax.ShapeDtypeStruct((D, EXT), BF),
            jax.ShapeDtypeStruct((H, SEQ), F32),
            jax.ShapeDtypeStruct((2, D), F32),
            jax.ShapeDtypeStruct((4, 2, PROB_ROWS, 256), BF),
            jax.ShapeDtypeStruct((D, SEQ), F32),
            jax.ShapeDtypeStruct((D, SEG), F32),
            jax.ShapeDtypeStruct((4, 4, SEQ), F32),
            jax.ShapeDtypeStruct((D, SEQ), BF),
            jax.ShapeDtypeStruct((SEQ, D), BF),
        ],
        scratch_shapes=[
            pltpu.VMEM((D, EXT), BF),
            pltpu.VMEM((SEQ, D), BF),
            pltpu.VMEM((SEQ, D), BF),
            pltpu.VMEM((3 * D, SEQ), BF),
            pltpu.VMEM((D, SEQ), BF),
            pltpu.SemaphoreType.DMA,
            pltpu.SemaphoreType.DMA((4,)),
        ],
        compiler_params=pltpu.CompilerParams(vmem_limit_bytes=VLIMIT),
        cost_estimate=pl.CostEstimate(
            flops=12_000_000_000, bytes_accessed=30_000_000, transcendentals=6_000_000
        ),
        name="attention_forward",
    )(x, bias, *parts_a, *parts_b)


def ffn_kernel(owner_u, owner_d, count_u, count_d, split, *refs):
    x, cot, mixed, mixed_t, gains = refs[:5]
    parts_u = refs[5 : 5 + count_u]
    parts_d = refs[5 + count_u : 5 + count_u + count_d]
    outs = refs[5 + count_u + count_d :]
    layer_out, d_resid_o, dmix_t, dgain = outs[:4]
    count_o = 2 if split else 1
    grads_u = outs[4 : 4 + count_o]
    grads_d = outs[4 + count_o : 4 + 2 * count_o]
    rest = outs[4 + 2 * count_o :]
    w_out, w_up, w_dn, resid, hid, hidt, oacc, dacc, g_out, g_up, g_dn, in_sem, out_sem = rest
    step = pl.program_id(0)
    per = PIECES // count_o

    @pl.when(step == 0)
    def _():
        def load_u(first):
            def make(src, d):
                rows = pl.ds(pl.multiple_of(d * ROWS, ROWS), ROWS)
                if first:
                    return pltpu.make_async_copy(src.at[0], w_out.at[rows, :], in_sem.at[0])
                return pltpu.make_async_copy(
                    src.at[pl.ds(1, 4)], w_up.at[:, rows, :], in_sem.at[1]
                )

            return make

        start_pieces(parts_u, owner_u, load_u(True))
        start_pieces(parts_u, owner_u, load_u(False))
        start_pieces(
            parts_d,
            owner_d,
            lambda src, d: pltpu.make_async_copy(
                src, w_dn.at[pl.ds(pl.multiple_of(d * 64, 64), 64), :], in_sem.at[2]
            ),
        )
        pltpu.make_async_copy(g_out, w_out, in_sem.at[0]).wait()

        @pl.loop(0, 4)
        def _(block):
            rows = pl.ds(pl.multiple_of(block * 256, 256), 256)
            value = x[rows, :].astype(F32) + mm(mixed[rows, :], w_out[...])
            factor = lax.rsqrt(jnp.mean(value * value, axis=1, keepdims=True) + 1e-06)
            normed = (value * factor * gains[1:2, :]).astype(BF)
            resid[rows, :] = value
            hid[rows, :] = normed
            hidt[:, rows] = normed.T

        oacc[...] = jnp.zeros_like(oacc)
        dacc[...] = jnp.zeros_like(dacc)
        pltpu.make_async_copy(g_up, w_up, in_sem.at[1]).wait()
        pltpu.make_async_copy(g_dn, w_dn, in_sem.at[2]).wait()

    quarter = step // 2
    lanes = pl.ds(pl.multiple_of((step % 2) * 256, 256), 256)
    ff_rows = pl.ds(pl.multiple_of(step * 256, 256), 256)
    wu = w_up[quarter, :, lanes]
    wd = w_dn[ff_rows, :]
    upper = mm(hid[...], wu)
    c0 = 0.7978845608028654
    c1 = 0.044715
    square = upper * upper
    tanh = jnp.tanh(c0 * upper * (1.0 + c1 * square))
    half_t = 0.5 * tanh + 0.5
    act = (upper * half_t).astype(BF)
    slope = half_t + 0.5 * upper * (1.0 - tanh * tanh) * (c0 * (1.0 + 3.0 * c1 * square))
    d_act = mm_nt(cot[...], wd)
    d_up = (d_act * slope).astype(BF)
    oacc[...] += mm(act, wd)
    g_dn[ff_rows, :] = mm_tn(act, cot[...]).astype(BF)
    g_up[quarter, :, lanes] = mm(hidt[...], d_up).astype(BF)
    dacc[...] += mm_nt(d_up, wu)

    @pl.when(step == 7)
    def _():
        for piece in range(PIECES):
            d = owner_d(piece)
            pltpu.make_async_copy(
                g_dn.at[pl.ds(pl.multiple_of(d * 64, 64), 64), :],
                grads_d[piece // per].at[piece % per],
                out_sem.at[0],
            ).start()
            d = owner_u(piece)
            pltpu.make_async_copy(
                g_up.at[:, pl.ds(pl.multiple_of(d * ROWS, ROWS), ROWS), :],
                grads_u[piece // per].at[piece % per, pl.ds(1, 4)],
                out_sem.at[1],
            ).start()
        g_two = gains[1:2, :]
        dgain[...] = jnp.zeros_like(dgain)

        @pl.loop(0, 4)
        def _(block):
            rows = pl.ds(pl.multiple_of(block * 256, 256), 256)
            value = resid[rows, :]
            factor = lax.rsqrt(jnp.mean(value * value, axis=1, keepdims=True) + 1e-06)
            layer_out[rows, :] = (value + oacc[rows, :]).astype(BF)
            d_hid = dacc[rows, :]
            dgain[...] += jnp.sum(d_hid * value * factor, axis=0, keepdims=True)
            scaled = d_hid * g_two
            inner = jnp.mean(scaled * value, axis=1, keepdims=True)
            d_resid = cot[rows, :].astype(F32) + (
                factor * scaled - value * (factor * factor * factor * inner)
            )
            d_resid_o[rows, :] = d_resid
            d_resid_b = d_resid.astype(BF)
            hid[rows, :] = d_resid_b
            dmix_t[:, rows] = mm_nt(w_out[...], d_resid_b).astype(BF)

        g_out[...] = mm(mixed_t[...], hid[...]).astype(BF)
        for piece in range(PIECES):
            d = owner_u(piece)
            pltpu.make_async_copy(
                g_out.at[pl.ds(pl.multiple_of(d * ROWS, ROWS), ROWS), :],
                grads_u[piece // per].at[piece % per, 0],
                out_sem.at[2],
            ).start()
        pltpu.make_async_copy(g_dn, w_dn, out_sem.at[0]).wait()
        pltpu.make_async_copy(g_up, w_up, out_sem.at[1]).wait()
        pltpu.make_async_copy(g_out, w_out, out_sem.at[2]).wait()


def ffn(x, cot, mixed, mixed_t, gains, parts_u, parts_d, owner_u, owner_d, split):
    count_o = 2 if split else 1
    whole = pl.BlockSpec(memory_space=pltpu.VMEM)

    def body(*refs):
        ffn_kernel(owner_u, owner_d, len(parts_u), len(parts_d), split, *refs)

    const2 = lambda p: (0, 0)
    return pl.pallas_call(
        body,
        grid=(8,),
        in_specs=[
            pl.BlockSpec((SEQ, D), const2),
            pl.BlockSpec((SEQ, D), const2),
            pl.BlockSpec((SEQ, D), const2),
            pl.BlockSpec((D, SEQ), const2),
            pl.BlockSpec((2, D), const2),
        ]
        + [ANY] * (len(parts_u) + len(parts_d)),
        out_specs=[
            pl.BlockSpec((SEQ, D), const2),
            pl.BlockSpec((SEQ, D), const2),
            pl.BlockSpec((D, SEQ), const2),
            pl.BlockSpec((1, D), const2),
        ]
        + [ANY] * (2 * count_o),
        out_shape=[
            jax.ShapeDtypeStruct((SEQ, D), BF),
            jax.ShapeDtypeStruct((SEQ, D), F32),
            jax.ShapeDtypeStruct((D, SEQ), BF),
            jax.ShapeDtypeStruct((1, D), F32),
        ]
        + [jax.ShapeDtypeStruct((PIECES // count_o, 5, ROWS, D), BF)] * count_o
        + [jax.ShapeDtypeStruct((PIECES // count_o, 64, D), BF)] * count_o,
        scratch_shapes=[
            pltpu.VMEM((D, D), BF),
            pltpu.VMEM((4, D, D), BF),
            pltpu.VMEM((FF, D), BF),
            pltpu.VMEM((SEQ, D), F32),
            pltpu.VMEM((SEQ, D), BF),
            pltpu.VMEM((D, SEQ), BF),
            pltpu.VMEM((SEQ, D), F32),
            pltpu.VMEM((SEQ, D), F32),
            pltpu.VMEM((D, D), BF),
            pltpu.VMEM((4, D, D), BF),
            pltpu.VMEM((FF, D), BF),
            pltpu.SemaphoreType.DMA((3,)),
            pltpu.SemaphoreType.DMA((3,)),
        ],
        compiler_params=pltpu.CompilerParams(vmem_limit_bytes=VLIMIT),
        cost_estimate=pl.CostEstimate(
            flops=15_000_000_000, bytes_accessed=20_000_000, transcendentals=2_000_000
        ),
        name="feed_forward",
    )(x, cot, mixed, mixed_t, gains, *parts_u, *parts_d)


def attention_backward_kernel(owner, split, *refs):
    (x, d_resid, dgain_two, gains, gatet, w, hidt, probs, local_t, mem_t, inv_sums, dmix_t) = refs[
        :12
    ]
    qt, kt, vt, vtok = refs[12:16]
    count_o = 2 if split else 1
    grad_in = refs[16]
    grads = refs[17 : 17 + count_o]
    dqkvt, g_ext, out_sem = refs[17 + count_o :]
    pair = pl.program_id(0)
    per = PIECES // count_o

    @pl.when(pair == 0)
    def _():
        dqkvt[3 * D :, :] = jnp.zeros((128, SEQ), BF)

    for hh in range(2):
        rows = slice(hh * HD, (hh + 1) * HD)
        head = 2 * pair + hh
        gate = gatet[pl.ds(head, 1), :]
        d_mix = dmix_t[rows, :].astype(F32)
        local = local_t[rows, :]
        mem = mem_t[rows, :]
        inv_local = inv_sums[0, hh : hh + 1, :]
        inv_mem = inv_sums[0, 2 + hh : 3 + hh, 0:SEG]
        d_local = (d_mix * (gate * inv_local)).astype(BF)
        d_mem = (d_mix[:, SEG:] * ((1.0 - gate[:, SEG:]) * inv_mem)).astype(BF)
        dot_local = jnp.sum(d_local.astype(F32) * local, axis=0, keepdims=True)
        dot_mem = jnp.sum(d_mem.astype(F32) * mem, axis=0, keepdims=True)
        plain_local = jnp.sum(d_mix * local, axis=0, keepdims=True)
        plain_mem = jnp.sum(d_mix[:, SEG:] * mem, axis=0, keepdims=True)
        d_gate = gate * (1.0 - gate) * (
            plain_local - jnp.concatenate([jnp.zeros((1, SEG), F32), plain_mem], axis=1)
        )
        slot = lax.broadcasted_iota(jnp.int32, (16, SEQ), 0) == head
        dqkvt[3 * D : 3 * D + 16, :] = jnp.where(slot, d_gate.astype(BF), dqkvt[3 * D : 3 * D + 16, :])
        d_key = [jnp.zeros((HD, SEG), F32), jnp.zeros((HD, SEG), F32)]
        d_value = [jnp.zeros((HD, SEG), F32), jnp.zeros((HD, SEG), F32)]
        d_query = [None] * 4
        base = 0
        for seg in range(3):
            for ib in range(2):
                side = 1 if seg == 1 else 0
                key_first = side * SEG
                key_count = SEG if seg == 2 else 256 * (ib + 1)
                column = (0 if seg == 0 else SEG) + 256 * ib
                place = column // 256
                expo = probs[0, hh, base : base + key_count, :]
                base += key_count
                if seg == 2:
                    up = d_mem[:, 256 * ib : 256 * ib + 256]
                    dot = dot_mem[:, 256 * ib : 256 * ib + 256]
                else:
                    up = d_local[:, column : column + 256]
                    dot = dot_local[:, column : column + 256]
                d_prob = mm(vtok[key_first : key_first + key_count, :], head_half(up, hh))
                d_score = (expo.astype(F32) * (d_prob - dot)).astype(BF)
                term = mm(kt[rows, key_first : key_first + key_count], d_score)
                d_query[place] = term if d_query[place] is None else d_query[place] + term
                key_term = mm_nt(qt[rows, column : column + 256], d_score)
                value_term = mm_nt(up, expo)
                if key_count < SEG:
                    blank = jnp.zeros((HD, SEG - key_count), F32)
                    key_term = jnp.concatenate([key_term, blank], axis=1)
                    value_term = jnp.concatenate([value_term, blank], axis=1)
                d_key[side] = d_key[side] + key_term
                d_value[side] = d_value[side] + value_term
        for place in range(4):
            start = pl.multiple_of(pair * 128 + hh * HD, HD)
            dqkvt[pl.ds(start, HD), 256 * place : 256 * place + 256] = (
                d_query[place] * 0.125
            ).astype(BF)
        for side in range(2):
            columns = slice(side * SEG, (side + 1) * SEG)
            start = pl.multiple_of(D + pair * 128 + hh * HD, HD)
            dqkvt[pl.ds(start, HD), columns] = d_key[side].astype(BF)
            start = pl.multiple_of(2 * D + pair * 128 + hh * HD, HD)
            dqkvt[pl.ds(start, HD), columns] = d_value[side].astype(BF)

    @pl.when(pair == 3)
    def _():
        g_one = gains[0:1, :]
        total = jnp.zeros((1, D), F32)

        @pl.loop(0, 4)
        def _(block):
            lanes = pl.ds(pl.multiple_of(block * 384, 128), 384)
            g_ext[:, lanes] = mm_nt(hidt[...], dqkvt[lanes, :]).astype(BF)

        def row_block(block, total):
            rows = pl.ds(pl.multiple_of(block * 256, 256), 256)
            d_hid = mm(w[...], dqkvt[:, rows]).T
            xf = x[rows, :].astype(F32)
            factor = lax.rsqrt(jnp.mean(xf * xf, axis=1, keepdims=True) + 1e-06)
            total = total + jnp.sum(d_hid * xf * factor, axis=0, keepdims=True)
            scaled = d_hid * g_one
            inner = jnp.mean(scaled * xf, axis=1, keepdims=True)
            grad_in[rows, :] = (
                d_resid[rows, :] + factor * scaled - xf * (factor * factor * factor * inner)
            ).astype(BF)
            return total

        total = lax.fori_loop(0, 4, row_block, total)
        last = mm_nt(hidt[...], dqkvt[3 * D :, :]) + ext_from_rows(total, dgain_two[...])
        g_ext[:, 3 * D :] = last.astype(BF)
        for piece in range(PIECES):
            d = owner(piece)
            pltpu.make_async_copy(
                g_ext.at[pl.ds(pl.multiple_of(d * ROWS, ROWS), ROWS), :],
                grads[piece // per].at[piece % per],
                out_sem,
            ).start()
        pltpu.make_async_copy(g_ext, w, out_sem).wait()


def attention_backward(
    x, d_resid, dgain, gains, gatet, w, hidt, probs, local_t, mem_t, inv_sums, dmix_t, qkvt, vtok, owner, split
):
    count_o = 2 if split else 1
    const2 = lambda p: (0, 0)

    def body(*refs):
        attention_backward_kernel(owner, split, *refs)

    return pl.pallas_call(
        body,
        grid=(4,),
        in_specs=[
            pl.BlockSpec((SEQ, D), const2),
            pl.BlockSpec((SEQ, D), const2),
            pl.BlockSpec((1, D), const2),
            pl.BlockSpec((2, D), const2),
            pl.BlockSpec((H, SEQ), const2),
            pl.BlockSpec((D, EXT), const2),
            pl.BlockSpec((D, SEQ), const2),
            pl.BlockSpec((1, 2, PROB_ROWS, 256), lambda p: (p, 0, 0, 0)),
            pl.BlockSpec((128, SEQ), lambda p: (p, 0)),
            pl.BlockSpec((128, SEG), lambda p: (p, 0)),
            pl.BlockSpec((1, 4, SEQ), lambda p: (p, 0, 0)),
            pl.BlockSpec((128, SEQ), lambda p: (p, 0)),
            pl.BlockSpec((128, SEQ), lambda p: (p, 0)),
            pl.BlockSpec((128, SEQ), lambda p: (4 + p, 0)),
            pl.BlockSpec((128, SEQ), lambda p: (8 + p, 0)),
            pl.BlockSpec((SEQ, 128), lambda p: (0, p)),
        ],
        out_specs=[pl.BlockSpec((SEQ, D), const2)] + [ANY] * count_o,
        out_shape=[jax.ShapeDtypeStruct((SEQ, D), BF)]
        + [jax.ShapeDtypeStruct((PIECES // count_o, ROWS, EXT), BF)] * count_o,
        scratch_shapes=[
            pltpu.VMEM((EXT, SEQ), BF),
            pltpu.VMEM((D, EXT), BF),
            pltpu.SemaphoreType.DMA,
        ],
        compiler_params=pltpu.CompilerParams(vmem_limit_bytes=VLIMIT),
        cost_estimate=pl.CostEstimate(
            flops=15_000_000_000, bytes_accessed=30_000_000, transcendentals=0
        ),
        name="attention_backward",
    )(x, d_resid, dgain, gains, gatet, w, hidt, probs, local_t, mem_t, inv_sums, dmix_t, qkvt, qkvt, qkvt, vtok)


def ext_rows(qkv, gate, gains):
    count = qkv.shape[0]
    blank = jnp.zeros((count, 128 - GCOL - gains.shape[1]), BF)
    return jnp.concatenate([qkv, gate, gains, blank], axis=1)


def local(
    n, inputs, cotangent, doc_ids, slot_ids, qkv_flat, out_flat, norm_gains, gate_flat, up_flat, down_flat
):
    split = n == PIECES
    doc_row = doc_ids.reshape(1, SEQ)
    doc_col = doc_ids.reshape(SEQ, 1)
    slots = slot_ids.reshape(SEG, K).T
    half = 7 * 128
    if split:
        gains_rows = jnp.broadcast_to(norm_gains.reshape(1, GLEN), (ROWS, GLEN))
        shard_a = ext_rows(qkv_flat.reshape(ROWS, 3 * D), gate_flat.reshape(ROWS, H), gains_rows)
        a_z = gather_z(shard_a)
        parts_a = gather_rest(a_z[:, :, :half], 1, 2)
        parts_b = gather_rest(a_z[:, :, half:], 2, 1)
        f_up = jnp.concatenate(
            [
                out_flat.reshape(1, ROWS, D),
                up_flat.reshape(ROWS, 4, D).transpose(1, 0, 2),
            ]
        )
        f_all = jnp.concatenate([f_up.reshape(5 * ROWS, D), down_flat.reshape(64, D)])
        f_z = gather_z(f_all)
        parts_u = gather_rest(f_z[:, : 5 * ROWS].reshape(4, 5, ROWS, D), 1, 2)
        parts_d = gather_rest(f_z[:, 5 * ROWS :], 2, 1)
    else:
        whole = [
            lax.all_gather(v, AXES, axis=0, tiled=True)
            for v in (qkv_flat, out_flat, norm_gains, gate_flat, up_flat, down_flat)
        ]
        gains_rows = jnp.repeat(whole[2].reshape(PIECES, GLEN), ROWS, axis=0)
        ext = ext_rows(whole[0].reshape(D, 3 * D), whole[3].reshape(D, H), gains_rows)
        ext = ext.reshape(PIECES, ROWS, EXT)
        parts_a = (ext[:, :, :half],)
        parts_b = (ext[:, :, half:],)
        f_up = jnp.concatenate(
            [
                whole[1].reshape(PIECES, 1, ROWS, D),
                whole[4].reshape(PIECES, ROWS, 4, D).transpose(0, 2, 1, 3),
            ],
            axis=1,
        )
        parts_u = (f_up,)
        parts_d = (whole[5].reshape(PIECES, 64, D),)
    owner_x = owner_fn(split, True)
    owner_y = owner_fn(split, False)

    bias = pl.pallas_call(
        bias_kernel,
        out_shape=jax.ShapeDtypeStruct((3, SEG, SEG), F32),
        name="masks",
    )(doc_row, doc_col, slots)

    (
        qkvt,
        vtok,
        hidt,
        w_ext,
        gatet,
        gains,
        probs,
        local_t,
        mem_t,
        inv_sums,
        mixed_t,
        mixed,
    ) = attention_forward(inputs, bias, parts_a, parts_b, (owner_x, owner_y))
    outs = ffn(
        inputs, cotangent, mixed, mixed_t, gains, parts_u, parts_d, owner_x, owner_y, split
    )
    layer_out, d_resid, dmix_t, dgain_two = outs[:4]
    if split:
        up_keep, up_send, dn_keep, dn_send = outs[4:]
        up_sum = reduce_bit(reduce_bit(reduce_core(up_keep, up_send), 2), 1)
        dn_sum = reduce_bit(reduce_bit(reduce_core(dn_keep, dn_send), 1), 2)
        f_sum = reduce_z(
            jnp.concatenate([up_sum.reshape(4, 5 * ROWS, D), dn_sum], axis=1)
        )
        grad_out = f_sum[:ROWS].reshape(-1)
        grad_up = f_sum[ROWS : 5 * ROWS].reshape(4, ROWS, D).transpose(1, 0, 2).reshape(-1)
        grad_down = f_sum[5 * ROWS :].reshape(-1)
    grad_outs = attention_backward(
        inputs,
        d_resid,
        dgain_two,
        gains,
        gatet,
        w_ext,
        hidt,
        probs,
        local_t,
        mem_t,
        inv_sums,
        dmix_t,
        qkvt,
        vtok,
        owner_x,
        split,
    )
    grad_input = grad_outs[0]
    if split:
        total = reduce_core(grad_outs[1], grad_outs[2])
        ext_sum = reduce_z(reduce_bit(reduce_bit(total, 2), 1))
        grad_qkv = ext_sum[:, : 3 * D].reshape(-1)
        grad_gate = ext_sum[:, 3 * D : 3 * D + H].reshape(-1)
        grad_gains = ext_sum[0, 3 * D + GCOL : 3 * D + GCOL + GLEN]
    else:

        def scatter(v):
            return lax.psum_scatter(
                v.astype(F32).reshape(-1), AXES, scatter_dimension=0, tiled=True
            )

        grad_out = scatter(outs[4][:, 0])
        grad_up = scatter(outs[4][:, 1:].transpose(0, 2, 1, 3))
        grad_down = scatter(outs[5])
        ext = grad_outs[1]
        grad_qkv = scatter(ext[:, :, : 3 * D])
        grad_gate = scatter(ext[:, :, 3 * D : 3 * D + H])
        grad_gains = scatter(ext[:, 0, 3 * D + GCOL : 3 * D + GCOL + GLEN])
    return (layer_out, grad_input, grad_qkv, grad_out, grad_gains, grad_gate, grad_up, grad_down)


def solution(mesh):
    n = mesh.shape["dp"] * mesh.shape["fsdp"]

    def per_device(*args):
        return local(n, *args)

    rows = P(AXES, None)
    flat = P(AXES)
    return jax.shard_map(
        per_device,
        mesh=mesh,
        in_specs=(rows, rows, rows, P(AXES, None, None), flat, flat, flat, flat, flat, flat),
        out_specs=(rows, rows, flat, flat, flat, flat, flat, flat),
        check_vma=False,
    )
```

time: 799 us -> 207 us (0.26); the launches traced: 788 us -> 207 us
  local copies, waits for them, and re-layouts: 240 us -> 11.1 us
  blocking collectives: 159 us -> 0 us
  waiting for transfers between devices: 166 us -> 54.8 us
  matrix products: 106 us -> 0 us
  other arithmetic: 101 us -> 6.42 us
  Pallas kernels: 0 us -> 88 us
  starting transfers between devices: 0.15 us -> 45.3 us
  between operations: 15 us -> 1.04 us
    unnamed x5 -> x0, waiting for transfers between devices: 166 us -> none
    dot_general x29 -> x0, matrix products: 106 us -> none  [the longest x4 12.1 us: block_scores(): jnp.einsum('ihd,jhd->hij', query_h, key_h, preferred_element_type=jnp.flo...]
    pallas_call x0 -> x4, Pallas kernels: none -> 88 us  [the longest x1 30 us: ffn(): pl.pallas_call(body, grid=(8,), in_specs=[pl.BlockSpec((SEQ, D), const2),...]
    unnamed x2 -> x0, blocking collectives: 81 us -> none
    all_gather x2 -> x0, blocking collectives: 78.4 us -> none  [the longest x1 40 us: local(): lax.all_gather(gate_flat, ('dp', 'fsdp'), axis=0, tiled=True)]
    gather x7 -> x0, local copies, waits for them, and re-layouts: 56.4 us -> none  [pick_rows(): source_rows[picked]]
    ppermute x0 -> x33, waiting for transfers between devices: none -> 54.8 us  [the longest x14 42.8 us: perm_bit(): return lax.ppermute(v, 'dp', [(i, i ^ bit) for i in range(16)])]
    ppermute x0 -> x33, starting transfers between devices: none -> 45.3 us  [the longest x12 28 us: perm_z(): return lax.ppermute(v, 'dp', [(i, (i + 4 * shift) % 16) for i in range(16)])]
  transfers between devices with their start and end apart: 4 -> 33, of which waited for: 1 -> 14; matrix products, arithmetic and copies ran while one was open for 28% -> 6% of each run, Pallas kernels for 0% -> 14%
where the time goes in v1:
time: 207 us
  Pallas kernels  88 us (43%)
  waiting for transfers between devices  54.8 us (26%)
  starting transfers between devices  45.3 us (22%)
  local copies, waits for them, and re-layouts  11.1 us (5%)
  other arithmetic  6.42 us (3%)
    ppermute x14, waiting for transfers between devices, perm_bit(): return lax.ppermute(v, 'dp', [(i, i ^ bit) for i in range(16)])  42.8 us
    pallas_call x1, Pallas kernels, ffn(): pl.pallas_call(body, grid=(8,), in_specs=[pl.BlockSpec((SEQ, D), const2),...  30 us
    pallas_call x1, Pallas kernels, attention_backward(): pl.pallas_call(body, grid=(4,), in_specs=[pl.BlockSpec((SEQ, D), const2),...  28.8 us
    ppermute x12, starting transfers between devices, perm_z(): return lax.ppermute(v, 'dp', [(i, (i + 4 * shift) % 16) for i in range(16)])  28 us
    pallas_call x1, Pallas kernels, attention_forward(): pl.pallas_call(body, grid=(4,), in_specs=[pl.BlockSpec((SEQ, D), const2),...  25.7 us
    ppermute x14, starting transfers between devices, perm_bit(): return lax.ppermute(v, 'dp', [(i, i ^ bit) for i in range(16)])  15.4 us
    ppermute x12, waiting for transfers between devices, perm_z(): return lax.ppermute(v, 'dp', [(i, (i + 4 * shift) % 16) for i in range(16)])  10.1 us
  transfers between devices with their start and end apart: 33, of which 14 were waited for; matrix products, arithmetic and copies ran while one was open for 6% of the time, Pallas kernels for 14%

profile of v1, /device:TPU:0, one launch (start us, length us, event | category | flops | bytes accessed | tf_op | source)
XLA Modules:
  0.0 206.7 jit_solution(16442600004718742267)
XLA Ops:
  3.3 4.1 %collective-permute-start.10 = (bf16[144,512]{1,0:T(8,128)(2,1)S(1)}, bf16[144,512]{1,0:T(8,128)(2,1)S(1)}, u32[]{:S(2)}, u32[]{:S(2)}) collective-permute-start(bf16[144,512]{1,0:T(8,128)(2,1)S(1)} %get-tuple-element.65), channel_id=1, source_target_pairs={{0,16},{2,18},{4,20},{6,22},{8,24},{10,26},{12,28},{14,30},{16,0},... | collective-permute-start | bytes 442376 | tf_op jit(solution)/shard_map/ppermute | solution.py:43
  13.4 2.1 %collective-permute-start.1 = (bf16[16,1664]{1,0:T(8,128)(2,1)S(1)}, bf16[16,1664]{1,0:T(8,128)(2,1)S(1)}, u32[]{:S(2)}, u32[]{:S(2)}) collective-permute-start(bf16[16,1664]{1,0:T(8,128)(2,1)S(1)} %concatenate.40), channel_id=1, source_target_pairs={{0,16},{2,18},{4,20},{6,22},{8,24},{10,26},{12,28},{14,30},{16,0},... | collective-permute-start | bytes 159752 | tf_op jit(solution)/shard_map/ppermute | solution.py:43
  16.0 5.3 %collective-permute-start = (bf16[16,1664]{1,0:T(8,128)(2,1)S(1)}, bf16[16,1664]{1,0:T(8,128)(2,1)S(1)}, u32[]{:S(2)}, u32[]{:S(2)}) collective-permute-start(bf16[16,1664]{1,0:T(8,128)(2,1)S(1)} %concatenate.40), channel_id=1, source_target_pairs={{0,24},{2,26},{4,28},{6,30},{8,0},{10,2},{12,4},{14,6},{16,8},{18,... | collective-permute-start | bytes 159752 | tf_op jit(solution)/shard_map/ppermute | solution.py:43
  23.0 1.7 collective-permute-done.1
  24.8 1.6 collective-permute-start.6
  28.5 3.4 %collective-permute-done.12 = bf16[4,5,16,512]{3,2,1,0:T(8,128)(2,1)S(1)} collective-permute-done((bf16[4,5,16,512]{3,2,1,0:T(8,128)(2,1)S(1)}, bf16[4,5,16,512]{3,2,1,0:T(8,128)(2,1)S(1)}, u32[]{:S(2)}, u32[]{:S(2)}) %collective-permute-start.12) | collective-permute-done | bytes 327712 | tf_op jit(solution)/shard_map/ppermute | solution.py:47
  32.0 1.6 collective-permute-start.13
  37.4 16.4 %collective-permute-done.4 = bf16[8,16,896]{2,1,0:T(8,128)(2,1)S(1)} collective-permute-done((bf16[8,16,896]{2,1,0:T(8,128)(2,1)S(1)}, bf16[8,16,896]{2,1,0:T(8,128)(2,1)S(1)}, u32[]{:S(2)}, u32[]{:S(2)}) %collective-permute-start.4) | collective-permute-done | bytes 229408 | tf_op jit(solution)/shard_map/ppermute | solution.py:47
  57.3 3.6 %masks.1.refs_1_ = f32[3,512,512]{2,1,0:T(8,128)} custom-call(s32[1,1024]{1,0:T(1,128)} %doc_row.1, s32[1024,1]{1,0:T(8,128)} %copy.20.doc_col, s32[4,512]{1,0:T(4,128)} %bitcast.87), custom_call_target="tpu_custom_call" | custom-call | tf_op jit(solution)/shard_map/masks/pallas_call | solution.py:716
  62.5 25.7 %attention_forward.1 = (bf16[1536,1024]{1,0:T(8,128)(2,1)}, bf16[1024,512]{1,0:T(8,128)(2,1)}, bf16[512,1024]{1,0:T(8,128)(2,1)}, bf16[512,1664]{1,0:T(8,128)(2,...) custom-call(bf16[1024,512]{1,0:T(8,128)(2,1)} %refs_0_.5, ...), custom_call_target="tpu_custom_call" | custom-call | flops 12000000000 | bytes 30000000 | tf_op jit(solution)/shard_map/attention_forward/pallas_call | solution.py:271
  88.2 30.0 %feed_forward.1 = (bf16[1024,512]{1,0:T(8,128)(2,1)}, f32[1024,512]{1,0:T(8,128)}, bf16[512,1024]{1,0:T(8,128)(2,1)}, f32[1,512]{1,0:T(1,128)}, bf16[16,5,16,512...) custom-call(bf16[1024,512]{1,0:T(8,128)(2,1)} %refs_0_.5, ...), custom_call_target="tpu_custom_call" | custom-call | flops 15000000512 | bytes 20000000 | tf_op jit(solution)/shard_map/feed_forward/pallas_call | solution.py:454
  118.2 28.8 %attention_backward.1 = (bf16[1024,512]{1,0:T(8,128)(2,1)}, bf16[16,16,1664]{2,1,0:T(8,128)(2,1)}, bf16[16,16,1664]{2,1,0:T(8,128)(2,1)}) custom-call(bf16[1024,512]{1,0:T(8,128)(2,1)} %refs_0_.5, f32[1024,512]{1,0:T(8,128)} %get-tuple-element.35.refs_1_, f32[1,512]{1,0:T(1,128)} %get-tuple-element.36.refs_2_, f32[2,512]{1,0:T(2,128)} %get-tuple-element.33.refs_4_.refs_3_, ...), custom_call_target="tpu_custom_call" | custom-call | flops 15000000512 | bytes 30000000 | tf_op jit(solution)/shard_map/attention_backward/pallas_call | solution.py:627
  147.8 1.8 collective-permute-done.18
  153.2 9.9 %collective-permute-done.19 = bf16[8,16,1664]{2,1,0:T(8,128)(2,1)S(1)} collective-permute-done((bf16[8,16,1664]{2,1,0:T(8,128)(2,1)S(1)}, bf16[8,16,1664]{2,1,0:T(8,128)(2,1)S(1)}, u32[]{:S(2)}, u32[]{:S(2)}) %collective-permute-start.19) | collective-permute-done | bytes 426016 | tf_op jit(solution)/shard_map/ppermute | solution.py:47
  165.6 5.0 %collective-permute-done.20 = bf16[4,16,1664]{2,1,0:T(8,128)(2,1)S(1)} collective-permute-done((bf16[4,16,1664]{2,1,0:T(8,128)(2,1)S(1)}, bf16[4,16,1664]{2,1,0:T(8,128)(2,1)S(1)}, u32[]{:S(2)}, u32[]{:S(2)}) %collective-permute-start.20) | collective-permute-done | bytes 213024 | tf_op jit(solution)/shard_map/ppermute | solution.py:47
  170.6 3.0 %collective-permute-start.21 = (bf16[16,1664]{1,0:T(8,128)(2,1)S(1)}, bf16[16,1664]{1,0:T(8,128)(2,1)S(1)}, u32[]{:S(2)}, u32[]{:S(2)}) collective-permute-start(bf16[16,1664]{1,0:T(8,128)(2,1)S(1)} %get-tuple-element.61), channel_id=1, source_target_pairs={{0,8},{2,10},{4,12},{6,14},{8,16},{10,18},{12,20},{14,22},{16,24},... | collective-permute-start | bytes 159752 | tf_op jit(solution)/shard_map/ppermute | solution.py:43
  173.7 2.6 %collective-permute-start.23 = (bf16[16,1664]{1,0:T(8,128)(2,1)S(1)}, bf16[16,1664]{1,0:T(8,128)(2,1)S(1)}, u32[]{:S(2)}, u32[]{:S(2)}) collective-permute-start(bf16[16,1664]{1,0:T(8,128)(2,1)S(1)} %get-tuple-element.62), channel_id=1, source_target_pairs={{0,24},{2,26},{4,28},{6,30},{8,0},{10,2},{12,4},{14,6},{16,8},{18,... | collective-permute-start | bytes 159752 | tf_op jit(solution)/shard_map/ppermute | solution.py:43
  178.6 3.0 %collective-permute-done.25 = bf16[8,5,16,512]{3,2,1,0:T(8,128)(2,1)S(1)} collective-permute-done((bf16[8,5,16,512]{3,2,1,0:T(8,128)(2,1)S(1)}, bf16[8,5,16,512]{3,2,1,0:T(8,128)(2,1)S(1)}, u32[]{:S(2)}, u32[]{:S(2)}) %collective-permute-start.25) | collective-permute-done | bytes 655392 | tf_op jit(solution)/shard_map/ppermute | solution.py:47
  186.1 3.0 %collective-permute-done.26 = bf16[4,5,16,512]{3,2,1,0:T(8,128)(2,1)S(1)} collective-permute-done((bf16[4,5,16,512]{3,2,1,0:T(8,128)(2,1)S(1)}, bf16[4,5,16,512]{3,2,1,0:T(8,128)(2,1)S(1)}, u32[]{:S(2)}, u32[]{:S(2)}) %collective-permute-start.26) | collective-permute-done | bytes 327712 | tf_op jit(solution)/shard_map/ppermute | solution.py:47
  189.3 3.3 %collective-permute-start.30 = (bf16[144,512]{1,0:T(8,128)(2,1)S(1)}, bf16[144,512]{1,0:T(8,128)(2,1)S(1)}, u32[]{:S(2)}, u32[]{:S(2)}) collective-permute-start(bf16[144,512]{1,0:T(8,128)(2,1)S(1)} %get-tuple-element.56), channel_id=1, source_target_pairs={{0,8},{2,10},{4,12},{6,14},{8,16},{10,18},{12,20},{14,22},{16,24},... | collective-permute-start | bytes 442376 | tf_op jit(solution)/shard_map/ppermute | solution.py:43
  192.6 2.9 %collective-permute-start.32 = (bf16[144,512]{1,0:T(8,128)(2,1)S(1)}, bf16[144,512]{1,0:T(8,128)(2,1)S(1)}, u32[]{:S(2)}, u32[]{:S(2)}) collective-permute-start(bf16[144,512]{1,0:T(8,128)(2,1)S(1)} %get-tuple-element.57), channel_id=1, source_target_pairs={{0,24},{2,26},{4,28},{6,30},{8,0},{10,2},{12,4},{14,6},{16,8},{18,... | collective-permute-start | bytes 442376 | tf_op jit(solution)/shard_map/ppermute | solution.py:43
  196.6 2.1 %collective-permute-done.30 = bf16[144,512]{1,0:T(8,128)(2,1)S(1)} collective-permute-done((bf16[144,512]{1,0:T(8,128)(2,1)S(1)}, bf16[144,512]{1,0:T(8,128)(2,1)S(1)}, u32[]{:S(2)}, u32[]{:S(2)}) %collective-permute-start.30) | collective-permute-done | bytes 147488 | tf_op jit(solution)/shard_map/ppermute | solution.py:43
  198.7 2.1 %collective-permute-done.32 = bf16[144,512]{1,0:T(8,128)(2,1)S(1)} collective-permute-done((bf16[144,512]{1,0:T(8,128)(2,1)S(1)}, bf16[144,512]{1,0:T(8,128)(2,1)S(1)}, u32[]{:S(2)}, u32[]{:S(2)}) %collective-permute-start.32) | collective-permute-done | bytes 147488 | tf_op jit(solution)/shard_map/ppermute | solution.py:43
  200.8 3.7 %collective-permute-done.31 = bf16[144,512]{1,0:T(8,128)(2,1)S(1)} collective-permute-done((bf16[144,512]{1,0:T(8,128)(2,1)S(1)}, bf16[144,512]{1,0:T(8,128)(2,1)S(1)}, u32[]{:S(2)}, u32[]{:S(2)}) %collective-permute-start.31) | collective-permute-done | bytes 147488 | tf_op jit(solution)/shard_map/ppermute | solution.py:43
  (117 shorter events, 38.9 us)
Async XLA Ops:
  3.3 12.8 %collective-permute-start.10 = (bf16[144,512]{1,0:T(8,128)(2,1)S(1)}, bf16[144,512]{1,0:T(8,128)(2,1)S(1)}, u32[]{:S(2)}, u32[]{:S(2)}) collective-permute-start(bf16[144,512]{1,0:T(8,128)(2,1)S(1)} %get-tuple-element.65), channel_id=1, source_target_pairs={{0,16},{2,18},{4,20},{6,22},{8,24},{10,26},{12,28},{14,30},{16,0},... | collective-permute-start | bytes 442376 | tf_op jit(solution)/shard_map/ppermute | solution.py:43
  7.4 13.9 %collective-permute-start.9 = (bf16[144,512]{1,0:T(8,128)(2,1)S(1)}, bf16[144,512]{1,0:T(8,128)(2,1)S(1)}, u32[]{:S(2)}, u32[]{:S(2)}) collective-permute-start(bf16[144,512]{1,0:T(8,128)(2,1)S(1)} %get-tuple-element.65), channel_id=1, source_target_pairs={{0,24},{2,26},{4,28},{6,30},{8,0},{10,2},{12,4},{14,6},{16,8},{18,... | collective-permute-start | bytes 442376 | tf_op jit(solution)/shard_map/ppermute | solution.py:43
  8.7 12.6 %collective-permute-start.11 = (bf16[144,512]{1,0:T(8,128)(2,1)S(1)}, bf16[144,512]{1,0:T(8,128)(2,1)S(1)}, u32[]{:S(2)}, u32[]{:S(2)}) collective-permute-start(bf16[144,512]{1,0:T(8,128)(2,1)S(1)} %get-tuple-element.65), channel_id=1, source_target_pairs={{0,8},{2,10},{4,12},{6,14},{8,16},{10,18},{12,20},{14,22},{16,24},... | collective-permute-start | bytes 442376 | tf_op jit(solution)/shard_map/ppermute | solution.py:43
  11.8 11.2 %collective-permute-start.2 = (bf16[16,1664]{1,0:T(8,128)(2,1)S(1)}, bf16[16,1664]{1,0:T(8,128)(2,1)S(1)}, u32[]{:S(2)}, u32[]{:S(2)}) collective-permute-start(bf16[16,1664]{1,0:T(8,128)(2,1)S(1)} %concatenate.40), channel_id=1, source_target_pairs={{0,8},{2,10},{4,12},{6,14},{8,16},{10,18},{12,20},{14,22},{16,24},... | collective-permute-start | bytes 159752 | tf_op jit(solution)/shard_map/ppermute | solution.py:43
  13.4 11.3 %collective-permute-start.1 = (bf16[16,1664]{1,0:T(8,128)(2,1)S(1)}, bf16[16,1664]{1,0:T(8,128)(2,1)S(1)}, u32[]{:S(2)}, u32[]{:S(2)}) collective-permute-start(bf16[16,1664]{1,0:T(8,128)(2,1)S(1)} %concatenate.40), channel_id=1, source_target_pairs={{0,16},{2,18},{4,20},{6,22},{8,24},{10,26},{12,28},{14,30},{16,0},... | collective-permute-start | bytes 159752 | tf_op jit(solution)/shard_map/ppermute | solution.py:43
  16.0 8.7 %collective-permute-start = (bf16[16,1664]{1,0:T(8,128)(2,1)S(1)}, bf16[16,1664]{1,0:T(8,128)(2,1)S(1)}, u32[]{:S(2)}, u32[]{:S(2)}) collective-permute-start(bf16[16,1664]{1,0:T(8,128)(2,1)S(1)} %concatenate.40), channel_id=1, source_target_pairs={{0,24},{2,26},{4,28},{6,30},{8,0},{10,2},{12,4},{14,6},{16,8},{18,... | collective-permute-start | bytes 159752 | tf_op jit(solution)/shard_map/ppermute | solution.py:43
  21.4 10.5 %collective-permute-start.12 = (bf16[4,5,16,512]{3,2,1,0:T(8,128)(2,1)S(1)}, bf16[4,5,16,512]{3,2,1,0:T(8,128)(2,1)S(1)}, u32[]{:S(2)}, u32[]{:S(2)}) collective-permute-start(bf16[4,5,16,512]{3,2,1,0:T(8,128)(2,1)S(1)} %bitcast.62), channel_id=1, source_target_pairs={{0,2},{2,0},{4,6},{6,4},{8,10},{10,8},{12,14},{14,12},{16,18},{18,... | collective-permute-start | bytes 983048 | tf_op jit(solution)/shard_map/ppermute | solution.py:47
  24.8 10.0 %collective-permute-start.6 = (bf16[4,16,768]{2,1,0:T(8,128)(2,1)S(1)}, bf16[4,16,768]{2,1,0:T(8,128)(2,1)S(1)}, u32[]{:S(2)}, u32[]{:S(2)}) collective-permute-start(bf16[4,16,768]{2,1,0:T(8,128)(2,1)S(1)} %pad_maximum_fusion.14), channel_id=1, source_target_pairs={{0,4},{2,6},{4,0},{6,2},{8,12},{10,14},{12,8},{14,10},{16,20},{18,... | collective-permute-start | bytes 294920 | tf_op jit(solution)/shard_map/ppermute | solution.py:47
  27.9 9.3 %collective-permute-start.15 = (bf16[4,64,512]{2,1,0:T(8,128)(2,1)S(1)}, bf16[4,64,512]{2,1,0:T(8,128)(2,1)S(1)}, u32[]{:S(2)}, u32[]{:S(2)}) collective-permute-start(bf16[4,64,512]{2,1,0:T(8,128)(2,1)S(1)} %pad_maximum_fusion.8), channel_id=1, source_target_pairs={{0,4},{2,6},{4,0},{6,2},{8,12},{10,14},{12,8},{14,10},{16,20},{18,... | collective-permute-start | bytes 786440 | tf_op jit(solution)/shard_map/ppermute | solution.py:47
  32.0 24.0 %collective-permute-start.13 = (bf16[8,5,16,512]{3,2,1,0:T(8,128)(2,1)S(1)}, bf16[8,5,16,512]{3,2,1,0:T(8,128)(2,1)S(1)}, u32[]{:S(2)}, u32[]{:S(2)}) collective-permute-start(bf16[8,5,16,512]{3,2,1,0:T(8,128)(2,1)S(1)} %pad_maximum_fusion.3), channel_id=1, source_target_pairs={{0,4},{2,6},{4,0},{6,2},{8,12},{10,14},{12,8},{14,10},{16,20},{18,... | collective-permute-start | bytes 1966088 | tf_op jit(solution)/shard_map/ppermute | solution.py:47
  33.6 20.2 %collective-permute-start.4 = (bf16[8,16,896]{2,1,0:T(8,128)(2,1)S(1)}, bf16[8,16,896]{2,1,0:T(8,128)(2,1)S(1)}, u32[]{:S(2)}, u32[]{:S(2)}) collective-permute-start(bf16[8,16,896]{2,1,0:T(8,128)(2,1)S(1)} %pad_maximum_fusion.9), channel_id=1, source_target_pairs={{0,4},{2,6},{4,0},{6,2},{8,12},{10,14},{12,8},{14,10},{16,20},{18,... | collective-permute-start | bytes 688136 | tf_op jit(solution)/shard_map/ppermute | solution.py:47
  34.8 19.8 %collective-permute-start.7 = (bf16[8,16,768]{2,1,0:T(8,128)(2,1)S(1)}, bf16[8,16,768]{2,1,0:T(8,128)(2,1)S(1)}, u32[]{:S(2)}, u32[]{:S(2)}) collective-permute-start(bf16[8,16,768]{2,1,0:T(8,128)(2,1)S(1)} %pad_maximum_fusion.11), channel_id=1, source_target_pairs={{0,2},{2,0},{4,6},{6,4},{8,10},{10,8},{12,14},{14,12},{16,18},{18,... | collective-permute-start | bytes 589832 | tf_op jit(solution)/shard_map/ppermute | solution.py:47
  37.3 23.6 %collective-permute-start.16 = (bf16[8,64,512]{2,1,0:T(8,128)(2,1)S(1)}, bf16[8,64,512]{2,1,0:T(8,128)(2,1)}, u32[]{:S(2)}, u32[]{:S(2)}) collective-permute-start(bf16[8,64,512]{2,1,0:T(8,128)(2,1)S(1)} %pad_maximum_fusion.5), channel_id=1, source_target_pairs={{0,2},{2,0},{4,6},{6,4},{8,10},{10,8},{12,14},{14,12},{16,18},{18,... | collective-permute-start | bytes 1572872 | tf_op jit(solution)/shard_map/ppermute | solution.py:47
  56.1 32.2 %collective-permute-start.14 = (bf16[16,5,16,512]{3,2,1,0:T(8,128)(2,1)S(1)}, bf16[16,5,16,512]{3,2,1,0:T(8,128)(2,1)}, u32[]{:S(2)}, u32[]{:S(2)}) collective-permute-start(bf16[16,5,16,512]{3,2,1,0:T(8,128)(2,1)S(1)} %pad_maximum_fusion.1.refs_5_), channel_id=1, source_target_pairs={{0,1},{1,0},{2,3},{3,2},{4,5},{5,4},{6,7},{7,6},{8,9},{9,8},{10,11... | collective-permute-start | bytes 3932168 | tf_op jit(solution)/shard_map/ppermute | solution.py:51
  62.1 26.2 %collective-permute-start.17 = (bf16[16,64,512]{2,1,0:T(8,128)(2,1)S(1)}, bf16[16,64,512]{2,1,0:T(8,128)(2,1)}, u32[]{:S(2)}, u32[]{:S(2)}) collective-permute-start(bf16[16,64,512]{2,1,0:T(8,128)(2,1)S(1)} %pad_maximum_fusion.2.refs_7_), channel_id=1, source_target_pairs={{0,1},{1,0},{2,3},{3,2},{4,5},{5,4},{6,7},{7,6},{8,9},{9,8},{10,11... | collective-permute-start | bytes 3145736 | tf_op jit(solution)/shard_map/ppermute | solution.py:51
  147.6 16.3 %collective-permute-start.24 = (bf16[16,5,16,512]{3,2,1,0:T(8,128)(2,1)S(1)}, bf16[16,5,16,512]{3,2,1,0:T(8,128)(2,1)S(1)}, u32[]{:S(2)}, u32[]{:S(2)}) collective-permute-start(bf16[16,5,16,512]{3,2,1,0:T(8,128)(2,1)S(1)} %copy-done.5), channel_id=1, source_target_pairs={{0,1},{1,0},{2,3},{3,2},{4,5},{5,4},{6,7},{7,6},{8,9},{9,8},{10,11... | collective-permute-start | bytes 3932168 | tf_op jit(solution)/shard_map/ppermute | solution.py:51
  151.1 12.0 %collective-permute-start.19 = (bf16[8,16,1664]{2,1,0:T(8,128)(2,1)S(1)}, bf16[8,16,1664]{2,1,0:T(8,128)(2,1)S(1)}, u32[]{:S(2)}, u32[]{:S(2)}) collective-permute-start(bf16[8,16,1664]{2,1,0:T(8,128)(2,1)S(1)} %slice.205), channel_id=1, source_target_pairs={{0,4},{2,6},{4,0},{6,2},{8,12},{10,14},{12,8},{14,10},{16,20},{18,... | collective-permute-start | bytes 1277960 | tf_op jit(solution)/shard_map/ppermute | solution.py:47
  152.1 24.6 %collective-permute-start.28 = (bf16[8,64,512]{2,1,0:T(8,128)(2,1)S(1)}, bf16[8,64,512]{2,1,0:T(8,128)(2,1)S(1)}, u32[]{:S(2)}, u32[]{:S(2)}) collective-permute-start(bf16[8,64,512]{2,1,0:T(8,128)(2,1)S(1)} %slice.204), channel_id=1, source_target_pairs={{0,2},{2,0},{4,6},{6,4},{8,10},{10,8},{12,14},{14,12},{16,18},{18,... | collective-permute-start | bytes 1572872 | tf_op jit(solution)/shard_map/ppermute | solution.py:47
  164.5 17.1 %collective-permute-start.25 = (bf16[8,5,16,512]{3,2,1,0:T(8,128)(2,1)S(1)}, bf16[8,5,16,512]{3,2,1,0:T(8,128)(2,1)S(1)}, u32[]{:S(2)}, u32[]{:S(2)}) collective-permute-start(bf16[8,5,16,512]{3,2,1,0:T(8,128)(2,1)S(1)} %slice.203), channel_id=1, source_target_pairs={{0,4},{2,6},{4,0},{6,2},{8,12},{10,14},{12,8},{14,10},{16,20},{18,... | collective-permute-start | bytes 1966088 | tf_op jit(solution)/shard_map/ppermute | solution.py:47
  170.6 12.8 %collective-permute-start.21 = (bf16[16,1664]{1,0:T(8,128)(2,1)S(1)}, bf16[16,1664]{1,0:T(8,128)(2,1)S(1)}, u32[]{:S(2)}, u32[]{:S(2)}) collective-permute-start(bf16[16,1664]{1,0:T(8,128)(2,1)S(1)} %get-tuple-element.61), channel_id=1, source_target_pairs={{0,8},{2,10},{4,12},{6,14},{8,16},{10,18},{12,20},{14,22},{16,24},... | collective-permute-start | bytes 159752 | tf_op jit(solution)/shard_map/ppermute | solution.py:43
  173.7 9.8 %collective-permute-start.23 = (bf16[16,1664]{1,0:T(8,128)(2,1)S(1)}, bf16[16,1664]{1,0:T(8,128)(2,1)S(1)}, u32[]{:S(2)}, u32[]{:S(2)}) collective-permute-start(bf16[16,1664]{1,0:T(8,128)(2,1)S(1)} %get-tuple-element.62), channel_id=1, source_target_pairs={{0,24},{2,26},{4,28},{6,30},{8,0},{10,2},{12,4},{14,6},{16,8},{18,... | collective-permute-start | bytes 159752 | tf_op jit(solution)/shard_map/ppermute | solution.py:43
  177.7 8.3 %collective-permute-start.29 = (bf16[4,64,512]{2,1,0:T(8,128)(2,1)}, bf16[4,64,512]{2,1,0:T(8,128)(2,1)S(1)}, u32[]{:S(2)}, u32[]{:S(2)}) collective-permute-start(bf16[4,64,512]{2,1,0:T(8,128)(2,1)} %slice.207), channel_id=1, source_target_pairs={{0,4},{2,6},{4,0},{6,2},{8,12},{10,14},{12,8},{14,10},{16,20},{18,... | collective-permute-start | bytes 786440 | tf_op jit(solution)/shard_map/ppermute | solution.py:47
  189.3 9.4 %collective-permute-start.30 = (bf16[144,512]{1,0:T(8,128)(2,1)S(1)}, bf16[144,512]{1,0:T(8,128)(2,1)S(1)}, u32[]{:S(2)}, u32[]{:S(2)}) collective-permute-start(bf16[144,512]{1,0:T(8,128)(2,1)S(1)} %get-tuple-element.56), channel_id=1, source_target_pairs={{0,8},{2,10},{4,12},{6,14},{8,16},{10,18},{12,20},{14,22},{16,24},... | collective-permute-start | bytes 442376 | tf_op jit(solution)/shard_map/ppermute | solution.py:43
  195.5 9.0 %collective-permute-start.31 = (bf16[144,512]{1,0:T(8,128)(2,1)S(1)}, bf16[144,512]{1,0:T(8,128)(2,1)S(1)}, u32[]{:S(2)}, u32[]{:S(2)}) collective-permute-start(bf16[144,512]{1,0:T(8,128)(2,1)S(1)} %get-tuple-element.58), channel_id=1, source_target_pairs={{0,16},{2,18},{4,20},{6,22},{8,24},{10,26},{12,28},{14,30},{16,0},... | collective-permute-start | bytes 442376 | tf_op jit(solution)/shard_map/ppermute | solution.py:43
  (16 other events, 163.0 us)

commit v2 on v1

v2 whole, which is shorter than its diff:
```python
import jax
import jax.numpy as jnp
from jax import lax
from jax.experimental import pallas as pl
from jax.experimental.pallas import tpu as pltpu
from jax.sharding import PartitionSpec as P

D = 512
H = 8
HD = 64
K = 4
FF = 2048
SEQ = 1024
SEG = 512
PIECES = 32
ROWS = D // PIECES
EXT = 3 * D + 128
GCOL = 8
GLEN = 2 * D // PIECES
NEG = -1e30
BF = jnp.bfloat16
F32 = jnp.float32
AXES = ("dp", "fsdp")
NT = (((1,), (1,)), ((), ()))
TN = (((0,), (0,)), ((), ()))
ANY = pl.BlockSpec(memory_space=pl.ANY)
VLIMIT = 60 * 1024 * 1024


def mm(a, b):
    return jnp.dot(a, b, preferred_element_type=F32)


def mm_nt(a, b):
    return lax.dot_general(a, b, NT, preferred_element_type=F32)


def mm_tn(a, b):
    return lax.dot_general(a, b, TN, preferred_element_type=F32)


def perm_z(v, shift):
    return lax.ppermute(v, "dp", [(i, (i + 4 * shift) % 16) for i in range(16)])


def perm_bit(v, bit):
    return lax.ppermute(v, "dp", [(i, i ^ bit) for i in range(16)])


def perm_core(v):
    return lax.ppermute(v, "fsdp", [(0, 1), (1, 0)])


def after(values, *others):
    done = lax.optimization_barrier((tuple(values), tuple(others)))
    return done[0]


def gather_z(shard):
    return jnp.stack([shard] + [perm_z(shard, -k) for k in (1, 2, 3)])


def gather_plane(stacked):
    return [stacked] + [perm_bit(stacked, bits) for bits in (1, 2, 3)]


def gather_core(parts):
    return list(parts) + [perm_core(part) for part in parts]


def add(keep, got):
    return keep.astype(F32) + got.astype(F32)


def add_z(total):
    out = total[0]
    for k in (1, 2, 3):
        out = out + perm_z(total[k].astype(BF), k).astype(F32)
    return out


def owner_fn(relative, x_first):
    def owner(piece):
        place = lax.axis_index("dp")
        z, y, x = place >> 2, (place >> 1) & 1, place & 1
        kz, low, high, kc = piece & 3, (piece >> 2) & 1, (piece >> 3) & 1, piece >> 4
        kx, ky = (low, high) if x_first else (high, low)
        chip = ((((z + kz) & 3) * 2 + (y ^ ky)) * 2) + (x ^ kx)
        return chip * 2 + (lax.axis_index("fsdp") ^ kc)

    return owner if relative else (lambda piece: piece)


def bias_kernel(doc_row, doc_col, slots, bias):
    sources = lax.broadcasted_iota(jnp.int32, (SEG, SEG), 0)
    places = lax.broadcasted_iota(jnp.int32, (SEG, SEG), 1)
    for seg in range(2):
        part = slice(seg * SEG, (seg + 1) * SEG)
        same = doc_col[part, :] == doc_row[:, part]
        bias[seg] = jnp.where((sources <= places) & same, 0.0, NEG)
    count = jnp.zeros((SEG, SEG), F32)
    for c in range(K):
        count = count + jnp.where(sources == slots[c : c + 1, :], 1.0, 0.0)
    kept = (doc_col[0:SEG, :] == doc_row[:, SEG : 2 * SEG]) & (count > 0.0)
    bias[2] = jnp.where(kept, jnp.log(jnp.maximum(count, 1.0)), NEG)


def rows_from_ext(ext):
    pick = lax.broadcasted_iota(jnp.int32, (PIECES, D), 1) == ROWS * lax.broadcasted_iota(
        jnp.int32, (PIECES, D), 0
    )
    gains = mm(pick.astype(BF), ext).astype(BF)
    source = lax.broadcasted_iota(jnp.int32, (128, D), 0) - GCOL
    column = lax.broadcasted_iota(jnp.int32, (128, D), 1)
    spread = mm(gains, (source == (column & (GLEN - 1))).astype(BF))
    piece = lax.broadcasted_iota(jnp.int32, (PIECES, D), 0)
    block = lax.broadcasted_iota(jnp.int32, (PIECES, D), 1) // GLEN
    one = jnp.sum(jnp.where(block == piece, spread, 0.0), axis=0, keepdims=True)
    two = jnp.sum(jnp.where(block + D // GLEN == piece, spread, 0.0), axis=0, keepdims=True)
    return one, two


def ext_from_gains(column, gain, two):
    row_id = lax.broadcasted_iota(jnp.int32, (D, 128), 0)
    lane = lax.broadcasted_iota(jnp.int32, (D, 128), 1) - GCOL
    target = (lane == (row_id & (GLEN - 1))).astype(BF)
    piece = lax.broadcasted_iota(jnp.int32, (PIECES, D), 0)
    block = lax.broadcasted_iota(jnp.int32, (PIECES, D), 1) // GLEN
    gain_rows = jnp.where(block == piece, 1.0 / gain, 0.0)
    one = lax.dot_general(
        gain_rows,
        jnp.where(lane == (row_id & (GLEN - 1)), column, 0.0),
        (((1,), (0,)), ((), ())),
        precision=lax.Precision.HIGHEST,
        preferred_element_type=F32,
    )
    laid = jnp.where(block + D // GLEN == piece, two, 0.0)
    packed = (one + mm(laid.astype(BF), target)).astype(BF)
    pick = lax.broadcasted_iota(jnp.int32, (D, PIECES), 0) == ROWS * lax.broadcasted_iota(
        jnp.int32, (D, PIECES), 1
    )
    return mm(pick.astype(BF), packed)


def start_pieces(parts, owner, make):
    base = 0
    for part in parts:
        for i in range(part.shape[0]):
            make(part.at[i], owner(base + i)).start()
        base += part.shape[0]


def head_half(rows, upper_half):
    blank = jnp.zeros_like(rows)
    return jnp.concatenate([blank, rows] if upper_half else [rows, blank], axis=0)


PROB_ROWS = 2 * 768 + 1024


def params():
    return pltpu.CompilerParams(vmem_limit_bytes=VLIMIT)


def shape(*dims, dtype=BF):
    return jax.ShapeDtypeStruct(dims, dtype)


def block_rows(d, size):
    return pl.ds(pl.multiple_of(d * size, size), size)


SPOTS = [(seg, ib) for seg in range(3) for ib in range(2)]


def spot(seg, ib):
    key_first = SEG if seg == 1 else 0
    key_count = SEG if seg == 2 else 256 * (ib + 1)
    column = (0 if seg == 0 else SEG) + 256 * ib
    base = 768 * seg + ib * (SEG if seg == 2 else 256)
    return key_first, key_count, column, base


def attention_kernel(owner, count, *refs):
    x_hbm, bias_hbm = refs[:2]
    parts = refs[2 : 2 + count]
    (
        w_o,
        vtok_o,
        qkvt_o,
        hidt_o,
        gatet,
        gains,
        probs,
        local_t,
        mem_t,
        inv_sums,
        mixed_t,
        x,
        bias,
        w,
        ktok,
        vtok,
        qkvt,
        hidt,
        in_sem,
        out_sem,
    ) = refs[2 + count :]
    pair = pl.program_id(0)
    late_out = [(w, w_o), (vtok, vtok_o), (qkvt, qkvt_o), (hidt, hidt_o)]

    @pl.when(pair == 0)
    def _():
        start_pieces(
            parts,
            owner,
            lambda src, d: pltpu.make_async_copy(src, w.at[block_rows(d, ROWS)], in_sem.at[0]),
        )
        pltpu.make_async_copy(x_hbm, x, in_sem.at[1]).start()
        pltpu.make_async_copy(bias_hbm, bias, in_sem.at[2]).start()
        pltpu.make_async_copy(w_o, w, in_sem.at[0]).wait()
        pltpu.make_async_copy(x_hbm, x, in_sem.at[1]).wait()
        g_one, g_two = rows_from_ext(w[:, 3 * D :])
        gains[...] = jnp.concatenate([g_one, g_two], axis=0)
        for block in range(4):
            rows = slice(256 * block, 256 * block + 256)
            xf = x[rows, :].astype(F32)
            factor = lax.rsqrt(jnp.mean(xf * xf, axis=1, keepdims=True) + 1e-06)
            hid = (xf * factor * g_one).astype(BF)
            hidt[:, rows] = hid.T
            query = mm(hid, w[:, 0:D]).astype(BF) * 0.125
            qkvt[0:D, rows] = query.T
            key = mm(hid, w[:, D : 2 * D]).astype(BF)
            ktok[rows, :] = key
            value = mm(hid, w[:, 2 * D : 3 * D]).astype(BF)
            vtok[rows, :] = value
            qkvt[D : 2 * D, rows] = key.T
            qkvt[2 * D : 3 * D, rows] = value.T
            gatet[:, rows] = jax.nn.sigmoid(mm(hid, w[:, 3 * D :])).T[0:H, :]
        for i, (src, dst) in enumerate(late_out):
            pltpu.make_async_copy(src, dst, out_sem.at[i]).start()
        pltpu.make_async_copy(bias_hbm, bias, in_sem.at[2]).wait()

    lanes = block_rows(pair, 128)
    gates = [gatet[pl.ds(2 * pair + hh, 1), :] for hh in range(2)]

    def head_rows(third, hh, first, count):
        start = pl.multiple_of(third * D + pair * 128 + hh * HD, HD)
        return qkvt[pl.ds(start, HD), first : first + count]

    def scores(hh, seg, ib):
        key_first, key_count, column, base = spot(seg, ib)
        query = head_half(head_rows(0, hh, column, 256), hh)
        return mm(ktok[key_first : key_first + key_count, lanes], query)

    def soft(score, hh, seg, ib):
        key_first, key_count, column, base = spot(seg, ib)
        score = score + bias[seg, 0:key_count, 256 * ib : 256 * ib + 256]
        peak = jnp.max(score, axis=0, keepdims=True)
        if seg == 2:
            peak = jnp.maximum(peak, 0.0)
        expo = jnp.exp(score - peak)
        total = jnp.sum(expo, axis=0, keepdims=True)
        if seg == 2:
            total = total + jnp.exp(-peak)
        expo_b = expo.astype(BF)
        probs[0, hh, base : base + key_count, :] = expo_b
        return expo_b, 1.0 / total

    held = {}

    def close(expo_b, inverse, hh, seg, ib):
        key_first, key_count, column, base = spot(seg, ib)
        rows = slice(hh * HD, (hh + 1) * HD)
        found = mm(head_rows(2, hh, key_first, key_count), expo_b) * inverse
        here = gates[hh][:, column : column + 256]
        if seg < 2:
            local_t[rows, column : column + 256] = found.astype(BF)
            inv_sums[0, hh : hh + 1, column : column + 256] = inverse
            if seg == 0:
                mixed_t[rows, column : column + 256] = (here * found).astype(BF)
            else:
                held[hh, ib] = here * found
            return
        mem_t[rows, 256 * ib : 256 * ib + 256] = found.astype(BF)
        inv_sums[0, 2 + hh : 3 + hh, 256 * ib : 256 * ib + 256] = inverse
        mixed_t[rows, column : column + 256] = (
            held.pop((hh, ib)) + (1.0 - here) * found
        ).astype(BF)

    order = [(hh, seg, ib) for ib in range(2) for seg in range(3) for hh in range(2)]
    waiting = scores(*order[0])
    late = None
    for i, item in enumerate(order):
        score = waiting
        if i + 1 < len(order):
            waiting = scores(*order[i + 1])
        expo_b, inverse = soft(score, *item)
        if late is not None:
            close(*late)
        late = (expo_b, inverse) + item
    close(*late)
    inv_sums[0, 2:4, SEG:] = jnp.zeros((2, SEG), F32)

    @pl.when(pair == 3)
    def _():
        for i, (src, dst) in enumerate(late_out):
            pltpu.make_async_copy(src, dst, out_sem.at[i]).wait()


def attention(x, bias, parts, owner, deps=()):
    count_in = 2 + len(parts)

    def body(*refs):
        attention_kernel(owner, len(parts), *refs[:count_in], *refs[count_in + len(deps) :])

    const2 = lambda p: (0, 0)
    down = lambda p: (p, 0)
    return pl.pallas_call(
        body,
        grid=(4,),
        in_specs=[ANY] * (count_in + len(deps)),
        out_specs=[
            ANY,
            ANY,
            ANY,
            ANY,
            pl.BlockSpec((H, SEQ), const2),
            pl.BlockSpec((2, D), const2),
            pl.BlockSpec((1, 2, PROB_ROWS, 256), lambda p: (p, 0, 0, 0)),
            pl.BlockSpec((128, SEQ), down),
            pl.BlockSpec((128, SEG), down),
            pl.BlockSpec((1, 4, SEQ), lambda p: (p, 0, 0)),
            pl.BlockSpec((128, SEQ), down),
        ],
        out_shape=[
            shape(D, EXT),
            shape(SEQ, D),
            shape(3 * D, SEQ),
            shape(D, SEQ),
            shape(H, SEQ, dtype=F32),
            shape(2, D, dtype=F32),
            shape(4, 2, PROB_ROWS, 256),
            shape(D, SEQ),
            shape(D, SEG),
            shape(4, 4, SEQ, dtype=F32),
            shape(D, SEQ),
        ],
        scratch_shapes=[
            pltpu.VMEM((SEQ, D), BF),
            pltpu.VMEM((3, SEG, SEG), F32),
            pltpu.VMEM((D, EXT), BF),
            pltpu.VMEM((SEQ, D), BF),
            pltpu.VMEM((SEQ, D), BF),
            pltpu.VMEM((3 * D, SEQ), BF),
            pltpu.VMEM((D, SEQ), BF),
            pltpu.SemaphoreType.DMA((3,)),
            pltpu.SemaphoreType.DMA((4,)),
        ],
        compiler_params=params(),
        cost_estimate=pl.CostEstimate(
            flops=18_000_000_000, bytes_accessed=40_000_000, transcendentals=6_000_000
        ),
        name="attention",
    )(x, bias, *parts, *deps)


TILE = 256
TILES = FF // TILE


def ffn_kernel(owner_u, owner_d, count, count_o, *refs):
    x_hbm, cot_hbm, mixt_hbm, gains = refs[:4]
    parts_u = refs[4 : 4 + count]
    parts_d = refs[4 + count : 4 + 2 * count]
    refs = refs[4 + 2 * count :]
    layer_o, d_resid_o, dmix_o, dgain = refs[:4]
    grads_u = refs[4 : 4 + count_o]
    grads_d = refs[4 + count_o : 4 + 2 * count_o]
    (
        x,
        cot,
        mixt,
        w_out,
        w_up,
        w_dn,
        hid,
        hidt,
        resid,
        oacc,
        dacc,
        dmix,
        g_out,
        g_up,
        g_dn,
        held_up,
        held_act,
        acts,
        d_ups,
        factors,
        in_sem,
        out_sem,
    ) = refs[4 + 2 * count_o :]
    per = PIECES // count_o

    def lanes_of(tile):
        return pl.ds(pl.multiple_of((tile % 2) * TILE, TILE), TILE)

    def up_tile(tile):
        return w_up[tile // 2, :, lanes_of(tile)]

    def dn_tile(tile):
        return w_dn[pl.ds(tile * (TILE // ROWS), TILE // ROWS)].reshape(TILE, D)

    def head_up(tile, slot):
        held_up[slot] = mm(hid[...], up_tile(tile))

    def head_act(tile, slot):
        held_act[slot] = mm_nt(cot[...], dn_tile(tile))

    def head(tile, slot):
        head_up(tile, slot)
        head_act(tile, slot)

    def gelu(slot, first, last):
        c0 = 0.7978845608028654
        c1 = 0.044715
        for block in range(first, last):
            rows = slice(64 * block, 64 * block + 64)
            upper = held_up[slot, rows, :]
            square = upper * upper
            tanh = jnp.tanh(upper * (c0 + (c0 * c1) * square))
            half_t = 0.5 * tanh + 0.5
            slope = half_t + upper * (1.0 - tanh * tanh) * (0.5 * c0 + (1.5 * c0 * c1) * square)
            acts[slot, rows, :] = (upper * half_t).astype(BF)
            d_ups[slot, rows, :] = (held_act[slot, rows, :] * slope).astype(BF)

    def tail_out(tile, slot):
        oacc[...] += mm(acts[slot], dn_tile(tile))

    def tail_hid(tile, slot):
        dacc[...] += mm_nt(d_ups[slot], up_tile(tile))

    def tail_dn(tile, slot):
        g_dn[pl.ds(tile * (TILE // ROWS), TILE // ROWS)] = (
            mm_tn(acts[slot], cot[...]).astype(BF).reshape(TILE // ROWS, ROWS, D)
        )

    def tail_up(tile, slot):
        g_up[tile // 2, :, lanes_of(tile)] = mm(hidt[...], d_ups[slot]).astype(BF)

    def tail(tile, slot):
        tail_out(tile, slot)
        tail_hid(tile, slot)
        tail_dn(tile, slot)
        tail_up(tile, slot)

    def spread(step, now):
        later = jnp.minimum(step + 1, TILES - 1)
        before = jnp.maximum(step - 1, 0)
        jobs = (tail_dn, tail_out, head_up, tail_up, tail_hid, head_act)
        count = 16
        for i, job in enumerate(jobs):
            gelu(now, count * i // 6, count * (i + 1) // 6)
            job(later if job in (head_up, head_act) else before, 1 - now)

    start_pieces(
        parts_u,
        owner_u,
        lambda src, d: pltpu.make_async_copy(
            src.at[0], w_out.at[block_rows(d, ROWS), :], in_sem.at[0]
        ),
    )
    pltpu.make_async_copy(mixt_hbm, mixt, in_sem.at[4]).start()
    pltpu.make_async_copy(x_hbm, x, in_sem.at[5]).start()
    start_pieces(
        parts_u,
        owner_u,
        lambda src, d: pltpu.make_async_copy(
            src.at[pl.ds(1, 4)], w_up.at[:, block_rows(d, ROWS), :], in_sem.at[1]
        ),
    )
    start_pieces(
        parts_d,
        owner_d,
        lambda src, d: pltpu.make_async_copy(src, w_dn.at[pl.ds(d * 4, 4)], in_sem.at[2]),
    )
    pltpu.make_async_copy(cot_hbm, cot, in_sem.at[3]).start()
    pltpu.make_async_copy(g_out, w_out, in_sem.at[0]).wait()
    pltpu.make_async_copy(mixt_hbm, mixt, in_sem.at[4]).wait()
    pltpu.make_async_copy(x_hbm, x, in_sem.at[5]).wait()
    dacc[...] = jnp.zeros_like(dacc)
    acts[1] = jnp.zeros((SEQ, TILE), BF)
    d_ups[1] = jnp.zeros((SEQ, TILE), BF)
    for block in range(4):
        rows = slice(256 * block, 256 * block + 256)
        value = x[rows, :].astype(F32) + mm_tn(mixt[:, rows], w_out[...])
        factor = lax.rsqrt(jnp.mean(value * value, axis=1, keepdims=True) + 1e-06)
        normed = (value * factor * gains[1:2, :]).astype(BF)
        factors[rows, :] = factor
        resid[rows, :] = value
        oacc[rows, :] = value
        hid[rows, :] = normed
        hidt[:, rows] = normed.T
    pltpu.make_async_copy(g_up, w_up, in_sem.at[1]).wait()
    pltpu.make_async_copy(g_dn, w_dn, in_sem.at[2]).wait()
    pltpu.make_async_copy(cot_hbm, cot, in_sem.at[3]).wait()
    head(0, 0)

    @pl.loop(0, TILES)
    def _(step):
        spread(step, step % 2)

    tail(TILES - 1, (TILES - 1) % 2)
    for piece in range(PIECES):
        pltpu.make_async_copy(
            g_up.at[:, block_rows(owner_u(piece), ROWS), :],
            grads_u[piece // per].at[piece % per, pl.ds(1, 4)],
            out_sem.at[0],
        ).start()
        pltpu.make_async_copy(
            g_dn.at[pl.ds(owner_d(piece) * 4, 4)],
            grads_d[piece // per].at[piece % per],
            out_sem.at[1],
        ).start()
    g_two = gains[1:2, :]
    total = jnp.zeros((1, D), F32)
    for block in range(16):
        rows = slice(64 * block, 64 * block + 64)
        value = resid[rows, :]
        factor = factors[rows, :]
        d_hid = dacc[rows, :]
        product = d_hid * value
        total = total + jnp.sum(product * factor, axis=0, keepdims=True)
        inner = jnp.mean(product * g_two, axis=1, keepdims=True)
        d_resid = cot[rows, :].astype(F32) + (
            factor * (d_hid * g_two) - value * (factor * factor * factor * inner)
        )
        x[rows, :] = oacc[rows, :].astype(BF)
        resid[rows, :] = d_resid
        hid[rows, :] = d_resid.astype(BF)
    dgain[...] = total
    pltpu.make_async_copy(x, layer_o, out_sem.at[2]).start()
    pltpu.make_async_copy(resid, d_resid_o, out_sem.at[3]).start()
    g_out[...] = mm(mixt[...], hid[...]).astype(BF)
    for piece in range(PIECES):
        pltpu.make_async_copy(
            g_out.at[block_rows(owner_u(piece), ROWS), :],
            grads_u[piece // per].at[piece % per, 0],
            out_sem.at[5],
        ).start()
    dmix[...] = mm_nt(w_out[...], hid[...]).astype(BF)
    pltpu.make_async_copy(dmix, dmix_o, out_sem.at[4]).start()
    pltpu.make_async_copy(g_up, w_up, out_sem.at[0]).wait()
    pltpu.make_async_copy(g_dn, w_dn, out_sem.at[1]).wait()
    pltpu.make_async_copy(x, layer_o, out_sem.at[2]).wait()
    pltpu.make_async_copy(resid, d_resid_o, out_sem.at[3]).wait()
    pltpu.make_async_copy(g_out, w_out, out_sem.at[5]).wait()
    pltpu.make_async_copy(dmix, dmix_o, out_sem.at[4]).wait()


def ffn(x, cot, mixed_t, gains, parts_u, parts_d, owner_u, owner_d, count_o):
    def body(*refs):
        ffn_kernel(owner_u, owner_d, len(parts_u), count_o, *refs)

    return pl.pallas_call(
        body,
        in_specs=[ANY, ANY, ANY, pl.BlockSpec(memory_space=pltpu.VMEM)]
        + [ANY] * (len(parts_u) + len(parts_d)),
        out_specs=[ANY, ANY, ANY, pl.BlockSpec(memory_space=pltpu.VMEM)] + [ANY] * (2 * count_o),
        out_shape=[
            shape(SEQ, D),
            shape(SEQ, D, dtype=F32),
            shape(D, SEQ),
            shape(1, D, dtype=F32),
        ]
        + [shape(PIECES // count_o, 5, ROWS, D)] * count_o
        + [shape(PIECES // count_o, 4, ROWS, D)] * count_o,
        scratch_shapes=[
            pltpu.VMEM((SEQ, D), BF),
            pltpu.VMEM((SEQ, D), BF),
            pltpu.VMEM((D, SEQ), BF),
            pltpu.VMEM((D, D), BF),
            pltpu.VMEM((4, D, D), BF),
            pltpu.VMEM((FF // ROWS, ROWS, D), BF),
            pltpu.VMEM((SEQ, D), BF),
            pltpu.VMEM((D, SEQ), BF),
            pltpu.VMEM((SEQ, D), F32),
            pltpu.VMEM((SEQ, D), F32),
            pltpu.VMEM((SEQ, D), F32),
            pltpu.VMEM((D, SEQ), BF),
            pltpu.VMEM((D, D), BF),
            pltpu.VMEM((4, D, D), BF),
            pltpu.VMEM((FF // ROWS, ROWS, D), BF),
            pltpu.VMEM((2, SEQ, TILE), F32),
            pltpu.VMEM((2, SEQ, TILE), F32),
            pltpu.VMEM((2, SEQ, TILE), BF),
            pltpu.VMEM((2, SEQ, TILE), BF),
            pltpu.VMEM((SEQ, 1), F32),
            pltpu.SemaphoreType.DMA((6,)),
            pltpu.SemaphoreType.DMA((6,)),
        ],
        compiler_params=params(),
        cost_estimate=pl.CostEstimate(
            flops=25_000_000_000, bytes_accessed=25_000_000, transcendentals=2_000_000
        ),
        name="feed_forward",
    )(x, cot, mixed_t, gains, *parts_u, *parts_d)


def attention_back_kernel(first, last, owner, count_o, *refs):
    (gatet, w_hbm, hidt_hbm, probs, local_t, mem_t, inv_sums, dmix_t, qt, kt, vtok) = refs[:11]
    refs = refs[11:]
    if last:
        gains, dgain_two, before, gates_before, grad_before = refs[:5]
        refs = refs[5:]
    else:
        count_o = 1
    dqkvt, d_gates, *refs = refs
    if not last:
        weighted = refs[0]
        refs = refs[1:]
    grads = refs[:count_o]
    w, hidt, scratch, gate_rows, g_ext, in_sem, out_sem = refs[count_o:]
    pair = pl.program_id(0)
    per = PIECES // count_o

    def before_columns(third):
        return pltpu.make_async_copy(
            grad_before.at[third], g_ext.at[:, pl.ds(third * D, 256)], in_sem.at[2]
        )

    @pl.when(pair == 0)
    def _():
        pltpu.make_async_copy(hidt_hbm, hidt, in_sem.at[0]).start()
        pltpu.make_async_copy(w_hbm, w, in_sem.at[1]).start()
        if last:
            for third in range(3):
                before_columns(third).start()

    ups = {}
    dots = {}
    for hh in range(2):
        rows = slice(hh * HD, (hh + 1) * HD)
        gate = gatet[pl.ds(2 * (first + pair) + hh, 1), :]
        d_mix = dmix_t[rows, :].astype(F32)
        local = local_t[rows, :].astype(F32)
        mem = mem_t[rows, :].astype(F32)
        inv_local = inv_sums[0, hh : hh + 1, :]
        inv_mem = inv_sums[0, 2 + hh : 3 + hh, 0:SEG]
        d_local = (d_mix * (gate * inv_local)).astype(BF)
        d_mem = (d_mix[:, SEG:] * ((1.0 - gate[:, SEG:]) * inv_mem)).astype(BF)
        dot_local = jnp.sum(d_local.astype(F32) * local, axis=0, keepdims=True)
        dot_mem = jnp.sum(d_mem.astype(F32) * mem, axis=0, keepdims=True)
        plain_local = jnp.sum(d_mix * local, axis=0, keepdims=True)
        plain_mem = jnp.sum(d_mix[:, SEG:] * mem, axis=0, keepdims=True)
        d_gate = gate * (1.0 - gate) * (
            plain_local - jnp.concatenate([jnp.zeros((1, SEG), F32), plain_mem], axis=1)
        )
        d_gates[0, hh : hh + 1, :] = d_gate
        gate_rows[pl.ds(2 * pair + hh, 1), :] = d_gate
        for seg, ib in SPOTS:
            column = spot(seg, ib)[2]
            if seg == 2:
                ups[hh, seg, ib] = d_mem[:, 256 * ib : 256 * ib + 256]
                dots[hh, seg, ib] = dot_mem[:, 256 * ib : 256 * ib + 256]
            else:
                ups[hh, seg, ib] = d_local[:, column : column + 256]
                dots[hh, seg, ib] = dot_local[:, column : column + 256]

    sums_of = {}

    def add(key, value):
        sums_of[key] = value if key not in sums_of else sums_of[key] + value

    def begin(hh, seg, ib):
        key_first, key_count, column, base = spot(seg, ib)
        return mm(vtok[key_first : key_first + key_count, :], head_half(ups[hh, seg, ib], hh))

    def middle(d_prob, hh, seg, ib):
        key_first, key_count, column, base = spot(seg, ib)
        expo = probs[0, hh, base : base + key_count, :]
        return (expo.astype(F32) * (d_prob - dots[hh, seg, ib])).astype(BF), expo

    def close(d_score, expo, hh, seg, ib):
        key_first, key_count, column, base = spot(seg, ib)
        rows = slice(hh * HD, (hh + 1) * HD)
        add((0, hh, column // 256), mm(kt[rows, key_first : key_first + key_count], d_score))
        key_term = mm_nt(qt[rows, column : column + 256], d_score)
        value_term = mm_nt(ups[hh, seg, ib], expo)
        for part in range(key_count // 256):
            place = key_first // 256 + part
            add((1, hh, place), key_term[:, 256 * part : 256 * part + 256])
            add((2, hh, place), value_term[:, 256 * part : 256 * part + 256])

    order = [(hh, seg, ib) for seg in (0, 2, 1) for ib in range(2) for hh in range(2)]
    waiting = begin(*order[0])
    late = None
    for i, item in enumerate(order):
        d_prob = waiting
        if i + 1 < len(order):
            waiting = begin(*order[i + 1])
        d_score, expo = middle(d_prob, *item)
        if late is not None:
            close(*late)
        late = (d_score, expo) + item
    close(*late)
    for (third, hh, place), value in sums_of.items():
        if third == 0:
            value = value * 0.125
        rows = slice(hh * HD, (hh + 1) * HD)
        dqkvt[third, rows, 256 * place : 256 * place + 256] = value.astype(BF)
    scratch[:, block_rows(pair, 128), :] = dqkvt[...]

    @pl.when(pair == 1)
    def _():
        pltpu.make_async_copy(hidt_hbm, hidt, in_sem.at[0]).wait()
        pltpu.make_async_copy(w_hbm, w, in_sem.at[1]).wait()
        sums = jnp.zeros((D, 128), F32)
        for third in range(3):
            grad = mm_nt(hidt[...], scratch[third])
            start = third * D + first * 128
            for part in range(2):
                columns = slice(start + 128 * part, start + 128 * part + 128)
                sums = sums + grad[:, 128 * part : 128 * part + 128] * w[:, columns].astype(F32)
            if last:
                g_ext[:, third * D + 256 : third * D + 512] = grad.astype(BF)
            else:
                g_ext[third] = grad.astype(BF)
        if last:
            d_gate_b = jnp.concatenate(
                [
                    gates_before[0],
                    gates_before[1],
                    gate_rows[0:4, :],
                    jnp.zeros((120, SEQ), F32),
                ],
                axis=0,
            ).astype(BF)
            grad = mm_nt(hidt[...], d_gate_b)
            gate_lane = lax.broadcasted_iota(jnp.int32, (D, 128), 1) < H
            sums = sums + before[...] + jnp.where(
                gate_lane, grad * w[:, 3 * D :].astype(F32), 0.0
            )
            column = jnp.sum(sums, axis=1, keepdims=True)
            g_ext[:, 3 * D :] = (grad + ext_from_gains(column, gains[0:1, :], dgain_two[...])).astype(
                BF
            )
        if not last:
            weighted[...] = sums
            pltpu.make_async_copy(g_ext, grads[0], out_sem).start()
            pltpu.make_async_copy(g_ext, grads[0], out_sem).wait()
        else:
            for third in range(3):
                before_columns(third).wait()
            for piece in range(PIECES):
                pltpu.make_async_copy(
                    g_ext.at[block_rows(owner(piece), ROWS), :],
                    grads[piece // per].at[piece % per],
                    out_sem,
                ).start()
            pltpu.make_async_copy(w, g_ext, out_sem).wait()


def attention_back(
    first, gatet, w, hidt, saved, dmix_t, qkvt, vtok, owner, count_o, extra=(), deps=()
):
    last = len(extra) > 0
    const2 = lambda p: (0, 0)
    count_in = 11 + len(extra)

    def body(*refs):
        attention_back_kernel(
            first, last, owner, count_o, *refs[:count_in], *refs[count_in + len(deps) :]
        )

    extra_specs = []
    if last:
        extra_specs = [
            pl.BlockSpec((2, D), const2),
            pl.BlockSpec((1, D), const2),
            pl.BlockSpec((D, 128), const2),
            pl.BlockSpec((2, 2, SEQ), lambda p: (0, 0, 0)),
            ANY,
        ]
    sums_spec = [] if last else [pl.BlockSpec((D, 128), const2)]
    sums_shape = [] if last else [shape(D, 128, dtype=F32)]
    return pl.pallas_call(
        body,
        grid=(2,),
        in_specs=[
            pl.BlockSpec((H, SEQ), const2),
            ANY,
            ANY,
            pl.BlockSpec((1, 2, PROB_ROWS, 256), lambda p: (first + p, 0, 0, 0)),
            pl.BlockSpec((128, SEQ), lambda p: (first + p, 0)),
            pl.BlockSpec((128, SEG), lambda p: (first + p, 0)),
            pl.BlockSpec((1, 4, SEQ), lambda p: (first + p, 0, 0)),
            pl.BlockSpec((128, SEQ), lambda p: (first + p, 0)),
            pl.BlockSpec((128, SEQ), lambda p: (first + p, 0)),
            pl.BlockSpec((128, SEQ), lambda p: (4 + first + p, 0)),
            pl.BlockSpec((SEQ, 128), lambda p: (0, first + p)),
        ]
        + extra_specs
        + [ANY] * len(deps),
        out_specs=[
            pl.BlockSpec((3, 128, SEQ), lambda p: (0, p, 0)),
            pl.BlockSpec((1, 2, SEQ), lambda p: (p, 0, 0)),
        ]
        + sums_spec
        + [ANY] * (count_o if last else 1),
        out_shape=[shape(3, 256, SEQ), shape(2, 2, SEQ, dtype=F32)]
        + sums_shape
        + ([shape(PIECES // count_o, ROWS, EXT)] * count_o if last else [shape(3, D, 256)]),
        scratch_shapes=[
            pltpu.VMEM((D, EXT), BF),
            pltpu.VMEM((D, SEQ), BF),
            pltpu.VMEM((3, 256, SEQ), BF),
            pltpu.VMEM((8, SEQ), F32),
            pltpu.VMEM((D, EXT) if last else (3, D, 256), BF),
            pltpu.SemaphoreType.DMA((3,)),
            pltpu.SemaphoreType.DMA,
        ],
        compiler_params=params(),
        cost_estimate=pl.CostEstimate(
            flops=11_000_000_000, bytes_accessed=20_000_000, transcendentals=0
        ),
        name="attention_back",
    )(gatet, w, hidt, *saved, dmix_t, qkvt, qkvt, vtok, *extra, *deps)


def input_back_kernel(x, d_resid, gains, w, da, db, gates_a, gates_b, grad_in):
    d_gate = jnp.concatenate(
        [gates_a[0], gates_a[1], gates_b[0], gates_b[1], jnp.zeros((120, 256), F32)], axis=0
    ).astype(BF)
    d_hid = mm(w[:, 3 * D :], d_gate)
    for third in range(3):
        start = third * D
        d_hid = d_hid + mm(w[:, start : start + 256], da[third])
        d_hid = d_hid + mm(w[:, start + 256 : start + 512], db[third])
    d_hid = d_hid.T
    xf = x[...].astype(F32)
    factor = lax.rsqrt(jnp.mean(xf * xf, axis=1, keepdims=True) + 1e-06)
    scaled = d_hid * gains[0:1, :]
    inner = jnp.mean(scaled * xf, axis=1, keepdims=True)
    grad_in[...] = (
        d_resid[...] + factor * scaled - xf * (factor * factor * factor * inner)
    ).astype(BF)


def input_back(x, d_resid, gains, w, da, db, gates_a, gates_b, deps=()):
    def body(*refs):
        input_back_kernel(*refs[:8], refs[-1])

    const2 = lambda i: (0, 0)
    rows = lambda i: (i, 0)
    across = lambda i: (0, 0, i)
    return pl.pallas_call(
        body,
        grid=(4,),
        in_specs=[
            pl.BlockSpec((256, D), rows),
            pl.BlockSpec((256, D), rows),
            pl.BlockSpec((2, D), const2),
            pl.BlockSpec((D, EXT), const2),
            pl.BlockSpec((3, 256, 256), across),
            pl.BlockSpec((3, 256, 256), across),
            pl.BlockSpec((2, 2, 256), across),
            pl.BlockSpec((2, 2, 256), across),
        ]
        + [ANY] * len(deps),
        out_specs=pl.BlockSpec((256, D), rows),
        out_shape=shape(SEQ, D),
        compiler_params=params(),
        cost_estimate=pl.CostEstimate(
            flops=5_000_000_000, bytes_accessed=9_000_000, transcendentals=0
        ),
        name="input_back",
    )(x, d_resid, gains, w, da, db, gates_a, gates_b, *deps)


def ext_rows(qkv, gate, gains):
    count = qkv.shape[0]
    blank = jnp.zeros((count, 128 - GCOL - gains.shape[1]), BF)
    return jnp.concatenate([qkv, gate, gains, blank], axis=1)


def local(
    n, inputs, cotangent, doc_ids, slot_ids, qkv_flat, out_flat, norm_gains, gate_flat, up_flat, down_flat
):
    split = n == PIECES
    count_o = 2 if split else 1
    owner_x = owner_fn(split, True)
    owner_y = owner_fn(split, False)
    doc_row = doc_ids.reshape(1, SEQ)
    doc_col = doc_ids.reshape(SEQ, 1)
    slots = slot_ids.reshape(SEG, K).T
    bias = pl.pallas_call(
        bias_kernel,
        out_shape=shape(3, SEG, SEG, dtype=F32),
        name="masks",
    )(doc_row, doc_col, slots)
    if split:
        gains_rows = jnp.broadcast_to(norm_gains.reshape(1, GLEN), (ROWS, GLEN))
        shard_a = ext_rows(qkv_flat.reshape(ROWS, 3 * D), gate_flat.reshape(ROWS, H), gains_rows)
        z_a = gather_z(shard_a)
        shard_f = jnp.concatenate(
            [
                out_flat.reshape(1, ROWS, D),
                up_flat.reshape(ROWS, 4, D).transpose(1, 0, 2),
                down_flat.reshape(4, ROWS, D),
            ]
        )
        plane_a = after(gather_plane(z_a), bias)
        parts_a = gather_core(plane_a)
        z_f = gather_z(shard_f)
        z_u, z_d = z_f[:, :5], z_f[:, 5:]
        wide_u = jnp.concatenate([z_u, perm_bit(z_u, 1)])
        wide_d = jnp.concatenate([z_d, perm_bit(z_d, 2)])
        halves_u = [wide_u, perm_bit(wide_u, 2)]
        halves_d = [wide_d, perm_bit(wide_d, 1)]
        deps = (wide_u, wide_d)
    else:
        whole = [
            lax.all_gather(v, AXES, axis=0, tiled=True)
            for v in (qkv_flat, out_flat, norm_gains, gate_flat, up_flat, down_flat)
        ]
        gains_rows = jnp.repeat(whole[2].reshape(PIECES, GLEN), ROWS, axis=0)
        ext = ext_rows(whole[0].reshape(D, 3 * D), whole[3].reshape(D, H), gains_rows)
        parts_a = (ext.reshape(PIECES, ROWS, EXT),)
        parts_u = (
            jnp.concatenate(
                [
                    whole[1].reshape(PIECES, 1, ROWS, D),
                    whole[4].reshape(PIECES, ROWS, 4, D).transpose(0, 2, 1, 3),
                ],
                axis=1,
            ),
        )
        parts_d = (whole[5].reshape(PIECES, 4, ROWS, D),)
        deps = ()
    w_ext, vtok, qkvt, hidt, gatet, gains, *saved, mixed_t = attention(
        inputs, bias, parts_a, owner_x, deps
    )
    if split:
        far_u, far_d = after((halves_u[1], halves_d[1]), gatet)
        parts_u = gather_core((wide_u, far_u))
        parts_d = gather_core((wide_d, far_d))
    layer_out, d_resid, dmix_t, dgain_two, *grads_f = ffn(
        inputs, cotangent, mixed_t, gains, parts_u, parts_d, owner_x, owner_y, count_o
    )
    da, gates_a, weighted, grad_before = attention_back(
        0, gatet, w_ext, hidt, saved, dmix_t, qkvt, vtok, owner_x, count_o
    )
    deps = ()
    if split:
        keep_u, send_u, keep_d, send_d = grads_f
        got_u, got_d = after((perm_core(send_u), perm_core(send_d)), gates_a)
        firsts = (
            add(keep_u[:8], got_u[:8]),
            add(keep_u[8:], got_u[8:]).astype(BF),
            add(keep_d[:8], got_d[:8]),
            add(keep_d[8:], got_d[8:]).astype(BF),
        )
        deps = firsts
    db, gates_b, *grads_a = attention_back(
        2,
        gatet,
        w_ext,
        hidt,
        saved,
        dmix_t,
        qkvt,
        vtok,
        owner_x,
        count_o,
        (gains, dgain_two, weighted, gates_a, grad_before),
        deps,
    )
    deps = ()
    if split:
        got_u, got_d = after((perm_bit(firsts[1], 2), perm_bit(firsts[3], 1)), gates_b)
        seconds = (
            add(firsts[0][:4], got_u[:4]),
            add(firsts[0][4:], got_u[4:]).astype(BF),
            add(firsts[2][:4], got_d[:4]),
            add(firsts[2][4:], got_d[4:]).astype(BF),
        )
        keep_a, send_a = grads_a
        got_a = perm_core(send_a)
        sends_a = [
            add(keep_a[4 * k : 4 * k + 4], got_a[4 * k : 4 * k + 4]).astype(BF) for k in (1, 2, 3)
        ]
        deps = (*sends_a, seconds[1], seconds[3])
    grad_input = input_back(inputs, d_resid, gains, w_ext, da, db, gates_a, gates_b, deps)
    if split:
        got_u, got_d = after((perm_bit(seconds[1], 1), perm_bit(seconds[3], 2)), grad_input)
        sum_f = add_z(
            jnp.concatenate([add(seconds[0], got_u), add(seconds[2], got_d)], axis=1)
        )
        total_a = add(keep_a[:4], got_a[:4])
        for k in (1, 2, 3):
            total_a = add(total_a, perm_bit(sends_a[k - 1], k))
        sum_a = add_z(total_a)
        grad_out = sum_f[0].reshape(-1)
        grad_up = sum_f[1:5].transpose(1, 0, 2).reshape(-1)
        grad_down = sum_f[5:].reshape(-1)
        grad_qkv = sum_a[:, : 3 * D].reshape(-1)
        grad_gate = sum_a[:, 3 * D : 3 * D + H].reshape(-1)
        grad_gains = sum_a[0, 3 * D + GCOL : 3 * D + GCOL + GLEN]
    else:

        def scatter(v):
            return lax.psum_scatter(
                v.astype(F32).reshape(-1), AXES, scatter_dimension=0, tiled=True
            )

        grad_out = scatter(grads_f[0][:, 0])
        grad_up = scatter(grads_f[0][:, 1:].transpose(0, 2, 1, 3))
        grad_down = scatter(grads_f[1])
        ext = grads_a[0]
        grad_qkv = scatter(ext[:, :, : 3 * D])
        grad_gate = scatter(ext[:, :, 3 * D : 3 * D + H])
        grad_gains = scatter(ext[:, 0, 3 * D + GCOL : 3 * D + GCOL + GLEN])
    return (layer_out, grad_input, grad_qkv, grad_out, grad_gains, grad_gate, grad_up, grad_down)


def solution(mesh):
    n = mesh.shape["dp"] * mesh.shape["fsdp"]

    def per_device(*args):
        return local(n, *args)

    rows = P(AXES, None)
    flat = P(AXES)
    return jax.shard_map(
        per_device,
        mesh=mesh,
        in_specs=(rows, rows, rows, P(AXES, None, None), flat, flat, flat, flat, flat, flat),
        out_specs=(rows, rows, flat, flat, flat, flat, flat, flat),
        check_vma=False,
    )
```

time: 207 us -> 169 us (0.82)
  waiting for transfers between devices: 54.8 us -> 27.6 us
  Pallas kernels: 88 us -> 79 us
  starting transfers between devices: 45.3 us -> 37.8 us
  other arithmetic: 6.42 us -> 10.3 us
    ppermute x14, waiting for transfers between devices: 42.8 us -> 8.75 us  [perm_bit(): return lax.ppermute(v, 'dp', [(i, i ^ bit) for i in range(16)])]
    ppermute x12, starting transfers between devices: 28 us -> 18.9 us  [perm_z(): return lax.ppermute(v, 'dp', [(i, (i + 4 * shift) % 16) for i in range(16)])]
    pallas_call x4 -> x6, Pallas kernels: 88 us -> 79 us  [the longest x1 29.3 us: ffn(): pl.pallas_call(body, in_specs=[ANY, ANY, ANY, pl.BlockSpec(memory_space=p...]
    convert_element_type x0 -> x5, other arithmetic: none -> 6.35 us  [the longest x1 1.9 us: local(): add(firsts[2][4:], got_d[4:]).astype(BF)]
    ppermute x12, waiting for transfers between devices: 10.1 us -> 15.7 us  [perm_z(): return lax.ppermute(v, 'dp', [(i, (i + 4 * shift) % 16) for i in range(16)])]
    concatenate x9 -> x2, other arithmetic: 3.11 us -> 0.11 us  [the longest x1 0.06 us: local(): wide_u = jnp.concatenate([z_u, perm_bit(z_u, 1)])]
    unnamed x19 -> x48, local copies, waits for them, and re-layouts: 2.06 us -> 4.54 us
  transfers between devices with their start and end apart: 33 -> 37, of which waited for: 14 -> 10; matrix products, arithmetic and copies ran while one was open for 6% -> 8% of each run, Pallas kernels for 14% -> 30%
where the time goes in v2:
time: 169 us; the launch traced here: 168 us
  Pallas kernels  79 us (47%)
  starting transfers between devices  37.8 us (22%)
  waiting for transfers between devices  27.6 us (16%)
  local copies, waits for them, and re-layouts  12.5 us (7%)
  other arithmetic  10.3 us (6%)
    pallas_call x1, Pallas kernels, ffn(): pl.pallas_call(body, in_specs=[ANY, ANY, ANY, pl.BlockSpec(memory_space=p...  29.3 us
    pallas_call x2, Pallas kernels, attention_back(): pl.pallas_call(body, grid=(2,), in_specs=[pl.BlockSpec((H, SEQ), const2),...  22.1 us
    ppermute x12, starting transfers between devices, perm_z(): return lax.ppermute(v, 'dp', [(i, (i + 4 * shift) % 16) for i in range(16)])  18.9 us
    pallas_call x1, Pallas kernels, attention(): pl.pallas_call(body, grid=(4,), in_specs=[ANY] * (count_in + len(deps)),...  16.7 us
    ppermute x14, starting transfers between devices, perm_bit(): return lax.ppermute(v, 'dp', [(i, i ^ bit) for i in range(16)])  16.3 us
    ppermute x12, waiting for transfers between devices, perm_z(): return lax.ppermute(v, 'dp', [(i, (i + 4 * shift) % 16) for i in range(16)])  15.7 us
    ppermute x14, waiting for transfers between devices, perm_bit(): return lax.ppermute(v, 'dp', [(i, i ^ bit) for i in range(16)])  8.75 us
    pallas_call x1, Pallas kernels, input_back(): pl.pallas_call(body, grid=(4,), in_specs=[pl.BlockSpec((256, D), rows), p...  7.12 us
  transfers between devices with their start and end apart: 37, of which 10 were waited for; matrix products, arithmetic and copies ran while one was open for 8% of the time, Pallas kernels for 30%

profile of v2, /device:TPU:0, one launch (start us, length us, event | category | flops | bytes accessed | tf_op | source)
XLA Modules:
  0.0 168.3 jit_solution(17699812579290441084)
XLA Ops:
  3.0 3.0 %collective-permute-start.2 = (bf16[16,1664]{1,0:T(8,128)(2,1)S(1)}, bf16[16,1664]{1,0:T(8,128)(2,1)S(1)}, u32[]{:S(2)}, u32[]{:S(2)}) collective-permute-start(bf16[16,1664]{1,0:T(8,128)(2,1)S(1)} %concatenate.15), channel_id=1, source_target_pairs={{0,8},{2,10},{4,12},{6,14},{8,16},{10,18},{12,20},{14,22},{16,24},... | collective-permute-start | bytes 159752 | tf_op jit(solution)/shard_map/ppermute | solution.py:43
  6.1 2.6 %collective-permute-start.1 = (bf16[16,1664]{1,0:T(8,128)(2,1)S(1)}, bf16[16,1664]{1,0:T(8,128)(2,1)S(1)}, u32[]{:S(2)}, u32[]{:S(2)}) collective-permute-start(bf16[16,1664]{1,0:T(8,128)(2,1)S(1)} %concatenate.15), channel_id=1, source_target_pairs={{0,16},{2,18},{4,20},{6,22},{8,24},{10,26},{12,28},{14,30},{16,0},... | collective-permute-start | bytes 159752 | tf_op jit(solution)/shard_map/ppermute | solution.py:43
  12.8 2.9 %collective-permute-start.10 = (bf16[9,16,512]{2,1,0:T(8,128)(2,1)S(1)}, bf16[9,16,512]{2,1,0:T(8,128)(2,1)S(1)}, u32[]{:S(2)}, u32[]{:S(2)}) collective-permute-start(bf16[9,16,512]{2,1,0:T(8,128)(2,1)S(1)} %get-tuple-element.104), channel_id=1, source_target_pairs={{0,24},{2,26},{4,28},{6,30},{8,0},{10,2},{12,4},{14,6},{16,8},{18,... | collective-permute-start | bytes 442376 | tf_op jit(solution)/shard_map/ppermute | solution.py:43
  15.7 2.5 %collective-permute-start.5 = (bf16[4,16,1664]{2,1,0:T(8,128)(2,1)S(1)}, bf16[4,16,1664]{2,1,0:T(8,128)(2,1)S(1)}, u32[]{:S(2)}, u32[]{:S(2)}) collective-permute-start(bf16[4,16,1664]{2,1,0:T(8,128)(2,1)S(1)} %pad_maximum_fusion.5.refs_2_), channel_id=1, source_target_pairs={{0,6},{2,4},{4,2},{6,0},{8,14},{10,12},{12,10},{14,8},{16,22},{18,... | collective-permute-start | bytes 638984 | tf_op jit(solution)/shard_map/ppermute | solution.py:47
  18.8 6.3 %collective-permute-done.11 = bf16[9,16,512]{2,1,0:T(8,128)(2,1)S(1)} collective-permute-done((bf16[9,16,512]{2,1,0:T(8,128)(2,1)S(1)}, bf16[9,16,512]{2,1,0:T(8,128)(2,1)S(1)}, u32[]{:S(2)}, u32[]{:S(2)}) %collective-permute-start.11) | collective-permute-done | bytes 147488 | tf_op jit(solution)/shard_map/ppermute | solution.py:43
  26.6 1.6 collective-permute-start.14
  29.9 3.7 %masks.1.refs_1_ = f32[3,512,512]{2,1,0:T(8,128)} custom-call(s32[1,1024]{1,0:T(1,128)} %doc_row.1, s32[1024,1]{1,0:T(8,128)} %copy.18.doc_col, s32[4,512]{1,0:T(4,128)} %bitcast.74), custom_call_target="tpu_custom_call" | custom-call | tf_op jit(solution)/shard_map/masks/pallas_call | solution.py:898
  34.8 2.2 %collective-permute-done.13 = bf16[4,5,16,512]{3,2,1,0:T(8,128)(2,1)S(1)} collective-permute-done((bf16[4,5,16,512]{3,2,1,0:T(8,128)(2,1)S(1)}, bf16[4,5,16,512]{3,2,1,0:T(8,128)(2,1)S(1)}, u32[]{:S(2)}, u32[]{:S(2)}) %collective-permute-start.13) | collective-permute-done | bytes 327712 | tf_op jit(solution)/shard_map/ppermute | solution.py:47
  38.3 1.6 collective-permute-start.15
  40.6 16.7 %attention.1 = (bf16[512,1664]{1,0:T(8,128)(2,1)}, bf16[1024,512]{1,0:T(8,128)(2,1)}, bf16[1536,1024]{1,0:T(8,128)(2,1)}, bf16[512,1024]{1,0:T(8,128)(2,1)}, f32...) custom-call(bf16[1024,512]{1,0:T(8,128)(2,1)} %refs_0_.5, ...), custom_call_target="tpu_custom_call" | custom-call | flops 17999998976 | bytes 40000000 | tf_op jit(solution)/shard_map/attention/pallas_call | solution.py:319
  58.1 3.1 %collective-permute-done.19.refs_10_ = bf16[8,4,16,512]{3,2,1,0:T(8,128)(2,1)S(1)} collective-permute-done((bf16[8,4,16,512]{3,2,1,0:T(8,128)(2,1)}, bf16[8,4,16,512]{3,2,1,0:T(8,128)(2,1)S(1)}, u32[]{:S(2)}, u32[]{:S(2)}) %collective-permute-start.19) | collective-permute-done | bytes 524320 | tf_op jit(solution)/shard_map/ppermute | solution.py:51
  63.0 29.3 %feed_forward.1 = (bf16[1024,512]{1,0:T(8,128)(2,1)}, f32[1024,512]{1,0:T(8,128)}, bf16[512,1024]{1,0:T(8,128)(2,1)}, f32[1,512]{1,0:T(1,128)}, bf16[16,5,16,512...) custom-call(bf16[1024,512]{1,0:T(8,128)(2,1)} %refs_0_.5, ...), custom_call_target="tpu_custom_call" | custom-call | flops 24999999488 | bytes 25000000 | tf_op jit(solution)/shard_map/feed_forward/pallas_call | solution.py:566
  92.9 10.5 %attention_back.2 = (bf16[3,256,1024]{2,1,0:T(8,128)(2,1)}, f32[2,2,1024]{2,1,0:T(2,128)}, f32[512,128]{1,0:T(8,128)}, bf16[3,512,256]{2,1,0:T(8,128)(2,1)}) custom-call(f32[8,1024]{1,0:T(8,128)} %get-tuple-element.53.refs_0_, bf16[512,1664]{1,0:T(8,128)(2,1)} %get-tuple-element.58.refs_1_.refs_3_, bf16[512,1024]{1,0:T(8,128)(2,1)} %get-tuple-element.59.refs_2_, ...), custom_call_target="tpu_custom_call" | custom-call | flops 11000000512 | bytes 20000000 | tf_op jit(solution)/shard_map/attention_back/pallas_call | solution.py:788
  105.4 1.8 %add_convert_fusion = (bf16[8,5,16,512]{3,2,1,0:T(8,128)(2,1)}, f32[8,5,16,512]{3,2,1,0:T(8,128)}) fusion(bf16[16,5,16,512]{3,2,1,0:T(8,128)(2,1)S(1)} %collective-permute-done.21, bf16[16,5,16,512]{3,2,1,0:T(8,128)(2,1)S(1)} %copy-done.2), kind=kLoop, calls=%fused_computation.3 | loop fusion | flops 2293760 | bytes 4587520 | tf_op jit(solution)/shard_map/convert_element_type | solution.py:961
  108.1 11.7 %attention_back.3 = (bf16[3,256,1024]{2,1,0:T(8,128)(2,1)}, f32[2,2,1024]{2,1,0:T(2,128)}, bf16[16,16,1664]{2,1,0:T(8,128)(2,1)}, bf16[16,16,1664]{2,1,0:T(8,128)(2,1)}) custom-call(f32[8,1024]{1,0:T(8,128)} %get-tuple-element.53.refs_0_, bf16[512,1664]{1,0:T(8,128)(2,1)} %get-tuple-element.58.refs_1_.refs_3_, bf16[512,1024]{1,0:T(8,128)(2,1)} %get-tuple-element.59.refs_2_, ...), custom_call_target="tpu_custom_call" | custom-call | flops 11000000512 | bytes 20000000 | tf_op jit(solution)/shard_map/attention_back/pallas_call | solution.py:788
  119.9 4.0 %collective-permute-done.24 = bf16[8,5,16,512]{3,2,1,0:T(8,128)(2,1)S(1)} collective-permute-done((bf16[8,5,16,512]{3,2,1,0:T(8,128)(2,1)}, bf16[8,5,16,512]{3,2,1,0:T(8,128)(2,1)S(1)}, u32[]{:S(2)}, u32[]{:S(2)}) %collective-permute-start.24) | collective-permute-done | bytes 655392 | tf_op jit(solution)/shard_map/ppermute | solution.py:47
  123.9 1.9 %fusion.4.refs_12_ = bf16[4,4,16,512]{3,2,1,0:T(8,128)(2,1)} fusion(f32[8,4,16,512]{3,2,1,0:T(8,128)S(1)} %copy-done.1, bf16[8,4,16,512]{3,2,1,0:T(8,128)(2,1)} %collective-permute-done.25), kind=kLoop, calls=%fused_computation.17 | loop fusion | flops 393216 | bytes 1048576 | tf_op jit(solution)/shard_map/convert_element_type | solution.py:987
  132.7 7.1 %input_back.1 = bf16[1024,512]{1,0:T(8,128)(2,1)} custom-call(bf16[1024,512]{1,0:T(8,128)(2,1)} %refs_0_.5, f32[1024,512]{1,0:T(8,128)} %get-tuple-element.57.refs_1_, f32[2,512]{1,0:T(2,128)} %get-tuple-element.52.refs_3_.refs_11_.refs_2_, bf16[512,1664]{1,0:T(8,128)(2,1)} %get-tuple-element.58.refs_1_.refs_3_, ...), custom_call_target="tpu_custom_call" | custom-call | flops 5000000000 | bytes 9000000 | tf_op jit(solution)/shard_map/input_back/pallas_call | solution.py:858
  142.7 1.9 %collective-permute-done.26 = bf16[4,16,1664]{2,1,0:T(8,128)(2,1)} collective-permute-done((bf16[4,16,1664]{2,1,0:T(8,128)(2,1)}, bf16[4,16,1664]{2,1,0:T(8,128)(2,1)}, u32[]{:S(2)}, u32[]{:S(2)}) %collective-permute-start.26) | collective-permute-done | bytes 213024 | tf_op jit(solution)/shard_map/ppermute | solution.py:47
  145.9 2.0 %collective-permute-start.29 = (bf16[16,1664]{1,0:T(8,128)(2,1)S(1)}, bf16[16,1664]{1,0:T(8,128)(2,1)S(1)}, u32[]{:S(2)}, u32[]{:S(2)}) collective-permute-start(bf16[16,1664]{1,0:T(8,128)(2,1)S(1)} %get-tuple-element.100), channel_id=1, source_target_pairs={{0,8},{2,10},{4,12},{6,14},{8,16},{10,18},{12,20},{14,22},{16,24},... | collective-permute-start | bytes 159752 | tf_op jit(solution)/shard_map/ppermute | solution.py:43
  147.9 1.9 %collective-permute-start.31 = (bf16[16,1664]{1,0:T(8,128)(2,1)S(1)}, bf16[16,1664]{1,0:T(8,128)(2,1)S(1)}, u32[]{:S(2)}, u32[]{:S(2)}) collective-permute-start(bf16[16,1664]{1,0:T(8,128)(2,1)S(1)} %get-tuple-element.101), channel_id=1, source_target_pairs={{0,24},{2,26},{4,28},{6,30},{8,0},{10,2},{12,4},{14,6},{16,8},{18,... | collective-permute-start | bytes 159752 | tf_op jit(solution)/shard_map/ppermute | solution.py:43
  150.4 3.3 %collective-permute-start.36 = (bf16[9,16,512]{2,1,0:T(8,128)(2,1)S(1)}, bf16[9,16,512]{2,1,0:T(8,128)(2,1)S(1)}, u32[]{:S(2)}, u32[]{:S(2)}) collective-permute-start(bf16[9,16,512]{2,1,0:T(8,128)(2,1)S(1)} %get-tuple-element.96), channel_id=1, source_target_pairs={{0,24},{2,26},{4,28},{6,30},{8,0},{10,2},{12,4},{14,6},{16,8},{18,... | collective-permute-start | bytes 442376 | tf_op jit(solution)/shard_map/ppermute | solution.py:43
  154.8 1.6 collective-permute-done.30
  159.2 6.9 %collective-permute-done.35 = bf16[9,16,512]{2,1,0:T(8,128)(2,1)S(1)} collective-permute-done((bf16[9,16,512]{2,1,0:T(8,128)(2,1)S(1)}, bf16[9,16,512]{2,1,0:T(8,128)(2,1)S(1)}, u32[]{:S(2)}, u32[]{:S(2)}) %collective-permute-start.35) | collective-permute-done | bytes 147488 | tf_op jit(solution)/shard_map/ppermute | solution.py:43
  (141 shorter events, 37.1 us)
Async XLA Ops:
  3.0 12.6 %collective-permute-start.2 = (bf16[16,1664]{1,0:T(8,128)(2,1)S(1)}, bf16[16,1664]{1,0:T(8,128)(2,1)S(1)}, u32[]{:S(2)}, u32[]{:S(2)}) collective-permute-start(bf16[16,1664]{1,0:T(8,128)(2,1)S(1)} %concatenate.15), channel_id=1, source_target_pairs={{0,8},{2,10},{4,12},{6,14},{8,16},{10,18},{12,20},{14,22},{16,24},... | collective-permute-start | bytes 159752 | tf_op jit(solution)/shard_map/ppermute | solution.py:43
  6.1 9.6 %collective-permute-start.1 = (bf16[16,1664]{1,0:T(8,128)(2,1)S(1)}, bf16[16,1664]{1,0:T(8,128)(2,1)S(1)}, u32[]{:S(2)}, u32[]{:S(2)}) collective-permute-start(bf16[16,1664]{1,0:T(8,128)(2,1)S(1)} %concatenate.15), channel_id=1, source_target_pairs={{0,16},{2,18},{4,20},{6,22},{8,24},{10,26},{12,28},{14,30},{16,0},... | collective-permute-start | bytes 159752 | tf_op jit(solution)/shard_map/ppermute | solution.py:43
  12.6 12.5 %collective-permute-start.11 = (bf16[9,16,512]{2,1,0:T(8,128)(2,1)S(1)}, bf16[9,16,512]{2,1,0:T(8,128)(2,1)S(1)}, u32[]{:S(2)}, u32[]{:S(2)}) collective-permute-start(bf16[9,16,512]{2,1,0:T(8,128)(2,1)S(1)} %get-tuple-element.104), channel_id=1, source_target_pairs={{0,16},{2,18},{4,20},{6,22},{8,24},{10,26},{12,28},{14,30},{16,0},... | collective-permute-start | bytes 442376 | tf_op jit(solution)/shard_map/ppermute | solution.py:43
  12.8 13.8 %collective-permute-start.10 = (bf16[9,16,512]{2,1,0:T(8,128)(2,1)S(1)}, bf16[9,16,512]{2,1,0:T(8,128)(2,1)S(1)}, u32[]{:S(2)}, u32[]{:S(2)}) collective-permute-start(bf16[9,16,512]{2,1,0:T(8,128)(2,1)S(1)} %get-tuple-element.104), channel_id=1, source_target_pairs={{0,24},{2,26},{4,28},{6,30},{8,0},{10,2},{12,4},{14,6},{16,8},{18,... | collective-permute-start | bytes 442376 | tf_op jit(solution)/shard_map/ppermute | solution.py:43
  15.7 10.9 %collective-permute-start.12 = (bf16[9,16,512]{2,1,0:T(8,128)(2,1)S(1)}, bf16[9,16,512]{2,1,0:T(8,128)(2,1)S(1)}, u32[]{:S(2)}, u32[]{:S(2)}) collective-permute-start(bf16[9,16,512]{2,1,0:T(8,128)(2,1)S(1)} %get-tuple-element.104), channel_id=1, source_target_pairs={{0,8},{2,10},{4,12},{6,14},{8,16},{10,18},{12,20},{14,22},{16,24},... | collective-permute-start | bytes 442376 | tf_op jit(solution)/shard_map/ppermute | solution.py:43
  15.7 17.9 %collective-permute-start.5 = (bf16[4,16,1664]{2,1,0:T(8,128)(2,1)S(1)}, bf16[4,16,1664]{2,1,0:T(8,128)(2,1)S(1)}, u32[]{:S(2)}, u32[]{:S(2)}) collective-permute-start(bf16[4,16,1664]{2,1,0:T(8,128)(2,1)S(1)} %pad_maximum_fusion.5.refs_2_), channel_id=1, source_target_pairs={{0,6},{2,4},{4,2},{6,0},{8,14},{10,12},{12,10},{14,8},{16,22},{18,... | collective-permute-start | bytes 638984 | tf_op jit(solution)/shard_map/ppermute | solution.py:47
  18.3 15.4 %collective-permute-start.4 = (bf16[4,16,1664]{2,1,0:T(8,128)(2,1)S(1)}, bf16[4,16,1664]{2,1,0:T(8,128)(2,1)S(1)}, u32[]{:S(2)}, u32[]{:S(2)}) collective-permute-start(bf16[4,16,1664]{2,1,0:T(8,128)(2,1)S(1)} %pad_maximum_fusion.5.refs_2_), channel_id=1, source_target_pairs={{0,4},{2,6},{4,0},{6,2},{8,12},{10,14},{12,8},{14,10},{16,20},{18,... | collective-permute-start | bytes 638984 | tf_op jit(solution)/shard_map/ppermute | solution.py:47
  25.1 8.6 %collective-permute-start.3 = (bf16[4,16,1664]{2,1,0:T(8,128)(2,1)S(1)}, bf16[4,16,1664]{2,1,0:T(8,128)(2,1)S(1)}, u32[]{:S(2)}, u32[]{:S(2)}) collective-permute-start(bf16[4,16,1664]{2,1,0:T(8,128)(2,1)S(1)} %pad_maximum_fusion.5.refs_2_), channel_id=1, source_target_pairs={{0,2},{2,0},{4,6},{6,4},{8,10},{10,8},{12,14},{14,12},{16,18},{18,... | collective-permute-start | bytes 638984 | tf_op jit(solution)/shard_map/ppermute | solution.py:47
  28.3 8.8 %collective-permute-start.13 = (bf16[4,5,16,512]{3,2,1,0:T(8,128)(2,1)S(1)}, bf16[4,5,16,512]{3,2,1,0:T(8,128)(2,1)S(1)}, u32[]{:S(2)}, u32[]{:S(2)}) collective-permute-start(bf16[4,5,16,512]{3,2,1,0:T(8,128)(2,1)S(1)} %slice.166), channel_id=1, source_target_pairs={{0,2},{2,0},{4,6},{6,4},{8,10},{10,8},{12,14},{14,12},{16,18},{18,... | collective-permute-start | bytes 983048 | tf_op jit(solution)/shard_map/ppermute | solution.py:47
  37.1 20.2 %collective-permute-start.16 = (bf16[8,4,16,512]{3,2,1,0:T(8,128)(2,1)S(1)}, bf16[8,4,16,512]{3,2,1,0:T(8,128)(2,1)S(1)}, u32[]{:S(2)}, u32[]{:S(2)}) collective-permute-start(bf16[8,4,16,512]{3,2,1,0:T(8,128)(2,1)S(1)} %pad_maximum_fusion.3.refs_11_.refs_8_), channel_id=1, source_target_pairs={{0,2},{2,0},{4,6},{6,4},{8,10},{10,8},{12,14},{14,12},{16,18},{18,... | collective-permute-start | bytes 1572872 | tf_op jit(solution)/shard_map/ppermute | solution.py:47
  38.2 23.0 %collective-permute-start.17 = (bf16[8,5,16,512]{3,2,1,0:T(8,128)(2,1)S(1)}, bf16[8,5,16,512]{3,2,1,0:T(8,128)(2,1)S(1)}, u32[]{:S(2)}, u32[]{:S(2)}) collective-permute-start(bf16[8,5,16,512]{3,2,1,0:T(8,128)(2,1)S(1)} %pad_maximum_fusion.1.refs_10_.refs_4_), channel_id=1, source_target_pairs={{0,1},{1,0},{2,3},{3,2},{4,5},{5,4},{6,7},{7,6},{8,9},{9,8},{10,11... | collective-permute-start | bytes 1966088 | tf_op jit(solution)/shard_map/ppermute | solution.py:51
  38.3 19.1 %collective-permute-start.15 = (bf16[8,5,16,512]{3,2,1,0:T(8,128)(2,1)S(1)}, bf16[8,5,16,512]{3,2,1,0:T(8,128)(2,1)S(1)}, u32[]{:S(2)}, u32[]{:S(2)}) collective-permute-start(bf16[8,5,16,512]{3,2,1,0:T(8,128)(2,1)S(1)} %pad_maximum_fusion.1.refs_10_.refs_4_), channel_id=1, source_target_pairs={{0,4},{2,6},{4,0},{6,2},{8,12},{10,14},{12,8},{14,10},{16,20},{18,... | collective-permute-start | bytes 1966088 | tf_op jit(solution)/shard_map/ppermute | solution.py:47
  92.3 11.1 %collective-permute-start.21 = (bf16[16,5,16,512]{3,2,1,0:T(8,128)(2,1)}, bf16[16,5,16,512]{3,2,1,0:T(8,128)(2,1)S(1)}, u32[]{:S(2)}, u32[]{:S(2)}) collective-permute-start(bf16[16,5,16,512]{3,2,1,0:T(8,128)(2,1)} %get-tuple-element.73), channel_id=1, source_target_pairs={{0,1},{1,0},{2,3},{3,2},{4,5},{5,4},{6,7},{7,6},{8,9},{9,8},{10,11... | collective-permute-start | bytes 3932168 | tf_op jit(solution)/shard_map/ppermute | solution.py:51
  92.5 10.8 %collective-permute-start.22 = (bf16[16,4,16,512]{3,2,1,0:T(8,128)(2,1)}, bf16[16,4,16,512]{3,2,1,0:T(8,128)(2,1)S(1)}, u32[]{:S(2)}, u32[]{:S(2)}) collective-permute-start(bf16[16,4,16,512]{3,2,1,0:T(8,128)(2,1)} %get-tuple-element.74), channel_id=1, source_target_pairs={{0,1},{1,0},{2,3},{3,2},{4,5},{5,4},{6,7},{7,6},{8,9},{9,8},{10,11... | collective-permute-start | bytes 3145736 | tf_op jit(solution)/shard_map/ppermute | solution.py:51
  104.9 15.0 %collective-permute-start.25 = (bf16[8,4,16,512]{3,2,1,0:T(8,128)(2,1)}, bf16[8,4,16,512]{3,2,1,0:T(8,128)(2,1)}, u32[]{:S(2)}, u32[]{:S(2)}) collective-permute-start(bf16[8,4,16,512]{3,2,1,0:T(8,128)(2,1)} %get-tuple-element.90.refs_19_), channel_id=1, source_target_pairs={{0,2},{2,0},{4,6},{6,4},{8,10},{10,8},{12,14},{14,12},{16,18},{18,... | collective-permute-start | bytes 1572872 | tf_op jit(solution)/shard_map/ppermute | solution.py:47
  107.2 16.8 %collective-permute-start.24 = (bf16[8,5,16,512]{3,2,1,0:T(8,128)(2,1)}, bf16[8,5,16,512]{3,2,1,0:T(8,128)(2,1)S(1)}, u32[]{:S(2)}, u32[]{:S(2)}) collective-permute-start(bf16[8,5,16,512]{3,2,1,0:T(8,128)(2,1)} %get-tuple-element.88.refs_17_), channel_id=1, source_target_pairs={{0,4},{2,6},{4,0},{6,2},{8,12},{10,14},{12,8},{14,10},{16,20},{18,... | collective-permute-start | bytes 1966088 | tf_op jit(solution)/shard_map/ppermute | solution.py:47
  125.8 13.9 %collective-permute-start.33 = (bf16[4,4,16,512]{3,2,1,0:T(8,128)(2,1)}, bf16[4,4,16,512]{3,2,1,0:T(8,128)(2,1)}, u32[]{:S(2)}, u32[]{:S(2)}) collective-permute-start(bf16[4,4,16,512]{3,2,1,0:T(8,128)(2,1)} %fusion.4.refs_12_), channel_id=1, source_target_pairs={{0,4},{2,6},{4,0},{6,2},{8,12},{10,14},{12,8},{14,10},{16,20},{18,... | collective-permute-start | bytes 786440 | tf_op jit(solution)/shard_map/ppermute | solution.py:47
  126.9 12.9 %collective-permute-start.32 = (bf16[4,5,16,512]{3,2,1,0:T(8,128)(2,1)S(1)}, bf16[4,5,16,512]{3,2,1,0:T(8,128)(2,1)S(1)}, u32[]{:S(2)}, u32[]{:S(2)}) collective-permute-start(bf16[4,5,16,512]{3,2,1,0:T(8,128)(2,1)S(1)} %fusion.2.refs_11_), channel_id=1, source_target_pairs={{0,2},{2,0},{4,6},{6,4},{8,10},{10,8},{12,14},{14,12},{16,18},{18,... | collective-permute-start | bytes 983048 | tf_op jit(solution)/shard_map/ppermute | solution.py:47
  129.2 13.5 %collective-permute-start.28 = (bf16[4,16,1664]{2,1,0:T(8,128)(2,1)}, bf16[4,16,1664]{2,1,0:T(8,128)(2,1)S(1)}, u32[]{:S(2)}, u32[]{:S(2)}) collective-permute-start(bf16[4,16,1664]{2,1,0:T(8,128)(2,1)} %get-tuple-element.92.refs_10_), channel_id=1, source_target_pairs={{0,6},{2,4},{4,2},{6,0},{8,14},{10,12},{12,10},{14,8},{16,22},{18,... | collective-permute-start | bytes 638984 | tf_op jit(solution)/shard_map/ppermute | solution.py:47
  130.7 12.0 %collective-permute-start.27 = (bf16[4,16,1664]{2,1,0:T(8,128)(2,1)}, bf16[4,16,1664]{2,1,0:T(8,128)(2,1)S(1)}, u32[]{:S(2)}, u32[]{:S(2)}) collective-permute-start(bf16[4,16,1664]{2,1,0:T(8,128)(2,1)} %get-tuple-element.93.refs_9_), channel_id=1, source_target_pairs={{0,4},{2,6},{4,0},{6,2},{8,12},{10,14},{12,8},{14,10},{16,20},{18,... | collective-permute-start | bytes 638984 | tf_op jit(solution)/shard_map/ppermute | solution.py:47
  131.6 13.0 %collective-permute-start.26 = (bf16[4,16,1664]{2,1,0:T(8,128)(2,1)}, bf16[4,16,1664]{2,1,0:T(8,128)(2,1)}, u32[]{:S(2)}, u32[]{:S(2)}) collective-permute-start(bf16[4,16,1664]{2,1,0:T(8,128)(2,1)} %get-tuple-element.94.refs_8_), channel_id=1, source_target_pairs={{0,2},{2,0},{4,6},{6,4},{8,10},{10,8},{12,14},{14,12},{16,18},{18,... | collective-permute-start | bytes 638984 | tf_op jit(solution)/shard_map/ppermute | solution.py:47
  149.8 8.7 %collective-permute-start.34 = (bf16[9,16,512]{2,1,0:T(8,128)(2,1)S(1)}, bf16[9,16,512]{2,1,0:T(8,128)(2,1)S(1)}, u32[]{:S(2)}, u32[]{:S(2)}) collective-permute-start(bf16[9,16,512]{2,1,0:T(8,128)(2,1)S(1)} %get-tuple-element.95), channel_id=1, source_target_pairs={{0,8},{2,10},{4,12},{6,14},{8,16},{10,18},{12,20},{14,22},{16,24},... | collective-permute-start | bytes 442376 | tf_op jit(solution)/shard_map/ppermute | solution.py:43
  150.4 8.7 %collective-permute-start.36 = (bf16[9,16,512]{2,1,0:T(8,128)(2,1)S(1)}, bf16[9,16,512]{2,1,0:T(8,128)(2,1)S(1)}, u32[]{:S(2)}, u32[]{:S(2)}) collective-permute-start(bf16[9,16,512]{2,1,0:T(8,128)(2,1)S(1)} %get-tuple-element.96), channel_id=1, source_target_pairs={{0,24},{2,26},{4,28},{6,30},{8,0},{10,2},{12,4},{14,6},{16,8},{18,... | collective-permute-start | bytes 442376 | tf_op jit(solution)/shard_map/ppermute | solution.py:43
  153.7 12.4 %collective-permute-start.35 = (bf16[9,16,512]{2,1,0:T(8,128)(2,1)S(1)}, bf16[9,16,512]{2,1,0:T(8,128)(2,1)S(1)}, u32[]{:S(2)}, u32[]{:S(2)}) collective-permute-start(bf16[9,16,512]{2,1,0:T(8,128)(2,1)S(1)} %get-tuple-element.97), channel_id=1, source_target_pairs={{0,16},{2,18},{4,20},{6,22},{8,24},{10,26},{12,28},{14,30},{16,0},... | collective-permute-start | bytes 442376 | tf_op jit(solution)/shard_map/ppermute | solution.py:43
  (35 other events, 206.6 us)

commit v3 on v2

--- a/solution.py
+++ b/solution.py
@@ -18,13 +18,13 @@
 GCOL = 8
 GLEN = 2 * D // PIECES
 NEG = -1e30
+EARLY = 1
 BF = jnp.bfloat16
 F32 = jnp.float32
 AXES = ("dp", "fsdp")
 NT = (((1,), (1,)), ((), ()))
 TN = (((0,), (0,)), ((), ()))
 ANY = pl.BlockSpec(memory_space=pl.ANY)
-VLIMIT = 60 * 1024 * 1024
 
 
 def mm(a, b):
@@ -158,8 +158,8 @@
 PROB_ROWS = 2 * 768 + 1024
 
 
-def params():
-    return pltpu.CompilerParams(vmem_limit_bytes=VLIMIT)
+def params(mib):
+    return pltpu.CompilerParams(vmem_limit_bytes=mib * 1024 * 1024)
 
 
 def shape(*dims, dtype=BF):
@@ -357,7 +357,7 @@
             pltpu.SemaphoreType.DMA((3,)),
             pltpu.SemaphoreType.DMA((4,)),
         ],
-        compiler_params=params(),
+        compiler_params=params(60),
         cost_estimate=pl.CostEstimate(
             flops=18_000_000_000, bytes_accessed=40_000_000, transcendentals=6_000_000
         ),
@@ -600,7 +600,7 @@
             pltpu.SemaphoreType.DMA((6,)),
             pltpu.SemaphoreType.DMA((6,)),
         ],
-        compiler_params=params(),
+        compiler_params=params(60),
         cost_estimate=pl.CostEstimate(
             flops=25_000_000_000, bytes_accessed=25_000_000, transcendentals=2_000_000
         ),
@@ -608,12 +608,14 @@
     )(x, cot, mixed_t, gains, *parts_u, *parts_d)
 
 
-def attention_back_kernel(first, last, owner, count_o, *refs):
+def attention_back_kernel(first, pairs, spans, owner, count_o, *refs):
     (gatet, w_hbm, hidt_hbm, probs, local_t, mem_t, inv_sums, dmix_t, qt, kt, vtok) = refs[:11]
     refs = refs[11:]
+    last = len(spans) > 0
     if last:
-        gains, dgain_two, before, gates_before, grad_before = refs[:5]
-        refs = refs[5:]
+        gains, dgain_two = refs[:2]
+        befores = [refs[2 + 3 * i : 5 + 3 * i] for i in range(len(spans))]
+        refs = refs[2 + 3 * len(spans) :]
     else:
         count_o = 1
     dqkvt, d_gates, *refs = refs
@@ -621,22 +623,28 @@
         weighted = refs[0]
         refs = refs[1:]
     grads = refs[:count_o]
-    w, hidt, scratch, gate_rows, g_ext, in_sem, out_sem = refs[count_o:]
+    w, hidt, scratch, gate_rows, g_ext, d_probs, d_scores, in_sem, out_sem = refs[count_o:]
     pair = pl.program_id(0)
     per = PIECES // count_o
 
-    def before_columns(third):
-        return pltpu.make_async_copy(
-            grad_before.at[third], g_ext.at[:, pl.ds(third * D, 256)], in_sem.at[2]
-        )
+    def before_columns():
+        return [
+            pltpu.make_async_copy(
+                before[2].at[third],
+                g_ext.at[:, pl.ds(third * D + at * 128, count * 128)],
+                in_sem.at[2],
+            )
+            for third in range(3)
+            for (at, count), before in zip(spans, befores)
+        ]
 
     @pl.when(pair == 0)
     def _():
         pltpu.make_async_copy(hidt_hbm, hidt, in_sem.at[0]).start()
         pltpu.make_async_copy(w_hbm, w, in_sem.at[1]).start()
         if last:
-            for third in range(3):
-                before_columns(third).start()
+            for copy in before_columns():
+                copy.start()
 
     ups = {}
     dots = {}
@@ -673,38 +681,56 @@
     def add(key, value):
         sums_of[key] = value if key not in sums_of else sums_of[key] + value
 
-    def begin(hh, seg, ib):
+    def begin(slot, hh, seg, ib):
         key_first, key_count, column, base = spot(seg, ib)
-        return mm(vtok[key_first : key_first + key_count, :], head_half(ups[hh, seg, ib], hh))
-
-    def middle(d_prob, hh, seg, ib):
+        d_probs[slot, 0:key_count, :] = mm(
+            vtok[key_first : key_first + key_count, :], head_half(ups[hh, seg, ib], hh)
+        )
+
+    def middle(slot, part, hh, seg, ib):
         key_first, key_count, column, base = spot(seg, ib)
-        expo = probs[0, hh, base : base + key_count, :]
-        return (expo.astype(F32) * (d_prob - dots[hh, seg, ib])).astype(BF), expo
-
-    def close(d_score, expo, hh, seg, ib):
+        size = key_count // 4
+        for step in range(size // 64):
+            at = part * size + 64 * step
+            expo = probs[0, hh, base + at : base + at + 64, :].astype(F32)
+            d_scores[slot, at : at + 64, :] = (
+                expo * (d_probs[slot, at : at + 64, :] - dots[hh, seg, ib])
+            ).astype(BF)
+
+    def close(slot, part, hh, seg, ib):
         key_first, key_count, column, base = spot(seg, ib)
         rows = slice(hh * HD, (hh + 1) * HD)
-        add((0, hh, column // 256), mm(kt[rows, key_first : key_first + key_count], d_score))
-        key_term = mm_nt(qt[rows, column : column + 256], d_score)
-        value_term = mm_nt(ups[hh, seg, ib], expo)
-        for part in range(key_count // 256):
-            place = key_first // 256 + part
-            add((1, hh, place), key_term[:, 256 * part : 256 * part + 256])
-            add((2, hh, place), value_term[:, 256 * part : 256 * part + 256])
+        if part == 0:
+            value = mm(kt[rows, key_first : key_first + key_count], d_scores[slot, 0:key_count, :])
+            add((0, hh, column // 256), value)
+            return
+        if part == 1:
+            value = mm_nt(qt[rows, column : column + 256], d_scores[slot, 0:key_count, :])
+        else:
+            value = mm_nt(ups[hh, seg, ib], probs[0, hh, base : base + key_count, :])
+        for block in range(key_count // 256):
+            place = key_first // 256 + block
+            add((part, hh, place), value[:, 256 * block : 256 * block + 256])
 
     order = [(hh, seg, ib) for seg in (0, 2, 1) for ib in range(2) for hh in range(2)]
-    waiting = begin(*order[0])
-    late = None
-    for i, item in enumerate(order):
-        d_prob = waiting
+    begin(0, *order[0])
+    for i in range(len(order) + 1):
+        if i < len(order):
+            middle(i % 2, 0, *order[i])
+        if i > 0:
+            close((i - 1) % 2, 2, *order[i - 1])
+        if i < len(order):
+            middle(i % 2, 1, *order[i])
+        if i > 0:
+            close((i - 1) % 2, 0, *order[i - 1])
+        if i < len(order):
+            middle(i % 2, 2, *order[i])
+        if i > 0:
+            close((i - 1) % 2, 1, *order[i - 1])
+        if i < len(order):
+            middle(i % 2, 3, *order[i])
         if i + 1 < len(order):
-            waiting = begin(*order[i + 1])
-        d_score, expo = middle(d_prob, *item)
-        if late is not None:
-            close(*late)
-        late = (d_score, expo) + item
-    close(*late)
+            begin((i + 1) % 2, *order[i + 1])
     for (third, hh, place), value in sums_of.items():
         if third == 0:
             value = value * 0.125
@@ -712,7 +738,7 @@
         dqkvt[third, rows, 256 * place : 256 * place + 256] = value.astype(BF)
     scratch[:, block_rows(pair, 128), :] = dqkvt[...]
 
-    @pl.when(pair == 1)
+    @pl.when(pair == pairs - 1)
     def _():
         pltpu.make_async_copy(hidt_hbm, hidt, in_sem.at[0]).wait()
         pltpu.make_async_copy(w_hbm, w, in_sem.at[1]).wait()
@@ -720,28 +746,24 @@
         for third in range(3):
             grad = mm_nt(hidt[...], scratch[third])
             start = third * D + first * 128
-            for part in range(2):
+            for part in range(pairs):
                 columns = slice(start + 128 * part, start + 128 * part + 128)
                 sums = sums + grad[:, 128 * part : 128 * part + 128] * w[:, columns].astype(F32)
             if last:
-                g_ext[:, third * D + 256 : third * D + 512] = grad.astype(BF)
+                g_ext[:, start : start + 128 * pairs] = grad.astype(BF)
             else:
                 g_ext[third] = grad.astype(BF)
         if last:
             d_gate_b = jnp.concatenate(
-                [
-                    gates_before[0],
-                    gates_before[1],
-                    gate_rows[0:4, :],
-                    jnp.zeros((120, SEQ), F32),
-                ],
+                [before[1][i] for before in befores for i in range(before[1].shape[0])]
+                + [gate_rows[0 : 2 * pairs, :], jnp.zeros((120, SEQ), F32)],
                 axis=0,
             ).astype(BF)
             grad = mm_nt(hidt[...], d_gate_b)
             gate_lane = lax.broadcasted_iota(jnp.int32, (D, 128), 1) < H
-            sums = sums + before[...] + jnp.where(
-                gate_lane, grad * w[:, 3 * D :].astype(F32), 0.0
-            )
+            sums = sums + jnp.where(gate_lane, grad * w[:, 3 * D :].astype(F32), 0.0)
+            for before in befores:
+                sums = sums + before[0][...]
             column = jnp.sum(sums, axis=1, keepdims=True)
             g_ext[:, 3 * D :] = (grad + ext_from_gains(column, gains[0:1, :], dgain_two[...])).astype(
                 BF
@@ -751,8 +773,8 @@
             pltpu.make_async_copy(g_ext, grads[0], out_sem).start()
             pltpu.make_async_copy(g_ext, grads[0], out_sem).wait()
         else:
-            for third in range(3):
-                before_columns(third).wait()
+            for copy in before_columns():
+                copy.wait()
             for piece in range(PIECES):
                 pltpu.make_async_copy(
                     g_ext.at[block_rows(owner(piece), ROWS), :],
@@ -763,15 +785,17 @@
 
 
 def attention_back(
-    first, gatet, w, hidt, saved, dmix_t, qkvt, vtok, owner, count_o, extra=(), deps=()
+    first, pairs, gatet, w, hidt, saved, dmix_t, qkvt, vtok, owner, count_o, extra=(), befores=(), deps=()
 ):
     last = len(extra) > 0
+    spans = [span for span, *_ in befores]
+    extra = (*extra, *(array for _, *arrays in befores for array in arrays))
     const2 = lambda p: (0, 0)
     count_in = 11 + len(extra)
 
     def body(*refs):
         attention_back_kernel(
-            first, last, owner, count_o, *refs[:count_in], *refs[count_in + len(deps) :]
+            first, pairs, spans, owner, count_o, *refs[:count_in], *refs[count_in + len(deps) :]
         )
 
     extra_specs = []
@@ -779,15 +803,18 @@
         extra_specs = [
             pl.BlockSpec((2, D), const2),
             pl.BlockSpec((1, D), const2),
-            pl.BlockSpec((D, 128), const2),
-            pl.BlockSpec((2, 2, SEQ), lambda p: (0, 0, 0)),
-            ANY,
         ]
+        for _, count in spans:
+            extra_specs += [
+                pl.BlockSpec((D, 128), const2),
+                pl.BlockSpec((count, 2, SEQ), lambda p: (0, 0, 0)),
+                ANY,
+            ]
     sums_spec = [] if last else [pl.BlockSpec((D, 128), const2)]
     sums_shape = [] if last else [shape(D, 128, dtype=F32)]
     return pl.pallas_call(
         body,
-        grid=(2,),
+        grid=(pairs,),
         in_specs=[
             pl.BlockSpec((H, SEQ), const2),
             ANY,
@@ -809,19 +836,21 @@
         ]
         + sums_spec
         + [ANY] * (count_o if last else 1),
-        out_shape=[shape(3, 256, SEQ), shape(2, 2, SEQ, dtype=F32)]
+        out_shape=[shape(3, 128 * pairs, SEQ), shape(pairs, 2, SEQ, dtype=F32)]
         + sums_shape
-        + ([shape(PIECES // count_o, ROWS, EXT)] * count_o if last else [shape(3, D, 256)]),
+        + ([shape(PIECES // count_o, ROWS, EXT)] * count_o if last else [shape(3, D, 128 * pairs)]),
         scratch_shapes=[
             pltpu.VMEM((D, EXT), BF),
             pltpu.VMEM((D, SEQ), BF),
-            pltpu.VMEM((3, 256, SEQ), BF),
+            pltpu.VMEM((3, 128 * pairs, SEQ), BF),
             pltpu.VMEM((8, SEQ), F32),
-            pltpu.VMEM((D, EXT) if last else (3, D, 256), BF),
+            pltpu.VMEM((D, EXT) if last else (3, D, 128 * pairs), BF),
+            pltpu.VMEM((2, SEG, 256), F32),
+            pltpu.VMEM((2, SEG, 256), BF),
             pltpu.SemaphoreType.DMA((3,)),
             pltpu.SemaphoreType.DMA,
         ],
-        compiler_params=params(),
+        compiler_params=params((60, 24, 0, 24)[first]),
         cost_estimate=pl.CostEstimate(
             flops=11_000_000_000, bytes_accessed=20_000_000, transcendentals=0
         ),
@@ -829,15 +858,15 @@
     )(gatet, w, hidt, *saved, dmix_t, qkvt, qkvt, vtok, *extra, *deps)
 
 
-def input_back_kernel(x, d_resid, gains, w, da, db, gates_a, gates_b, grad_in):
+def input_back_kernel(x, d_resid, gains, w, parts, gates, grad_in):
     d_gate = jnp.concatenate(
-        [gates_a[0], gates_a[1], gates_b[0], gates_b[1], jnp.zeros((120, 256), F32)], axis=0
+        [gate[i] for gate in gates for i in range(gate.shape[0])] + [jnp.zeros((120, 256), F32)],
+        axis=0,
     ).astype(BF)
     d_hid = mm(w[:, 3 * D :], d_gate)
     for third in range(3):
-        start = third * D
-        d_hid = d_hid + mm(w[:, start : start + 256], da[third])
-        d_hid = d_hid + mm(w[:, start + 256 : start + 512], db[third])
+        rows = jnp.concatenate([part[third] for part in parts], axis=0)
+        d_hid = d_hid + mm(w[:, third * D : third * D + D], rows)
     d_hid = d_hid.T
     xf = x[...].astype(F32)
     factor = lax.rsqrt(jnp.mean(xf * xf, axis=1, keepdims=True) + 1e-06)
@@ -848,9 +877,11 @@
     ).astype(BF)
 
 
-def input_back(x, d_resid, gains, w, da, db, gates_a, gates_b, deps=()):
+def input_back(x, d_resid, gains, w, parts, gates, deps=()):
+    count = len(parts)
+
     def body(*refs):
-        input_back_kernel(*refs[:8], refs[-1])
+        input_back_kernel(*refs[:4], refs[4 : 4 + count], refs[4 + count : 4 + 2 * count], refs[-1])
 
     const2 = lambda i: (0, 0)
     rows = lambda i: (i, 0)
@@ -863,20 +894,18 @@
             pl.BlockSpec((256, D), rows),
             pl.BlockSpec((2, D), const2),
             pl.BlockSpec((D, EXT), const2),
-            pl.BlockSpec((3, 256, 256), across),
-            pl.BlockSpec((3, 256, 256), across),
-            pl.BlockSpec((2, 2, 256), across),
-            pl.BlockSpec((2, 2, 256), across),
         ]
+        + [pl.BlockSpec((3, part.shape[1], 256), across) for part in parts]
+        + [pl.BlockSpec((gate.shape[0], 2, 256), across) for gate in gates]
         + [ANY] * len(deps),
         out_specs=pl.BlockSpec((256, D), rows),
         out_shape=shape(SEQ, D),
-        compiler_params=params(),
+        compiler_params=params(20),
         cost_estimate=pl.CostEstimate(
             flops=5_000_000_000, bytes_accessed=9_000_000, transcendentals=0
         ),
         name="input_back",
-    )(x, d_resid, gains, w, da, db, gates_a, gates_b, *deps)
+    )(x, d_resid, gains, w, *parts, *gates, *deps)
 
 
 def ext_rows(qkv, gate, gains):
@@ -903,7 +932,6 @@
     if split:
         gains_rows = jnp.broadcast_to(norm_gains.reshape(1, GLEN), (ROWS, GLEN))
         shard_a = ext_rows(qkv_flat.reshape(ROWS, 3 * D), gate_flat.reshape(ROWS, H), gains_rows)
-        z_a = gather_z(shard_a)
         shard_f = jnp.concatenate(
             [
                 out_flat.reshape(1, ROWS, D),
@@ -911,6 +939,8 @@
                 down_flat.reshape(4, ROWS, D),
             ]
         )
+        shard_a, shard_f = lax.optimization_barrier((shard_a, shard_f))
+        z_a = gather_z(shard_a)
         plane_a = after(gather_plane(z_a), bias)
         parts_a = gather_core(plane_a)
         z_f = gather_z(shard_f)
@@ -949,13 +979,12 @@
     layer_out, d_resid, dmix_t, dgain_two, *grads_f = ffn(
         inputs, cotangent, mixed_t, gains, parts_u, parts_d, owner_x, owner_y, count_o
     )
-    da, gates_a, weighted, grad_before = attention_back(
-        0, gatet, w_ext, hidt, saved, dmix_t, qkvt, vtok, owner_x, count_o
-    )
+    shared = (gatet, w_ext, hidt, saved, dmix_t, qkvt, vtok, owner_x, count_o)
+    d_one, gates_one, *rest_one = attention_back(0, 1, *shared)
     deps = ()
     if split:
         keep_u, send_u, keep_d, send_d = grads_f
-        got_u, got_d = after((perm_core(send_u), perm_core(send_d)), gates_a)
+        got_u, got_d = after((perm_core(send_u), perm_core(send_d)), gates_one)
         firsts = (
             add(keep_u[:8], got_u[:8]),
             add(keep_u[8:], got_u[8:]).astype(BF),
@@ -963,45 +992,60 @@
             add(keep_d[8:], got_d[8:]).astype(BF),
         )
         deps = firsts
-    db, gates_b, *grads_a = attention_back(
-        2,
-        gatet,
-        w_ext,
-        hidt,
-        saved,
-        dmix_t,
-        qkvt,
-        vtok,
-        owner_x,
-        count_o,
-        (gains, dgain_two, weighted, gates_a, grad_before),
-        deps,
-    )
-    deps = ()
+    d_two, gates_two, *rest_two = attention_back(1, 2, *shared, deps=deps)
     if split:
-        got_u, got_d = after((perm_bit(firsts[1], 2), perm_bit(firsts[3], 1)), gates_b)
+        got_u, got_d = after((perm_bit(firsts[1], 2), perm_bit(firsts[3], 1)), gates_two)
         seconds = (
             add(firsts[0][:4], got_u[:4]),
             add(firsts[0][4:], got_u[4:]).astype(BF),
             add(firsts[2][:4], got_d[:4]),
             add(firsts[2][4:], got_d[4:]).astype(BF),
         )
+        deps = seconds
+    d_three, gates_three, *grads_a = attention_back(
+        3,
+        1,
+        *shared,
+        extra=(gains, dgain_two),
+        befores=(
+            ((0, 1), rest_one[0], gates_one, rest_one[1]),
+            ((1, 2), rest_two[0], gates_two, rest_two[1]),
+        ),
+        deps=deps,
+    )
+    deps = ()
+    if split:
         keep_a, send_a = grads_a
         got_a = perm_core(send_a)
+        got_u, got_d = after((perm_bit(seconds[1], 1), perm_bit(seconds[3], 2)), gates_three)
+        total_f = jnp.concatenate([add(seconds[0], got_u), add(seconds[2], got_d)], axis=1)
+        sends_f = [total_f[k].astype(BF) for k in (1, 2, 3)]
+        (got_a,) = after((got_a,), *sends_f)
         sends_a = [
             add(keep_a[4 * k : 4 * k + 4], got_a[4 * k : 4 * k + 4]).astype(BF) for k in (1, 2, 3)
         ]
-        deps = (*sends_a, seconds[1], seconds[3])
-    grad_input = input_back(inputs, d_resid, gains, w_ext, da, db, gates_a, gates_b, deps)
+        deps = sends_a
+    grad_input = input_back(
+        inputs,
+        d_resid,
+        gains,
+        w_ext,
+        (d_one, d_two, d_three),
+        (gates_one, gates_two, gates_three),
+        deps,
+    )
     if split:
-        got_u, got_d = after((perm_bit(seconds[1], 1), perm_bit(seconds[3], 2)), grad_input)
-        sum_f = add_z(
-            jnp.concatenate([add(seconds[0], got_u), add(seconds[2], got_d)], axis=1)
-        )
+        plane = after([perm_bit(sends_a[k - 1], k) for k in (1, 2, 3)], grad_input)
         total_a = add(keep_a[:4], got_a[:4])
+        for got in plane:
+            total_a = add(total_a, got)
+        sends_z = [total_a[k].astype(BF) for k in (1, 2, 3)]
+        sum_f = total_f[0]
+        for got in after([perm_z(sends_f[k - 1], k) for k in (1, 2, 3)], *sends_z):
+            sum_f = add(sum_f, got)
+        sum_a = total_a[0]
         for k in (1, 2, 3):
-            total_a = add(total_a, perm_bit(sends_a[k - 1], k))
-        sum_a = add_z(total_a)
+            sum_a = add(sum_a, perm_z(sends_z[k - 1], k))
         grad_out = sum_f[0].reshape(-1)
         grad_up = sum_f[1:5].transpose(1, 0, 2).reshape(-1)
         grad_down = sum_f[5:].reshape(-1)

time: 169 us -> 162 us (0.959)
  waiting for transfers between devices: 27.6 us -> 14.5 us
  local copies, waits for them, and re-layouts: 12.5 us -> 20.6 us
  starting transfers between devices: 37.8 us -> 42.5 us
  other arithmetic: 10.3 us -> 5.67 us
  Pallas kernels: 79 us -> 76.6 us
    ppermute x12, waiting for transfers between devices: 15.7 us -> 6.7 us  [perm_z(): return lax.ppermute(v, 'dp', [(i, (i + 4 * shift) % 16) for i in range(16)])]
    unnamed x48 -> x78, local copies, waits for them, and re-layouts: 4.54 us -> 12.7 us
    ppermute x14, waiting for transfers between devices: 8.75 us -> 4.62 us  [perm_bit(): return lax.ppermute(v, 'dp', [(i, i ^ bit) for i in range(16)])]
    ppermute x12, starting transfers between devices: 18.9 us -> 21.6 us  [perm_z(): return lax.ppermute(v, 'dp', [(i, (i + 4 * shift) % 16) for i in range(16)])]
    pallas_call x1, Pallas kernels: 7.12 us -> 4.62 us  [input_back(): pl.pallas_call(body, grid=(4,), in_specs=[pl.BlockSpec((256, D), rows), p...]
    ppermute x14, starting transfers between devices: 16.3 us -> 18.4 us  [perm_bit(): return lax.ppermute(v, 'dp', [(i, i ^ bit) for i in range(16)])]
    add x2 -> x4, other arithmetic: 2.26 us -> 0.28 us  [add(): return keep.astype(F32) + got.astype(F32)]
    convert_element_type x1, other arithmetic: 1.9 us -> 0.16 us  [local(): add(firsts[2][4:], got_d[4:]).astype(BF)]
  transfers between devices with their start and end apart: 37 -> 37, of which waited for: 10 -> 7; matrix products, arithmetic and copies ran while one was open for 8% -> 4% of each run, Pallas kernels for 30% -> 29%
where the time goes in v3:
time: 162 us; the launch traced here: 161 us
  Pallas kernels  76.6 us (47%)
  starting transfers between devices  42.5 us (26%)
  local copies, waits for them, and re-layouts  20.6 us (13%)
  waiting for transfers between devices  14.5 us (9%)
  other arithmetic  5.67 us (4%)
    pallas_call x1, Pallas kernels, ffn(): pl.pallas_call(body, in_specs=[ANY, ANY, ANY, pl.BlockSpec(memory_space=p...  29.3 us
    pallas_call x3, Pallas kernels, attention_back(): pl.pallas_call(body, grid=(pairs,), in_specs=[pl.BlockSpec((H, SEQ), cons...  22.4 us
    ppermute x12, starting transfers between devices, perm_z(): return lax.ppermute(v, 'dp', [(i, (i + 4 * shift) % 16) for i in range(16)])  21.6 us
    ppermute x14, starting transfers between devices, perm_bit(): return lax.ppermute(v, 'dp', [(i, i ^ bit) for i in range(16)])  18.4 us
    pallas_call x1, Pallas kernels, attention(): pl.pallas_call(body, grid=(4,), in_specs=[ANY] * (count_in + len(deps)),...  16.7 us
    unnamed x78, local copies, waits for them, and re-layouts  12.7 us
    ppermute x12, waiting for transfers between devices, perm_z(): return lax.ppermute(v, 'dp', [(i, (i + 4 * shift) % 16) for i in range(16)])  6.7 us
    ppermute x14, waiting for transfers between devices, perm_bit(): return lax.ppermute(v, 'dp', [(i, i ^ bit) for i in range(16)])  4.62 us
  transfers between devices with their start and end apart: 37, of which 7 were waited for; matrix products, arithmetic and copies ran while one was open for 4% of the time, Pallas kernels for 29%

profile of v3, /device:TPU:0, one launch (start us, length us, event | category | flops | bytes accessed | tf_op | source)
XLA Modules:
  0.0 161.3 jit_solution(7061025879105903903)
XLA Ops:
  5.6 3.0 %collective-permute-start.2 = (bf16[16,1664]{1,0:T(8,128)(2,1)S(1)}, bf16[16,1664]{1,0:T(8,128)(2,1)S(1)}, u32[]{:S(2)}, u32[]{:S(2)}) collective-permute-start(bf16[16,1664]{1,0:T(8,128)(2,1)S(1)} %concatenate.15), channel_id=1, source_target_pairs={{0,8},{2,10},{4,12},{6,14},{8,16},{10,18},{12,20},{14,22},{16,24},... | collective-permute-start | bytes 159752 | tf_op jit(solution)/shard_map/ppermute | solution.py:43
  8.6 2.6 %collective-permute-start.1 = (bf16[16,1664]{1,0:T(8,128)(2,1)S(1)}, bf16[16,1664]{1,0:T(8,128)(2,1)S(1)}, u32[]{:S(2)}, u32[]{:S(2)}) collective-permute-start(bf16[16,1664]{1,0:T(8,128)(2,1)S(1)} %concatenate.15), channel_id=1, source_target_pairs={{0,16},{2,18},{4,20},{6,22},{8,24},{10,26},{12,28},{14,30},{16,0},... | collective-permute-start | bytes 159752 | tf_op jit(solution)/shard_map/ppermute | solution.py:43
  13.6 2.8 %collective-permute-start.10 = (bf16[9,16,512]{2,1,0:T(8,128)(2,1)S(1)}, bf16[9,16,512]{2,1,0:T(8,128)(2,1)S(1)}, u32[]{:S(2)}, u32[]{:S(2)}) collective-permute-start(bf16[9,16,512]{2,1,0:T(8,128)(2,1)S(1)} %pad_maximum_fusion.6), channel_id=1, source_target_pairs={{0,24},{2,26},{4,28},{6,30},{8,0},{10,2},{12,4},{14,6},{16,8},{18,... | collective-permute-start | bytes 442376 | tf_op jit(solution)/shard_map/ppermute | solution.py:43
  16.5 2.5 %collective-permute-start.5 = (bf16[4,16,1664]{2,1,0:T(8,128)(2,1)S(1)}, bf16[4,16,1664]{2,1,0:T(8,128)(2,1)S(1)}, u32[]{:S(2)}, u32[]{:S(2)}) collective-permute-start(bf16[4,16,1664]{2,1,0:T(8,128)(2,1)S(1)} %pad_maximum_fusion.5.refs_2_), channel_id=1, source_target_pairs={{0,6},{2,4},{4,2},{6,0},{8,14},{10,12},{12,10},{14,8},{16,22},{18,... | collective-permute-start | bytes 638984 | tf_op jit(solution)/shard_map/ppermute | solution.py:47
  19.5 1.7 %collective-permute-done.12 = bf16[9,16,512]{2,1,0:T(8,128)(2,1)S(1)} collective-permute-done((bf16[9,16,512]{2,1,0:T(8,128)(2,1)S(1)}, bf16[9,16,512]{2,1,0:T(8,128)(2,1)S(1)}, u32[]{:S(2)}, u32[]{:S(2)}) %collective-permute-start.12) | collective-permute-done | bytes 147488 | tf_op jit(solution)/shard_map/ppermute | solution.py:43
  22.7 3.0 %collective-permute-done.11 = bf16[9,16,512]{2,1,0:T(8,128)(2,1)S(1)} collective-permute-done((bf16[9,16,512]{2,1,0:T(8,128)(2,1)S(1)}, bf16[9,16,512]{2,1,0:T(8,128)(2,1)S(1)}, u32[]{:S(2)}, u32[]{:S(2)}) %collective-permute-start.11) | collective-permute-done | bytes 147488 | tf_op jit(solution)/shard_map/ppermute | solution.py:43
  25.7 1.7 %collective-permute-start.14 = (bf16[4,4,16,512]{3,2,1,0:T(8,128)(2,1)S(1)}, bf16[4,4,16,512]{3,2,1,0:T(8,128)(2,1)S(1)}, u32[]{:S(2)}, u32[]{:S(2)}) collective-permute-start(bf16[4,4,16,512]{3,2,1,0:T(8,128)(2,1)S(1)} %pad_maximum_fusion.4), channel_id=1, source_target_pairs={{0,4},{2,6},{4,0},{6,2},{8,12},{10,14},{12,8},{14,10},{16,20},{18,... | collective-permute-start | bytes 786440 | tf_op jit(solution)/shard_map/ppermute | solution.py:47
  27.5 1.6 collective-permute-start.13
  30.1 3.7 %masks.1.refs_1_ = f32[3,512,512]{2,1,0:T(8,128)} custom-call(s32[1,1024]{1,0:T(1,128)} %doc_row.1, s32[1024,1]{1,0:T(8,128)} %copy.18.doc_col, s32[4,512]{1,0:T(4,128)} %bitcast.77), custom_call_target="tpu_custom_call" | custom-call | tf_op jit(solution)/shard_map/masks/pallas_call | solution.py:927
  39.2 16.7 %attention.1 = (bf16[512,1664]{1,0:T(8,128)(2,1)}, bf16[1024,512]{1,0:T(8,128)(2,1)}, bf16[1536,1024]{1,0:T(8,128)(2,1)}, bf16[512,1024]{1,0:T(8,128)(2,1)}, f32...) custom-call(bf16[1024,512]{1,0:T(8,128)(2,1)} %refs_0_.5, ...), custom_call_target="tpu_custom_call" | custom-call | flops 17999998976 | bytes 40000000 | tf_op jit(solution)/shard_map/attention/pallas_call | solution.py:319
  56.7 3.1 %collective-permute-done.19.refs_10_ = bf16[8,4,16,512]{3,2,1,0:T(8,128)(2,1)S(1)} collective-permute-done((bf16[8,4,16,512]{3,2,1,0:T(8,128)(2,1)}, bf16[8,4,16,512]{3,2,1,0:T(8,128)(2,1)S(1)}, u32[]{:S(2)}, u32[]{:S(2)}) %collective-permute-start.19) | collective-permute-done | bytes 524320 | tf_op jit(solution)/shard_map/ppermute | solution.py:51
  61.6 29.3 %feed_forward.1 = (bf16[1024,512]{1,0:T(8,128)(2,1)}, f32[1024,512]{1,0:T(8,128)}, bf16[512,1024]{1,0:T(8,128)(2,1)}, f32[1,512]{1,0:T(1,128)}, bf16[16,5,16,512...) custom-call(bf16[1024,512]{1,0:T(8,128)(2,1)} %refs_0_.5, ...), custom_call_target="tpu_custom_call" | custom-call | flops 24999999488 | bytes 25000000 | tf_op jit(solution)/shard_map/feed_forward/pallas_call | solution.py:566
  91.5 7.9 %attention_back.3 = (bf16[3,128,1024]{2,1,0:T(8,128)(2,1)}, f32[1,2,1024]{2,1,0:T(2,128)}, f32[512,128]{1,0:T(8,128)}, bf16[3,512,128]{2,1,0:T(8,128)(2,1)}) custom-call(f32[8,1024]{1,0:T(8,128)} %get-tuple-element.68.refs_0_, bf16[512,1664]{1,0:T(8,128)(2,1)} %get-tuple-element.73.refs_1_.refs_3_, bf16[512,1024]{1,0:T(8,128)(2,1)} %get-tuple-element.74.refs_2_, ...), custom_call_target="tpu_custom_call" | custom-call | flops 11000000512 | bytes 20000000 | tf_op jit(solution)/shard_map/attention_back/pallas_call | solution.py:815
  99.4 2.4 %add_convert_fusion.1 = (bf16[8,4,16,512]{3,2,1,0:T(8,128)(2,1)S(1)}, f32[8,4,16,512]{3,2,1,0:T(8,128)S(1)}) fusion(bf16[16,4,16,512]{3,2,1,0:T(8,128)(2,1)} %collective-permute-done.22, bf16[16,4,16,512]{3,2,1,0:T(8,128)(2,1)} %get-tuple-element.88), kind=kLoop, calls=%fused_computation.6 | loop fusion | flops 1835008 | bytes 3670016 | tf_op jit(solution)/shard_map/convert_element_type | solution.py:992
  102.6 1.9 %add_convert_fusion = (bf16[8,5,16,512]{3,2,1,0:T(8,128)(2,1)S(1)}, f32[8,5,16,512]{3,2,1,0:T(8,128)S(1)}) fusion(bf16[16,5,16,512]{3,2,1,0:T(8,128)(2,1)} %copy-done.19, bf16[16,5,16,512]{3,2,1,0:T(8,128)(2,1)S(1)} %copy-done.18), kind=kLoop, calls=%fused_computation.3 | loop fusion | flops 2293760 | bytes 4587520 | tf_op jit(solution)/shard_map/convert_element_type | solution.py:990
  106.1 4.0 %copy-done.1 = bf16[4,2,2560,256]{3,2,1,0:T(8,128)(2,1)S(1)} copy-done((bf16[4,2,2560,256]{3,2,1,0:T(8,128)(2,1)S(1)}, bf16[4,2,2560,256]{3,2,1,0:T(8,128)(2,1)}, u32[]{:S(2)}) %copy-start.1) | copy-done | bytes 10485784
  110.0 1.9 %copy-done.4 = bf16[1536,1024]{1,0:T(8,128)(2,1)S(1)} copy-done((bf16[1536,1024]{1,0:T(8,128)(2,1)S(1)}, bf16[1536,1024]{1,0:T(8,128)(2,1)}, u32[]{:S(2)}) %copy-start.4) | copy-done | bytes 3145752
  114.2 7.0 %attention_back.4 = (bf16[3,256,1024]{2,1,0:T(8,128)(2,1)S(1)}, f32[2,2,1024]{2,1,0:T(2,128)S(1)}, f32[512,128]{1,0:T(8,128)S(1)}, bf16[3,512,256]{2,1,0:T(8,128)(2,1)S(1)}) custom-call(f32[8,1024]{1,0:T(8,128)S(1)} %copy-done.14, bf16[512,1664]{1,0:T(8,128)(2,1)S(1)} %copy-done.3, bf16[512,1024]{1,0:T(8,128)(2,1)S(1)} %copy-done.7, ...), custom_call_target="tpu_custom_call" | custom-call | flops 11000000512 | bytes 20000000 | tf_op jit(solution)/shard_map/attention_back/pallas_call | solution.py:815
  124.6 7.5 %attention_back.5 = (bf16[3,128,1024]{2,1,0:T(8,128)(2,1)S(1)}, f32[1,2,1024]{2,1,0:T(2,128)S(1)}, bf16[16,16,1664]{2,1,0:T(8,128)(2,1)S(1)}, bf16[16,16,1664]{2,1,0:T(8,128)(2,1)S(1)}) custom-call(f32[8,1024]{1,0:T(8,128)S(1)} %copy-done.14, bf16[512,1664]{1,0:T(8,128)(2,1)S(1)} %copy-done.3, bf16[512,1024]{1,0:T(8,128)(2,1)S(1)} %copy-done.7, ...), custom_call_target="tpu_custom_call" | custom-call | flops 11000000512 | bytes 20000000 | tf_op jit(solution)/shard_map/attention_back/pallas_call | solution.py:815
  132.5 5.2 %collective-permute-start.36 = (bf16[9,16,512]{2,1,0:T(8,128)(2,1)S(1)}, bf16[9,16,512]{2,1,0:T(8,128)(2,1)S(1)}, u32[]{:S(2)}, u32[]{:S(2)}) collective-permute-start(bf16[9,16,512]{2,1,0:T(8,128)(2,1)S(1)} %get-tuple-element.125), channel_id=1, source_target_pairs={{0,24},{2,26},{4,28},{6,30},{8,0},{10,2},{12,4},{14,6},{16,8},{18,... | collective-permute-start | bytes 442376 | tf_op jit(solution)/shard_map/ppermute | solution.py:43
  141.5 4.6 %input_back.1 = bf16[1024,512]{1,0:T(8,128)(2,1)} custom-call(bf16[1024,512]{1,0:T(8,128)(2,1)S(1)} %copy-done, f32[1024,512]{1,0:T(8,128)S(1)} %copy-done.2, f32[2,512]{1,0:T(2,128)S(1)} %copy-done.16, bf16[512,1664]{1,0:T(8,128)(2,1)S(1)} %copy-done.3, bf16[3,128,1024]{2,1,0:T(8,128)(2,1)S(1)} %copy-done.5, ...), custom_call_target="tpu_custom_call" | custom-call | flops 5000000000 | bytes 9000000 | tf_op jit(solution)/shard_map/input_back/pallas_call | solution.py:889
  147.9 2.4 %collective-permute-done.29 = bf16[4,16,1664]{2,1,0:T(8,128)(2,1)S(1)} collective-permute-done((bf16[4,16,1664]{2,1,0:T(8,128)(2,1)S(1)}, bf16[4,16,1664]{2,1,0:T(8,128)(2,1)S(1)}, u32[]{:S(2)}, u32[]{:S(2)}) %collective-permute-start.29) | collective-permute-done | bytes 213024 | tf_op jit(solution)/shard_map/ppermute | solution.py:47
  151.6 2.7 %collective-permute-start.33 = (bf16[16,1664]{1,0:T(8,128)(2,1)S(1)}, bf16[16,1664]{1,0:T(8,128)(2,1)S(1)}, u32[]{:S(2)}, u32[]{:S(2)}) collective-permute-start(bf16[16,1664]{1,0:T(8,128)(2,1)S(1)} %get-tuple-element.131), channel_id=1, source_target_pairs={{0,24},{2,26},{4,28},{6,30},{8,0},{10,2},{12,4},{14,6},{16,8},{18,... | collective-permute-start | bytes 159752 | tf_op jit(solution)/shard_map/ppermute | solution.py:43
  157.4 2.0 %collective-permute-done.32 = bf16[16,1664]{1,0:T(8,128)(2,1)S(1)} collective-permute-done((bf16[16,1664]{1,0:T(8,128)(2,1)S(1)}, bf16[16,1664]{1,0:T(8,128)(2,1)S(1)}, u32[]{:S(2)}, u32[]{:S(2)}) %collective-permute-start.32) | collective-permute-done | bytes 53280 | tf_op jit(solution)/shard_map/ppermute | solution.py:43
  (173 shorter events, 38.8 us)
Async XLA Ops:
  5.6 8.0 %collective-permute-start.2 = (bf16[16,1664]{1,0:T(8,128)(2,1)S(1)}, bf16[16,1664]{1,0:T(8,128)(2,1)S(1)}, u32[]{:S(2)}, u32[]{:S(2)}) collective-permute-start(bf16[16,1664]{1,0:T(8,128)(2,1)S(1)} %concatenate.15), channel_id=1, source_target_pairs={{0,8},{2,10},{4,12},{6,14},{8,16},{10,18},{12,20},{14,22},{16,24},... | collective-permute-start | bytes 159752 | tf_op jit(solution)/shard_map/ppermute | solution.py:43
  12.6 8.6 %collective-permute-start.12 = (bf16[9,16,512]{2,1,0:T(8,128)(2,1)S(1)}, bf16[9,16,512]{2,1,0:T(8,128)(2,1)S(1)}, u32[]{:S(2)}, u32[]{:S(2)}) collective-permute-start(bf16[9,16,512]{2,1,0:T(8,128)(2,1)S(1)} %pad_maximum_fusion.6), channel_id=1, source_target_pairs={{0,8},{2,10},{4,12},{6,14},{8,16},{10,18},{12,20},{14,22},{16,24},... | collective-permute-start | bytes 442376 | tf_op jit(solution)/shard_map/ppermute | solution.py:43
  13.2 12.4 %collective-permute-start.11 = (bf16[9,16,512]{2,1,0:T(8,128)(2,1)S(1)}, bf16[9,16,512]{2,1,0:T(8,128)(2,1)S(1)}, u32[]{:S(2)}, u32[]{:S(2)}) collective-permute-start(bf16[9,16,512]{2,1,0:T(8,128)(2,1)S(1)} %pad_maximum_fusion.6), channel_id=1, source_target_pairs={{0,16},{2,18},{4,20},{6,22},{8,24},{10,26},{12,28},{14,30},{16,0},... | collective-permute-start | bytes 442376 | tf_op jit(solution)/shard_map/ppermute | solution.py:43
  13.6 12.1 %collective-permute-start.10 = (bf16[9,16,512]{2,1,0:T(8,128)(2,1)S(1)}, bf16[9,16,512]{2,1,0:T(8,128)(2,1)S(1)}, u32[]{:S(2)}, u32[]{:S(2)}) collective-permute-start(bf16[9,16,512]{2,1,0:T(8,128)(2,1)S(1)} %pad_maximum_fusion.6), channel_id=1, source_target_pairs={{0,24},{2,26},{4,28},{6,30},{8,0},{10,2},{12,4},{14,6},{16,8},{18,... | collective-permute-start | bytes 442376 | tf_op jit(solution)/shard_map/ppermute | solution.py:43
  16.5 17.3 %collective-permute-start.5 = (bf16[4,16,1664]{2,1,0:T(8,128)(2,1)S(1)}, bf16[4,16,1664]{2,1,0:T(8,128)(2,1)S(1)}, u32[]{:S(2)}, u32[]{:S(2)}) collective-permute-start(bf16[4,16,1664]{2,1,0:T(8,128)(2,1)S(1)} %pad_maximum_fusion.5.refs_2_), channel_id=1, source_target_pairs={{0,6},{2,4},{4,2},{6,0},{8,14},{10,12},{12,10},{14,8},{16,22},{18,... | collective-permute-start | bytes 638984 | tf_op jit(solution)/shard_map/ppermute | solution.py:47
  19.0 14.8 %collective-permute-start.4 = (bf16[4,16,1664]{2,1,0:T(8,128)(2,1)S(1)}, bf16[4,16,1664]{2,1,0:T(8,128)(2,1)S(1)}, u32[]{:S(2)}, u32[]{:S(2)}) collective-permute-start(bf16[4,16,1664]{2,1,0:T(8,128)(2,1)S(1)} %pad_maximum_fusion.5.refs_2_), channel_id=1, source_target_pairs={{0,4},{2,6},{4,0},{6,2},{8,12},{10,14},{12,8},{14,10},{16,20},{18,... | collective-permute-start | bytes 638984 | tf_op jit(solution)/shard_map/ppermute | solution.py:47
  21.2 12.6 %collective-permute-start.3 = (bf16[4,16,1664]{2,1,0:T(8,128)(2,1)S(1)}, bf16[4,16,1664]{2,1,0:T(8,128)(2,1)S(1)}, u32[]{:S(2)}, u32[]{:S(2)}) collective-permute-start(bf16[4,16,1664]{2,1,0:T(8,128)(2,1)S(1)} %pad_maximum_fusion.5.refs_2_), channel_id=1, source_target_pairs={{0,2},{2,0},{4,6},{6,4},{8,10},{10,8},{12,14},{14,12},{16,18},{18,... | collective-permute-start | bytes 638984 | tf_op jit(solution)/shard_map/ppermute | solution.py:47
  25.7 8.8 %collective-permute-start.14 = (bf16[4,4,16,512]{3,2,1,0:T(8,128)(2,1)S(1)}, bf16[4,4,16,512]{3,2,1,0:T(8,128)(2,1)S(1)}, u32[]{:S(2)}, u32[]{:S(2)}) collective-permute-start(bf16[4,4,16,512]{3,2,1,0:T(8,128)(2,1)S(1)} %pad_maximum_fusion.4), channel_id=1, source_target_pairs={{0,4},{2,6},{4,0},{6,2},{8,12},{10,14},{12,8},{14,10},{16,20},{18,... | collective-permute-start | bytes 786440 | tf_op jit(solution)/shard_map/ppermute | solution.py:47
  27.5 8.7 %collective-permute-start.13 = (bf16[4,5,16,512]{3,2,1,0:T(8,128)(2,1)S(1)}, bf16[4,5,16,512]{3,2,1,0:T(8,128)(2,1)S(1)}, u32[]{:S(2)}, u32[]{:S(2)}) collective-permute-start(bf16[4,5,16,512]{3,2,1,0:T(8,128)(2,1)S(1)} %slice.166), channel_id=1, source_target_pairs={{0,2},{2,0},{4,6},{6,4},{8,10},{10,8},{12,14},{14,12},{16,18},{18,... | collective-permute-start | bytes 983048 | tf_op jit(solution)/shard_map/ppermute | solution.py:47
  36.2 19.7 %collective-permute-start.16 = (bf16[8,4,16,512]{3,2,1,0:T(8,128)(2,1)S(1)}, bf16[8,4,16,512]{3,2,1,0:T(8,128)(2,1)S(1)}, u32[]{:S(2)}, u32[]{:S(2)}) collective-permute-start(bf16[8,4,16,512]{3,2,1,0:T(8,128)(2,1)S(1)} %pad_maximum_fusion.3.refs_11_.refs_8_), channel_id=1, source_target_pairs={{0,2},{2,0},{4,6},{6,4},{8,10},{10,8},{12,14},{14,12},{16,18},{18,... | collective-permute-start | bytes 1572872 | tf_op jit(solution)/shard_map/ppermute | solution.py:47
  37.8 22.0 %collective-permute-start.17 = (bf16[8,5,16,512]{3,2,1,0:T(8,128)(2,1)S(1)}, bf16[8,5,16,512]{3,2,1,0:T(8,128)(2,1)S(1)}, u32[]{:S(2)}, u32[]{:S(2)}) collective-permute-start(bf16[8,5,16,512]{3,2,1,0:T(8,128)(2,1)S(1)} %pad_maximum_fusion.1.refs_10_.refs_4_), channel_id=1, source_target_pairs={{0,1},{1,0},{2,3},{3,2},{4,5},{5,4},{6,7},{7,6},{8,9},{9,8},{10,11... | collective-permute-start | bytes 1966088 | tf_op jit(solution)/shard_map/ppermute | solution.py:51
  37.9 18.0 %collective-permute-start.15 = (bf16[8,5,16,512]{3,2,1,0:T(8,128)(2,1)S(1)}, bf16[8,5,16,512]{3,2,1,0:T(8,128)(2,1)S(1)}, u32[]{:S(2)}, u32[]{:S(2)}) collective-permute-start(bf16[8,5,16,512]{3,2,1,0:T(8,128)(2,1)S(1)} %pad_maximum_fusion.1.refs_10_.refs_4_), channel_id=1, source_target_pairs={{0,4},{2,6},{4,0},{6,2},{8,12},{10,14},{12,8},{14,10},{16,20},{18,... | collective-permute-start | bytes 1966088 | tf_op jit(solution)/shard_map/ppermute | solution.py:47
  90.9 8.5 %collective-permute-start.21 = (bf16[16,5,16,512]{3,2,1,0:T(8,128)(2,1)}, bf16[16,5,16,512]{3,2,1,0:T(8,128)(2,1)S(1)}, u32[]{:S(2)}, u32[]{:S(2)}) collective-permute-start(bf16[16,5,16,512]{3,2,1,0:T(8,128)(2,1)} %get-tuple-element.84), channel_id=1, source_target_pairs={{0,1},{1,0},{2,3},{3,2},{4,5},{5,4},{6,7},{7,6},{8,9},{9,8},{10,11... | collective-permute-start | bytes 3932168 | tf_op jit(solution)/shard_map/ppermute | solution.py:51
  91.1 8.3 %collective-permute-start.22 = (bf16[16,4,16,512]{3,2,1,0:T(8,128)(2,1)}, bf16[16,4,16,512]{3,2,1,0:T(8,128)(2,1)}, u32[]{:S(2)}, u32[]{:S(2)}) collective-permute-start(bf16[16,4,16,512]{3,2,1,0:T(8,128)(2,1)} %get-tuple-element.85), channel_id=1, source_target_pairs={{0,1},{1,0},{2,3},{3,2},{4,5},{5,4},{6,7},{7,6},{8,9},{9,8},{10,11... | collective-permute-start | bytes 3145736 | tf_op jit(solution)/shard_map/ppermute | solution.py:51
  101.8 19.4 %collective-permute-start.24 = (bf16[8,4,16,512]{3,2,1,0:T(8,128)(2,1)S(1)}, bf16[8,4,16,512]{3,2,1,0:T(8,128)(2,1)S(1)}, u32[]{:S(2)}, u32[]{:S(2)}) collective-permute-start(bf16[8,4,16,512]{3,2,1,0:T(8,128)(2,1)S(1)} %get-tuple-element.116.refs_14_), channel_id=1, source_target_pairs={{0,2},{2,0},{4,6},{6,4},{8,10},{10,8},{12,14},{14,12},{16,18},{18,... | collective-permute-start | bytes 1572872 | tf_op jit(solution)/shard_map/ppermute | solution.py:47
  104.5 16.7 %collective-permute-start.23 = (bf16[8,5,16,512]{3,2,1,0:T(8,128)(2,1)S(1)}, bf16[8,5,16,512]{3,2,1,0:T(8,128)(2,1)S(1)}, u32[]{:S(2)}, u32[]{:S(2)}) collective-permute-start(bf16[8,5,16,512]{3,2,1,0:T(8,128)(2,1)S(1)} %get-tuple-element.114.refs_12_), channel_id=1, source_target_pairs={{0,4},{2,6},{4,0},{6,2},{8,12},{10,14},{12,8},{14,10},{16,20},{18,... | collective-permute-start | bytes 1966088 | tf_op jit(solution)/shard_map/ppermute | solution.py:47
  121.7 10.4 %collective-permute-start.27 = (bf16[4,4,16,512]{3,2,1,0:T(8,128)(2,1)S(1)}, bf16[4,4,16,512]{3,2,1,0:T(8,128)(2,1)S(1)}, u32[]{:S(2)}, u32[]{:S(2)}) collective-permute-start(bf16[4,4,16,512]{3,2,1,0:T(8,128)(2,1)S(1)} %get-tuple-element.123.refs_22_), channel_id=1, source_target_pairs={{0,4},{2,6},{4,0},{6,2},{8,12},{10,14},{12,8},{14,10},{16,20},{18,... | collective-permute-start | bytes 786440 | tf_op jit(solution)/shard_map/ppermute | solution.py:47
  123.1 9.1 %collective-permute-start.26 = (bf16[4,5,16,512]{3,2,1,0:T(8,128)(2,1)S(1)}, bf16[4,5,16,512]{3,2,1,0:T(8,128)(2,1)S(1)}, u32[]{:S(2)}, u32[]{:S(2)}) collective-permute-start(bf16[4,5,16,512]{3,2,1,0:T(8,128)(2,1)S(1)} %get-tuple-element.118.refs_20_), channel_id=1, source_target_pairs={{0,2},{2,0},{4,6},{6,4},{8,10},{10,8},{12,14},{14,12},{16,18},{18,... | collective-permute-start | bytes 983048 | tf_op jit(solution)/shard_map/ppermute | solution.py:47
  132.5 21.8 %collective-permute-start.36 = (bf16[9,16,512]{2,1,0:T(8,128)(2,1)S(1)}, bf16[9,16,512]{2,1,0:T(8,128)(2,1)S(1)}, u32[]{:S(2)}, u32[]{:S(2)}) collective-permute-start(bf16[9,16,512]{2,1,0:T(8,128)(2,1)S(1)} %get-tuple-element.125), channel_id=1, source_target_pairs={{0,24},{2,26},{4,28},{6,30},{8,0},{10,2},{12,4},{14,6},{16,8},{18,... | collective-permute-start | bytes 442376 | tf_op jit(solution)/shard_map/ppermute | solution.py:43
  137.7 17.5 %collective-permute-start.35 = (bf16[9,16,512]{2,1,0:T(8,128)(2,1)S(1)}, bf16[9,16,512]{2,1,0:T(8,128)(2,1)S(1)}, u32[]{:S(2)}, u32[]{:S(2)}) collective-permute-start(bf16[9,16,512]{2,1,0:T(8,128)(2,1)S(1)} %get-tuple-element.126), channel_id=1, source_target_pairs={{0,16},{2,18},{4,20},{6,22},{8,24},{10,26},{12,28},{14,30},{16,0},... | collective-permute-start | bytes 442376 | tf_op jit(solution)/shard_map/ppermute | solution.py:43
  137.9 9.1 %collective-permute-start.30 = (bf16[4,16,1664]{2,1,0:T(8,128)(2,1)S(1)}, bf16[4,16,1664]{2,1,0:T(8,128)(2,1)S(1)}, u32[]{:S(2)}, u32[]{:S(2)}) collective-permute-start(bf16[4,16,1664]{2,1,0:T(8,128)(2,1)S(1)} %get-tuple-element.120.refs_12_), channel_id=1, source_target_pairs={{0,6},{2,4},{4,2},{6,0},{8,14},{10,12},{12,10},{14,8},{16,22},{18,... | collective-permute-start | bytes 638984 | tf_op jit(solution)/shard_map/ppermute | solution.py:47
  139.5 10.8 %collective-permute-start.29 = (bf16[4,16,1664]{2,1,0:T(8,128)(2,1)S(1)}, bf16[4,16,1664]{2,1,0:T(8,128)(2,1)S(1)}, u32[]{:S(2)}, u32[]{:S(2)}) collective-permute-start(bf16[4,16,1664]{2,1,0:T(8,128)(2,1)S(1)} %get-tuple-element.121.refs_11_), channel_id=1, source_target_pairs={{0,4},{2,6},{4,0},{6,2},{8,12},{10,14},{12,8},{14,10},{16,20},{18,... | collective-permute-start | bytes 638984 | tf_op jit(solution)/shard_map/ppermute | solution.py:47
  140.2 10.1 %collective-permute-start.28 = (bf16[4,16,1664]{2,1,0:T(8,128)(2,1)S(1)}, bf16[4,16,1664]{2,1,0:T(8,128)(2,1)S(1)}, u32[]{:S(2)}, u32[]{:S(2)}) collective-permute-start(bf16[4,16,1664]{2,1,0:T(8,128)(2,1)S(1)} %get-tuple-element.122.refs_10_), channel_id=1, source_target_pairs={{0,2},{2,0},{4,6},{6,4},{8,10},{10,8},{12,14},{14,12},{16,18},{18,... | collective-permute-start | bytes 638984 | tf_op jit(solution)/shard_map/ppermute | solution.py:47
  147.0 8.2 %collective-permute-start.34 = (bf16[9,16,512]{2,1,0:T(8,128)(2,1)S(1)}, bf16[9,16,512]{2,1,0:T(8,128)(2,1)S(1)}, u32[]{:S(2)}, u32[]{:S(2)}) collective-permute-start(bf16[9,16,512]{2,1,0:T(8,128)(2,1)S(1)} %get-tuple-element.127), channel_id=1, source_target_pairs={{0,8},{2,10},{4,12},{6,14},{8,16},{10,18},{12,20},{14,22},{16,24},... | collective-permute-start | bytes 442376 | tf_op jit(solution)/shard_map/ppermute | solution.py:43
  (50 other events, 263.9 us)
